TPU v7x, 32 devices: a whole 2x2x4 slice. The times are simulated.
32 devices in a mesh: lon: 16 (over z, y, core), rad: 2 (over x).
Axes of the slice: x: 2, y: 2, z: 4, core: 2. Of those that a mesh axis runs over, the one named last changes fastest.
Arguments:
- logvisc: float32 [96, 64, 512], P('rad', 'lon'), may hold values from -1 to 1
- momentum: float32 [96, 64, 512], P('rad', 'lon'), may hold values from -6 to 6
- displacement: float32 [3, 96, 64, 512], P(None, 'rad', 'lon'), may hold values from -6 to 6
- ice_history: float32 [8, 64, 512], P(None, 'lon'), may hold values from -6 to 6
- load_steps: int32 [2], replicated, may hold values from 0 to 7
- site_cells: int32 [192], P('lon'), may hold values from 0 to 32767
- observed: float32 [3, 192], P(None, 'lon'), may hold values from -6 to 6
- site_weight: float32 [3, 192], P(None, 'lon'), may hold values from 2 to 6
Outputs:
- new_logvisc: float32 [96, 64, 512], P('rad', 'lon')
- half_momentum: float32 [96, 64, 512], P('rad', 'lon')
- misfit: float32 [1], replicated
Inputs may be any that keep to these rules, and one draw needn't show every extreme that they name: site_cells holds lon * 512 + lat of the surface cell where the site stands. load_steps indexes the first dimension of ice_history.
All inputs are finite; a program needn't handle non-finite values.
Results may differ from a plain program's by a relative error of at most 0.0003.
Values sent between devices are 32-bit elements; how exact they have to be, the bound alone decides.
No kernel may reach another device: no remote copies, remote signals or barrier semaphores. Data moves between devices by JAX's collectives and lax.ppermute only.
A program may use at most 64 MiB of HBM per device.

v0:
```python
import math

import jax
import jax.numpy as jnp
from jax import lax
from jax.sharding import PartitionSpec as P

RELAX = 2


RELAX_RATE = 0.05
KERNEL_WIDTH = 0.1
KERNEL_WAVE = 40.0
PRIOR_WEIGHT = 0.1
LOAD_FACTOR = 1.0


def extended(block, sides, width, periodic):
    for axis, dim in sides:
        count = lax.axis_size(axis)
        forward = [(i, i + 1) for i in range(count - 1)]
        if periodic:
            forward.append((count - 1, 0))
        backward = [(target, source) for source, target in forward]
        low = lax.ppermute(
            lax.slice_in_dim(block, block.shape[dim] - width, None, axis=dim), axis, forward
        )
        high = lax.ppermute(lax.slice_in_dim(block, 0, width, axis=dim), axis, backward)
        block = jnp.concatenate([low, block, high], axis=dim)
    return block


def harmonic(center_fluid, other_fluid):
    summed = center_fluid + other_fluid
    coeff = 2.0 * center_fluid * other_fluid / summed
    slope = 2.0 * other_fluid * other_fluid / (summed * summed)
    return (coeff, slope)


def neighbours(padded):
    return [
        padded[:, 2:, 1:-1, 1:-1],
        padded[:, :-2, 1:-1, 1:-1],
        padded[:, 1:-1, 2:, 1:-1],
        padded[:, 1:-1, :-2, 1:-1],
        padded[:, 1:-1, 1:-1, 2:],
        padded[:, 1:-1, 1:-1, :-2],
    ]


def middle(padded):
    return padded[:, 1:-1, 1:-1, 1:-1]


def apply_operator(field_pad, fluid_pad):
    fluid_mid = middle(fluid_pad)
    field_mid = middle(field_pad)
    total = jnp.zeros(field_mid.shape, jnp.float32)
    for fluid_side, field_side in zip(neighbours(fluid_pad), neighbours(field_pad)):
        coeff, slope = harmonic(fluid_mid, fluid_side)
        total = total + coeff * (field_side - field_mid)
    return total


def fluid_gradient(state_pad, adjoint_pad, fluid_pad):
    fluid_mid = middle(fluid_pad)
    state_mid = middle(state_pad)
    adjoint_mid = middle(adjoint_pad)
    total = jnp.zeros(fluid_mid.shape, jnp.float32)
    for fluid_side, state_side, adjoint_side in zip(
        neighbours(fluid_pad), neighbours(state_pad), neighbours(adjoint_pad)
    ):
        coeff, slope = harmonic(fluid_mid, fluid_side)
        product = jnp.sum(
            (state_side - state_mid) * (adjoint_side - adjoint_mid), axis=0, keepdims=True
        )
        total = total + slope * product
    return -RELAX_RATE * total


def extend(field):
    layered = extended(field, (("rad", 1),), 1, False)
    beside_all = extended(layered, (("lon", 2),), 1, True)
    return jnp.pad(beside_all, ((0, 0), (0, 0), (0, 0), (1, 1)))


def cell_features(lon_index, lat_index, total_lon, total_lat):
    theta = math.pi * (lat_index.astype(jnp.float32) + 0.5) / total_lat
    phi = 2.0 * math.pi * lon_index.astype(jnp.float32) / total_lon
    upward = jnp.broadcast_to(jnp.cos(theta)[None, :], (phi.shape[0], theta.shape[0]))
    eastern = jnp.sin(theta)[None, :] * jnp.cos(phi)[:, None]
    northern = jnp.sin(theta)[None, :] * jnp.sin(phi)[:, None]
    return jnp.stack([upward, eastern, northern]).reshape(3, -1)


def site_features(cells, total_lon, total_lat):
    lon_index = cells // total_lat
    lat_index = cells % total_lat
    theta = math.pi * (lat_index.astype(jnp.float32) + 0.5) / total_lat
    phi = 2.0 * math.pi * lon_index.astype(jnp.float32) / total_lon
    return jnp.stack(
        [jnp.cos(theta), jnp.sin(theta) * jnp.cos(phi), jnp.sin(theta) * jnp.sin(phi)], axis=1
    )


def kernel(site_feats, cell_feats):
    cosine = (
        site_feats[:, 0:1] * cell_feats[0:1]
        + site_feats[:, 1:2] * cell_feats[1:2]
        + site_feats[:, 2:3] * cell_feats[2:3]
    )
    chord = 2.0 - 2.0 * cosine
    return 1.0 / (1.0 + chord / KERNEL_WIDTH) + 0.5 * jnp.cos(KERNEL_WAVE * chord)


def group_size(total_rows, unit, cells):
    blocks = total_rows // unit
    chosen = 1
    for candidate in range(1, 9):
        if blocks % candidate == 0 and candidate * unit * cells <= 1048576:
            chosen = candidate
    return chosen * unit


def predict_rows(feats, cell_feats, surface_flat, unit):
    size = group_size(feats.shape[0], unit, cell_feats.shape[1])
    blocks = feats.reshape(-1, size, 3)

    def one_block(block):
        weights = kernel(block, cell_feats)
        return jnp.einsum(
            "sm,cm->sc",
            weights,
            surface_flat,
            precision=lax.Precision.HIGHEST,
            preferred_element_type=jnp.float32,
        )

    return lax.map(one_block, blocks).reshape(-1, 3)


def body(
    logvisc, momentum, displacement, ice_history, load_steps, site_cells, observed, site_weight
):
    rad_rows = logvisc.shape[0]
    lon_cols = logvisc.shape[1]
    lat_cells = logvisc.shape[2]
    site_rows = site_cells.shape[0]
    total_rad = rad_rows * lax.axis_size("rad")
    total_lon = lon_cols * lax.axis_size("lon")
    lat_width = lat_cells // lax.axis_size("rad")
    scale = 1.0 / math.sqrt(total_lon * lat_cells)
    rad_global = lax.axis_index("rad") * rad_rows + jnp.arange(rad_rows)
    lon_global = lax.axis_index("lon") * lon_cols + jnp.arange(lon_cols)
    depth_weight = jnp.exp(4.0 * (rad_global.astype(jnp.float32) - (total_rad - 1)) / total_rad)
    top_row = (rad_global == total_rad - 1).astype(jnp.float32)[None, :, None, None]
    upward = (jnp.arange(3) == 0).astype(jnp.float32)[:, None, None, None]
    fluidity = jnp.exp(-logvisc)
    fluid_pad = extend(fluidity[None])
    state = displacement
    saved = []
    for level in range(RELAX):
        padded = extend(state)
        saved.append(padded)
        load = lax.dynamic_index_in_dim(ice_history, load_steps[level], 0, keepdims=False)
        state = (
            state
            + RELAX_RATE * apply_operator(padded, fluid_pad)
            - LOAD_FACTOR * upward * top_row * load[None, None]
        )
    column = jnp.sum(depth_weight[None, :, None, None] * state, axis=1)
    lat_start = lax.axis_index("rad") * lat_width
    lat_band = lat_start + jnp.arange(lat_width)
    whole_column = lax.psum(column, "rad")
    band = lax.dynamic_slice_in_dim(whole_column, lat_start, lat_width, 2)
    band_feats = cell_features(lon_global, lat_band, total_lon, lat_cells)
    own_feats = site_features(site_cells, total_lon, lat_cells)
    all_feats = lax.all_gather(own_feats, "lon", axis=0, tiled=True)
    band_flat = band.reshape(3, -1)
    partial_pred = lax.psum_scatter(
        predict_rows(all_feats, band_feats, band_flat, site_rows) * scale,
        "lon",
        scatter_dimension=0,
        tiled=True,
    )
    predicted = lax.psum(partial_pred, "rad").T
    weighted = site_weight * (predicted - observed)
    misfit = lax.psum(jnp.sum(weighted * weighted), "lon") / (3 * total_lon // lon_cols * site_rows)
    adjoint_cells = cell_features(lon_global, jnp.arange(lat_cells), total_lon, lat_cells)
    packet = jnp.concatenate([own_feats, (site_weight * weighted).T], axis=1)
    piece = lax.all_gather(packet, "lon", axis=0, tiled=True)
    size = group_size(piece.shape[0], site_rows, adjoint_cells.shape[1])
    blocks = piece.reshape(-1, size, 6)

    def add_block(running, block):
        weights = kernel(block[:, :3], adjoint_cells)
        return (
            running
            + jnp.einsum(
                "sc,sm->cm",
                block[:, 3:],
                weights,
                precision=lax.Precision.HIGHEST,
                preferred_element_type=jnp.float32,
            ),
            None,
        )

    running, unused = lax.scan(
        add_block, jnp.zeros((3, adjoint_cells.shape[1]), jnp.float32), blocks
    )
    surface_adjoint = (running * scale).reshape(3, lon_cols, lat_cells)
    adjoint = depth_weight[None, :, None, None] * surface_adjoint[:, None]
    gradient_fluid = jnp.zeros((1, rad_rows, lon_cols, lat_cells), jnp.float32)
    for level in range(RELAX - 1, -1, -1):
        adjoint_pad = extend(adjoint)
        gradient_fluid = gradient_fluid + fluid_gradient(saved[level], adjoint_pad, fluid_pad)
        if level > 0:
            adjoint = adjoint + RELAX_RATE * apply_operator(adjoint_pad, fluid_pad)
    gradient = -fluidity * gradient_fluid[0] + PRIOR_WEIGHT * logvisc
    half_momentum = momentum - 0.5 * gradient
    new_logvisc = logvisc + half_momentum
    return (new_logvisc, half_momentum, misfit.reshape(1))


def solution(mesh):
    return jax.shard_map(
        body,
        mesh=mesh,
        in_specs=(
            P("rad", "lon", None),
            P("rad", "lon", None),
            P(None, "rad", "lon", None),
            P(None, "lon", None),
            P(),
            P("lon"),
            P(None, "lon"),
            P(None, "lon"),
        ),
        out_specs=(P("rad", "lon", None), P("rad", "lon", None), P()),
        check_vma=False,
    )
```

profile of v0, /device:TPU:0, one launch (start us, length us, event | category | flops | bytes accessed | tf_op | source)
XLA Modules:
  0.0 236.2 jit_solution(7258114195875611112)
XLA Ops:
  1.8 4.8 %collective-permute-start.2 = (f32[1,1,4,512]{3,1,2,0:T(1,128)S(1)}, f32[1,1,4,512]{3,1,2,0:T(1,128)S(1)}, u32[]{:S(2)}, u32[]{:S(2)}) collective-permute-start(f32[1,1,4,512]{3,1,2,0:T(1,128)S(1)} %get-tuple-element.177), channel_id=1, source_target_pairs={{0,1},{2,3},{4,5},{6,7},{8,9},{10,11},{12,13},{14,15},{16,17},{18,... | collective-permute-start | bytes 24584 | tf_op jit(solution)/shard_map/ppermute | solution.py:25
  9.7 4.5 %collective-permute-start.3 = (f32[3,1,4,512]{3,1,2,0:T(1,128)S(1)}, f32[3,1,4,512]{3,1,2,0:T(1,128)S(1)}, u32[]{:S(2)}, u32[]{:S(2)}) collective-permute-start(f32[3,1,4,512]{3,1,2,0:T(1,128)S(1)} %get-tuple-element.167), channel_id=1, source_target_pairs={{0,1},{2,3},{4,5},{6,7},{8,9},{10,11},{12,13},{14,15},{16,17},{18,... | collective-permute-start | bytes 73736 | tf_op jit(solution)/shard_map/ppermute | solution.py:25
  21.9 4.4 %collective-permute-start.4 = (f32[1,50,1,512]{3,1,2,0:T(8,128)S(1)}, f32[1,50,1,512]{3,1,2,0:T(8,128)S(1)}, u32[]{:S(2)}, u32[]{:S(2)}) collective-permute-start(f32[1,50,1,512]{3,1,2,0:T(8,128)S(1)} %get-tuple-element.174), channel_id=1, source_target_pairs={{2,0},{4,2},{6,4},{8,6},{10,8},{12,10},{14,12},{16,14},{18,16},{20... | collective-permute-start | bytes 307208 | tf_op jit(solution)/shard_map/ppermute | solution.py:28
  26.5 4.4 %collective-permute-start.5 = (f32[3,50,1,512]{3,1,2,0:T(8,128)S(1)}, f32[3,50,1,512]{3,1,2,0:T(8,128)S(1)}, u32[]{:S(2)}, u32[]{:S(2)}) collective-permute-start(f32[3,50,1,512]{3,1,2,0:T(8,128)S(1)} %get-tuple-element.160), channel_id=1, source_target_pairs={{2,0},{4,2},{6,4},{8,6},{10,8},{12,10},{14,12},{16,14},{18,16},{20... | collective-permute-start | bytes 921608 | tf_op jit(solution)/shard_map/ppermute | solution.py:28
  32.3 3.7 %collective-permute-done.7 = f32[3,50,1,512]{3,1,2,0:T(8,128)S(1)} collective-permute-done((f32[3,50,1,512]{3,1,2,0:T(8,128)S(1)}, f32[3,50,1,512]{3,1,2,0:T(8,128)S(1)}, u32[]{:S(2)}, u32[]{:S(2)}) %collective-permute-start.7) | collective-permute-done | bytes 307232 | tf_op jit(solution)/shard_map/ppermute | solution.py:25
  38.8 4.5 %collective-permute-start.9 = (f32[3,1,4,512]{3,1,2,0:T(1,128)S(1)}, f32[3,1,4,512]{3,1,2,0:T(1,128)S(1)}, u32[]{:S(2)}, u32[]{:S(2)}) collective-permute-start(f32[3,1,4,512]{3,1,2,0:T(1,128)S(1)} %get-tuple-element.165), channel_id=1, source_target_pairs={{0,1},{2,3},{4,5},{6,7},{8,9},{10,11},{12,13},{14,15},{16,17},{18,... | collective-permute-start | bytes 73736 | tf_op jit(solution)/shard_map/ppermute | solution.py:25
  44.7 19.7 %all-gather = f32[16,12,3]{1,2,0:T(4,128)S(1)} all-gather(f32[1,12,3]{1,2,0:T(4,128)S(1)} %maximum_bitcast_fusion.1), channel_id=1, replica_groups=mesh['lon'=16,'rad'=2] {'lon'}, dimensions={0}, use_global_device_ids=true | all-gather | bytes 2448 | tf_op jit(solution)/shard_map/all_gather | solution.py:178
  66.4 4.1 %collective-permute-start.10 = (f32[3,50,1,512]{3,1,2,0:T(8,128)S(1)}, f32[3,50,1,512]{3,1,2,0:T(8,128)S(1)}, u32[]{:S(2)}, u32[]{:S(2)}) collective-permute-start(f32[3,50,1,512]{3,1,2,0:T(8,128)S(1)} %get-tuple-element.158), channel_id=1, source_target_pairs={{2,0},{4,2},{6,4},{8,6},{10,8},{12,10},{14,12},{16,14},{18,16},{20... | collective-permute-start | bytes 921608 | tf_op jit(solution)/shard_map/ppermute | solution.py:28
  70.5 4.9 %collective-permute-done.11 = f32[3,50,1,512]{3,1,2,0:T(8,128)S(1)} collective-permute-done((f32[3,50,1,512]{3,1,2,0:T(8,128)S(1)}, f32[3,50,1,512]{3,1,2,0:T(8,128)S(1)}, u32[]{:S(2)}, u32[]{:S(2)}) %collective-permute-start.11) | collective-permute-done | bytes 307232 | tf_op jit(solution)/shard_map/ppermute | solution.py:25
  77.9 1.9 multiply_reduce_fusion.6
  79.8 9.4 %psum.21 = f32[3,4,512]{2,1,0:T(4,128)S(1)} all-reduce(f32[3,4,512]{2,1,0:T(4,128)S(1)} %multiply_reduce_fusion.6), channel_id=1, replica_groups=mesh['lon'=16,'rad'=2] {'rad'}, use_global_device_ids=true, to_apply=%region_1.2 | all-reduce | flops 6144 | bytes 49152 | tf_op jit(solution)/shard_map/psum | solution.py:174
  89.3 4.0 %while.21 = (s32[]{:T(128)}, f32[2,96,3]{1,2,0:T(4,128)S(1)}, f32[2,96,3]{1,0,2:T(2,128)S(1)}, f32[3,1024]{1,0:T(4,128)S(1)}, f32[3,1024]{1,0:T(4,128)S(1)}, /*index=5*/s32[]{:T(128)}) while((s32[]{:T(128)}, f32[2,96,3]{1,2,0:T(4,128)S(1)}, f32[2,96,3]{1,0,2:T(2,128)S(1)}, f32[3,1024]{1,0:T(4,128)S(1)}, f32[3,1024]{1,0:T(4,128)S(1)}, ...), condition=%wide.region_3.4_spmd, body=%wide.region_2.3_spmd.sunk | while | flops 4816898 | bytes 63829 | solution.py:139
  89.4 1.9 fusion.159
  91.3 1.9 fusion.159
  93.4 31.8 %all-reduce.5 = f32[192,3]{0,1:T(4,128)S(1)} all-reduce(f32[192,3]{0,1:T(4,128)S(1)} %mul.763), channel_id=2, replica_groups=mesh['lon'=16,'rad'=2] {'lon'}, use_global_device_ids=true, to_apply=%region_4.5.clone | all-reduce | flops 576 | bytes 4608
  125.2 4.9 %psum.22 = f32[3,12]{1,0:T(4,128)S(1)} all-reduce(f32[3,12]{1,0:T(4,128)S(1)} %dynamic-slice_bitcast_fusion.3), channel_id=1, replica_groups=mesh['lon'=16,'rad'=2] {'rad'}, use_global_device_ids=true, to_apply=%region_5.6 | all-reduce | flops 36 | bytes 288 | tf_op jit(solution)/shard_map/psum | solution.py:186
  130.8 17.5 %all-gather.1 = f32[16,12,6]{1,2,0:T(8,128)S(1)} all-gather(f32[1,12,6]{1,2,0:T(8,128)S(1)} %maximum_bitcast_fusion), channel_id=1, replica_groups=mesh['lon'=16,'rad'=2] {'lon'}, dimensions={0}, use_global_device_ids=true | all-gather | bytes 4896 | tf_op jit(solution)/shard_map/all_gather | solution.py:191
  148.4 7.0 %while.22 = (s32[]{:T(128)}, f32[3,2048]{1,0:T(4,128)S(1)}, f32[2,96,6]{1,0,2:T(2,128)S(1)}, f32[3,2048]{1,0:T(4,128)S(1)}, s32[]{:T(128)}, /*index=5*/s32[]{:T(128)}) while((s32[]{:T(128)}, f32[3,2048]{1,0:T(4,128)S(1)}, f32[2,96,6]{1,0,2:T(2,128)S(1)}, f32[3,2048]{1,0:T(4,128)S(1)}, s32[]{:T(128)}, /*index=5*/s32[]{:T(128)}) %tuple.101), condition=%wide.region_7.8_spmd.clone, body=%wide.region_6.7_spmd.clone.sunk | while | flops 9646083 | bytes 146267 | solution.py:209
  148.4 3.4 %convolution_add_fusion.2 = f32[3,2048]{1,0:T(4,128)S(1)} fusion(f32[2048]{0:T(1024)S(1)} %bitcast.253, f32[96]{0:T(128)S(1)} %get-tuple-element.268, f32[2048]{0:T(1024)S(1)} %bitcast.254, f32[96]{0:T(128)S(1)} %get-tuple-element.270, f32[2048]{0:T(1024)S(1)} %bitcast.252, f32[96]{0:T(128)S(1)} %get-tuple-element.272, ...), kind=kOutput, calls=%fused_computation.37.clone.1 | convolution fusion | flops 9646080 | bytes 85505 | tf_op jit(solution)/shard_map/while/body/eval_jaxpr/sc,sm->cm/dot_general | solution.py:199
  152.0 3.4 %convolution_add_fusion.2 = f32[3,2048]{1,0:T(4,128)S(1)} fusion(f32[2048]{0:T(1024)S(1)} %bitcast.253, f32[96]{0:T(128)S(1)} %get-tuple-element.268, f32[2048]{0:T(1024)S(1)} %bitcast.254, f32[96]{0:T(128)S(1)} %get-tuple-element.270, f32[2048]{0:T(1024)S(1)} %bitcast.252, f32[96]{0:T(128)S(1)} %get-tuple-element.272, ...), kind=kOutput, calls=%fused_computation.37.clone.1 | convolution fusion | flops 9646080 | bytes 85505 | tf_op jit(solution)/shard_map/while/body/eval_jaxpr/sc,sm->cm/dot_general | solution.py:199
  157.1 2.2 collective-permute-start.13
  160.8 4.2 %collective-permute-done.12 = f32[3,1,4,512]{3,1,2,0:T(1,128)S(1)} collective-permute-done((f32[3,1,4,512]{3,1,2,0:T(1,128)S(1)}, f32[3,1,4,512]{3,1,2,0:T(1,128)S(1)}, u32[]{:S(2)}, u32[]{:S(2)}) %collective-permute-start.12) | collective-permute-done | bytes 24608 | tf_op jit(solution)/shard_map/ppermute | solution.py:28
  166.0 4.4 %collective-permute-start.14 = (f32[3,50,1,512]{3,1,2,0:T(8,128)}, f32[3,50,1,512]{3,1,2,0:T(8,128)}, u32[]{:S(2)}, u32[]{:S(2)}) collective-permute-start(f32[3,50,1,512]{3,1,2,0:T(8,128)} %get-tuple-element.156), channel_id=1, source_target_pairs={{2,0},{4,2},{6,4},{8,6},{10,8},{12,10},{14,12},{16,14},{18,16},{20... | collective-permute-start | bytes 921608 | tf_op jit(solution)/shard_map/ppermute | solution.py:28
  170.5 32.7 %psum.23 = f32[]{:T(128)} all-reduce(f32[]{:T(128)} %get-tuple-element.183), channel_id=1, replica_groups=mesh['lon'=16,'rad'=2] {'lon'}, use_global_device_ids=true, to_apply=%region_21.22 | all-reduce | flops 1 | bytes 8 | tf_op jit(solution)/shard_map/psum | solution.py:188
  203.9 2.1 select_maximum_fusion.4
  206.2 2.8 %multiply_add_fusion = f32[3,48,4,512]{3,1,2,0:T(8,128)S(1)} fusion(f32[3,50,6,514]{3,1,2,0:T(8,128)S(1)} %select_maximum_fusion.4, f32[3,1,4,512]{3,1,2,0:T(1,128)S(1)} %copy-done.50, f32[3,48,4,512]{3,1,2,0:T(8,128)S(1)} %broadcast_multiply_fusion, f32[3,1,4,512]{3,1,2,0:T(1,128)S(1)} %copy-done.48, f32[3,4,512]{2,1,0:T(4,128)S(1)} %copy-done.51, ...), kind=kLoop, calls=%fused_computation.76 | loop fusion | flops 8257536 | bytes 7766208 | tf_op jit(solution)/shard_map/add | solution.py:219
  212.1 2.1 multiply_reduce_fusion.5
  214.2 2.2 collective-permute-done.16
  216.7 4.7 %collective-permute-start.18 = (f32[3,50,1,512]{3,1,2,0:T(8,128)S(1)}, f32[3,50,1,512]{3,1,2,0:T(8,128)S(1)}, u32[]{:S(2)}, u32[]{:S(2)}) collective-permute-start(f32[3,50,1,512]{3,1,2,0:T(8,128)S(1)} %get-tuple-element.154), channel_id=1, source_target_pairs={{2,0},{4,2},{6,4},{8,6},{10,8},{12,10},{14,12},{16,14},{18,16},{20... | collective-permute-start | bytes 921608 | tf_op jit(solution)/shard_map/ppermute | solution.py:28
  221.3 1.8 multiply_reduce_fusion.3
  223.2 2.8 %collective-permute-done.19 = f32[3,50,1,512]{3,1,2,0:T(8,128)S(1)} collective-permute-done((f32[3,50,1,512]{3,1,2,0:T(8,128)S(1)}, f32[3,50,1,512]{3,1,2,0:T(8,128)S(1)}, u32[]{:S(2)}, u32[]{:S(2)}) %collective-permute-start.19) | collective-permute-done | bytes 307232 | tf_op jit(solution)/shard_map/ppermute | solution.py:25
  229.3 2.5 %fusion.78 = (f32[48,4,512]{2,0,1:T(8,128)S(1)}, f32[48,4,512]{2,0,1:T(8,128)S(1)}, f32[48,4,512]{2,0,1:T(8,128)S(1)}, f32[48,4,512]{2,0,1:T(8,128)S(1)}) fusion(f32[3,48,4,512]{3,1,2,0:T(8,128)S(1)} %multiply_add_fusion, f32[3,1,4,512]{3,1,2,0:T(1,128)S(1)} %collective-permute-done.16, f32[3,48,4,512]{3,1,2,0:T(8,128)S(1)} %copy.52, ...), kind=kLoop, calls=%fused_computation.127 | loop fusion | flops 5505024 | bytes 9928704 | tf_op jit(solution)/shard_map/reduce_sum | solution.py:74
  (237 shorter events, 31.7 us)
Async XLA Ops:
  1.8 29.5 %copy-start.4 = (f32[1,48,4,512]{3,1,2,0:T(8,128)}, f32[1,48,4,512]{3,1,2,0:T(8,128)S(1)}, u32[]{:S(2)}) copy-start(f32[1,48,4,512]{3,1,2,0:T(8,128)S(1)} %fusion.126) | copy-start | bytes 1179652
  1.8 20.0 %collective-permute-start.2 = (f32[1,1,4,512]{3,1,2,0:T(1,128)S(1)}, f32[1,1,4,512]{3,1,2,0:T(1,128)S(1)}, u32[]{:S(2)}, u32[]{:S(2)}) collective-permute-start(f32[1,1,4,512]{3,1,2,0:T(1,128)S(1)} %get-tuple-element.177), channel_id=1, source_target_pairs={{0,1},{2,3},{4,5},{6,7},{8,9},{10,11},{12,13},{14,15},{16,17},{18,... | collective-permute-start | bytes 24584 | tf_op jit(solution)/shard_map/ppermute | solution.py:25
  6.7 12.5 %copy-start.58 = (s32[12]{0:T(128)S(1)}, s32[12]{0:T(128)}, u32[]{:S(2)}) copy-start(s32[12]{0:T(128)} %param.17) | copy-start | bytes 148
  6.7 15.1 %collective-permute-start = (f32[1,1,4,512]{3,1,2,0:T(1,128)S(1)}, f32[1,1,4,512]{3,1,2,0:T(1,128)S(1)}, u32[]{:S(2)}, u32[]{:S(2)}) collective-permute-start(f32[1,1,4,512]{3,1,2,0:T(1,128)S(1)} %get-tuple-element.178), channel_id=1, source_target_pairs={{1,0},{3,2},{5,4},{7,6},{9,8},{11,10},{13,12},{15,14},{17,16},{19,... | collective-permute-start | bytes 24584 | tf_op jit(solution)/shard_map/ppermute | solution.py:28
  9.7 16.6 %collective-permute-start.3 = (f32[3,1,4,512]{3,1,2,0:T(1,128)S(1)}, f32[3,1,4,512]{3,1,2,0:T(1,128)S(1)}, u32[]{:S(2)}, u32[]{:S(2)}) collective-permute-start(f32[3,1,4,512]{3,1,2,0:T(1,128)S(1)} %get-tuple-element.167), channel_id=1, source_target_pairs={{0,1},{2,3},{4,5},{6,7},{8,9},{10,11},{12,13},{14,15},{16,17},{18,... | collective-permute-start | bytes 73736 | tf_op jit(solution)/shard_map/ppermute | solution.py:25
  14.2 12.1 %collective-permute-start.1 = (f32[3,1,4,512]{3,1,2,0:T(1,128)S(1)}, f32[3,1,4,512]{3,1,2,0:T(1,128)S(1)}, u32[]{:S(2)}, u32[]{:S(2)}) collective-permute-start(f32[3,1,4,512]{3,1,2,0:T(1,128)S(1)} %get-tuple-element.168), channel_id=1, source_target_pairs={{1,0},{3,2},{5,4},{7,6},{9,8},{11,10},{13,12},{15,14},{17,16},{19,... | collective-permute-start | bytes 73736 | tf_op jit(solution)/shard_map/ppermute | solution.py:28
  21.8 9.1 %collective-permute-start.6 = (f32[1,50,1,512]{3,1,2,0:T(8,128)S(1)}, f32[1,50,1,512]{3,1,2,0:T(8,128)S(1)}, u32[]{:S(2)}, u32[]{:S(2)}) collective-permute-start(f32[1,50,1,512]{3,1,2,0:T(8,128)S(1)} %get-tuple-element.173), channel_id=1, source_target_pairs={{0,2},{2,4},{4,6},{6,8},{8,10},{10,12},{12,14},{14,16},{16,18},{18... | collective-permute-start | bytes 307208 | tf_op jit(solution)/shard_map/ppermute | solution.py:25
  21.9 9.1 %collective-permute-start.4 = (f32[1,50,1,512]{3,1,2,0:T(8,128)S(1)}, f32[1,50,1,512]{3,1,2,0:T(8,128)S(1)}, u32[]{:S(2)}, u32[]{:S(2)}) collective-permute-start(f32[1,50,1,512]{3,1,2,0:T(8,128)S(1)} %get-tuple-element.174), channel_id=1, source_target_pairs={{2,0},{4,2},{6,4},{8,6},{10,8},{12,10},{14,12},{16,14},{18,16},{20... | collective-permute-start | bytes 307208 | tf_op jit(solution)/shard_map/ppermute | solution.py:28
  26.3 10.6 %copy-start.39 = (f32[3,1,4,512]{3,1,2,0:T(1,128)}, f32[3,1,4,512]{3,1,2,0:T(1,128)S(1)}, u32[]{:S(2)}) copy-start(f32[3,1,4,512]{3,1,2,0:T(1,128)S(1)} %collective-permute-done.3) | copy-start | bytes 73732
  26.3 10.6 %copy-start.41 = (f32[3,1,4,512]{3,1,2,0:T(1,128)}, f32[3,1,4,512]{3,1,2,0:T(1,128)S(1)}, u32[]{:S(2)}) copy-start(f32[3,1,4,512]{3,1,2,0:T(1,128)S(1)} %collective-permute-done.1) | copy-start | bytes 73732
  26.5 9.5 %collective-permute-start.7 = (f32[3,50,1,512]{3,1,2,0:T(8,128)S(1)}, f32[3,50,1,512]{3,1,2,0:T(8,128)S(1)}, u32[]{:S(2)}, u32[]{:S(2)}) collective-permute-start(f32[3,50,1,512]{3,1,2,0:T(8,128)S(1)} %get-tuple-element.159), channel_id=1, source_target_pairs={{0,2},{2,4},{4,6},{6,8},{8,10},{10,12},{12,14},{14,16},{16,18},{18... | collective-permute-start | bytes 921608 | tf_op jit(solution)/shard_map/ppermute | solution.py:25
  26.5 9.5 %collective-permute-start.5 = (f32[3,50,1,512]{3,1,2,0:T(8,128)S(1)}, f32[3,50,1,512]{3,1,2,0:T(8,128)S(1)}, u32[]{:S(2)}, u32[]{:S(2)}) collective-permute-start(f32[3,50,1,512]{3,1,2,0:T(8,128)S(1)} %get-tuple-element.160), channel_id=1, source_target_pairs={{2,0},{4,2},{6,4},{8,6},{10,8},{12,10},{14,12},{16,14},{18,16},{20... | collective-permute-start | bytes 921608 | tf_op jit(solution)/shard_map/ppermute | solution.py:28
  32.3 44.2 %copy-start.8 = (f32[48,4,512]{2,0,1:T(8,128)}, f32[48,4,512]{2,0,1:T(8,128)S(1)}, u32[]{:S(2)}) copy-start(f32[48,4,512]{2,0,1:T(8,128)S(1)} %get-tuple-element.169) | copy-start | bytes 1179652
  32.3 44.2 %copy-start.10 = (f32[48,4,512]{2,0,1:T(8,128)}, f32[48,4,512]{2,0,1:T(8,128)S(1)}, u32[]{:S(2)}) copy-start(f32[48,4,512]{2,0,1:T(8,128)S(1)} %get-tuple-element.170) | copy-start | bytes 1179652
  37.0 27.5 %copy-start.59 = (u32[32]{0:T(128)S(1)}, u32[32]{0:T(128)}, u32[]{:S(2)}) copy-start(u32[32]{0:T(128)} %constant.164) | copy-start | bytes 388
  38.8 27.0 %collective-permute-start.9 = (f32[3,1,4,512]{3,1,2,0:T(1,128)S(1)}, f32[3,1,4,512]{3,1,2,0:T(1,128)S(1)}, u32[]{:S(2)}, u32[]{:S(2)}) collective-permute-start(f32[3,1,4,512]{3,1,2,0:T(1,128)S(1)} %get-tuple-element.165), channel_id=1, source_target_pairs={{0,1},{2,3},{4,5},{6,7},{8,9},{10,11},{12,13},{14,15},{16,17},{18,... | collective-permute-start | bytes 73736 | tf_op jit(solution)/shard_map/ppermute | solution.py:25
  43.4 22.5 %collective-permute-start.8 = (f32[3,1,4,512]{3,1,2,0:T(1,128)S(1)}, f32[3,1,4,512]{3,1,2,0:T(1,128)S(1)}, u32[]{:S(2)}, u32[]{:S(2)}) collective-permute-start(f32[3,1,4,512]{3,1,2,0:T(1,128)S(1)} %get-tuple-element.166), channel_id=1, source_target_pairs={{1,0},{3,2},{5,4},{7,6},{9,8},{11,10},{13,12},{15,14},{17,16},{19,... | collective-permute-start | bytes 73736 | tf_op jit(solution)/shard_map/ppermute | solution.py:28
  65.8 10.6 %copy-start.43 = (f32[3,1,4,512]{3,1,2,0:T(1,128)}, f32[3,1,4,512]{3,1,2,0:T(1,128)S(1)}, u32[]{:S(2)}) copy-start(f32[3,1,4,512]{3,1,2,0:T(1,128)S(1)} %collective-permute-done.9) | copy-start | bytes 73732
  65.8 10.6 %copy-start.45 = (f32[3,1,4,512]{3,1,2,0:T(1,128)}, f32[3,1,4,512]{3,1,2,0:T(1,128)S(1)}, u32[]{:S(2)}) copy-start(f32[3,1,4,512]{3,1,2,0:T(1,128)S(1)} %collective-permute-done.8) | copy-start | bytes 73732
  66.0 9.5 %collective-permute-start.11 = (f32[3,50,1,512]{3,1,2,0:T(8,128)S(1)}, f32[3,50,1,512]{3,1,2,0:T(8,128)S(1)}, u32[]{:S(2)}, u32[]{:S(2)}) collective-permute-start(f32[3,50,1,512]{3,1,2,0:T(8,128)S(1)} %get-tuple-element.157), channel_id=1, source_target_pairs={{0,2},{2,4},{4,6},{6,8},{8,10},{10,12},{12,14},{14,16},{16,18},{18... | collective-permute-start | bytes 921608 | tf_op jit(solution)/shard_map/ppermute | solution.py:25
  66.4 9.1 %collective-permute-start.10 = (f32[3,50,1,512]{3,1,2,0:T(8,128)S(1)}, f32[3,50,1,512]{3,1,2,0:T(8,128)S(1)}, u32[]{:S(2)}, u32[]{:S(2)}) collective-permute-start(f32[3,50,1,512]{3,1,2,0:T(8,128)S(1)} %get-tuple-element.158), channel_id=1, source_target_pairs={{2,0},{4,2},{6,4},{8,6},{10,8},{12,10},{14,12},{16,14},{18,16},{20... | collective-permute-start | bytes 921608 | tf_op jit(solution)/shard_map/ppermute | solution.py:28
  89.3 40.9 %copy-start.55 = (f32[3,12]{1,0:T(4,128)S(1)}, f32[3,12]{1,0:T(4,128)}, u32[]{:S(2)}) copy-start(f32[3,12]{1,0:T(4,128)} %param.19) | copy-start | bytes 436
  89.3 40.9 %copy-start.56 = (f32[3,12]{1,0:T(4,128)S(1)}, f32[3,12]{1,0:T(4,128)}, u32[]{:S(2)}) copy-start(f32[3,12]{1,0:T(4,128)} %param.18) | copy-start | bytes 436
  157.1 3.7 %collective-permute-start.13 = (f32[3,1,4,512]{3,1,2,0:T(1,128)S(1)}, f32[3,1,4,512]{3,1,2,0:T(1,128)S(1)}, u32[]{:S(2)}, u32[]{:S(2)}) collective-permute-start(f32[3,1,4,512]{3,1,2,0:T(1,128)S(1)} %get-tuple-element.163), channel_id=1, source_target_pairs={{0,1},{2,3},{4,5},{6,7},{8,9},{10,11},{12,13},{14,15},{16,17},{18,... | collective-permute-start | bytes 73736 | tf_op jit(solution)/shard_map/ppermute | solution.py:25
  159.3 5.7 %collective-permute-start.12 = (f32[3,1,4,512]{3,1,2,0:T(1,128)S(1)}, f32[3,1,4,512]{3,1,2,0:T(1,128)S(1)}, u32[]{:S(2)}, u32[]{:S(2)}) collective-permute-start(f32[3,1,4,512]{3,1,2,0:T(1,128)S(1)} %get-tuple-element.164), channel_id=1, source_target_pairs={{1,0},{3,2},{5,4},{7,6},{9,8},{11,10},{13,12},{15,14},{17,16},{19,... | collective-permute-start | bytes 73736 | tf_op jit(solution)/shard_map/ppermute | solution.py:28
  166.0 37.9 %collective-permute-start.15 = (f32[3,50,1,512]{3,1,2,0:T(8,128)}, f32[3,50,1,512]{3,1,2,0:T(8,128)}, u32[]{:S(2)}, u32[]{:S(2)}) collective-permute-start(f32[3,50,1,512]{3,1,2,0:T(8,128)} %get-tuple-element.155), channel_id=1, source_target_pairs={{0,2},{2,4},{4,6},{6,8},{8,10},{10,12},{12,14},{14,16},{16,18},{18... | collective-permute-start | bytes 921608 | tf_op jit(solution)/shard_map/ppermute | solution.py:25
  166.0 37.9 %collective-permute-start.14 = (f32[3,50,1,512]{3,1,2,0:T(8,128)}, f32[3,50,1,512]{3,1,2,0:T(8,128)}, u32[]{:S(2)}, u32[]{:S(2)}) collective-permute-start(f32[3,50,1,512]{3,1,2,0:T(8,128)} %get-tuple-element.156), channel_id=1, source_target_pairs={{2,0},{4,2},{6,4},{8,6},{10,8},{12,10},{14,12},{16,14},{18,16},{20... | collective-permute-start | bytes 921608 | tf_op jit(solution)/shard_map/ppermute | solution.py:28
  209.1 5.1 %collective-permute-start.17 = (f32[3,1,4,512]{3,1,2,0:T(1,128)S(1)}, f32[3,1,4,512]{3,1,2,0:T(1,128)S(1)}, u32[]{:S(2)}, u32[]{:S(2)}) collective-permute-start(f32[3,1,4,512]{3,1,2,0:T(1,128)S(1)} %get-tuple-element.161), channel_id=1, source_target_pairs={{0,1},{2,3},{4,5},{6,7},{8,9},{10,11},{12,13},{14,15},{16,17},{18,... | collective-permute-start | bytes 73736 | tf_op jit(solution)/shard_map/ppermute | solution.py:25
  210.7 5.7 %collective-permute-start.16 = (f32[3,1,4,512]{3,1,2,0:T(1,128)S(1)}, f32[3,1,4,512]{3,1,2,0:T(1,128)S(1)}, u32[]{:S(2)}, u32[]{:S(2)}) collective-permute-start(f32[3,1,4,512]{3,1,2,0:T(1,128)S(1)} %get-tuple-element.162), channel_id=1, source_target_pairs={{1,0},{3,2},{5,4},{7,6},{9,8},{11,10},{13,12},{15,14},{17,16},{19,... | collective-permute-start | bytes 73736 | tf_op jit(solution)/shard_map/ppermute | solution.py:28
  216.5 9.4 %collective-permute-start.19 = (f32[3,50,1,512]{3,1,2,0:T(8,128)S(1)}, f32[3,50,1,512]{3,1,2,0:T(8,128)S(1)}, u32[]{:S(2)}, u32[]{:S(2)}) collective-permute-start(f32[3,50,1,512]{3,1,2,0:T(8,128)S(1)} %get-tuple-element.153), channel_id=1, source_target_pairs={{0,2},{2,4},{4,6},{6,8},{8,10},{10,12},{12,14},{14,16},{16,18},{18... | collective-permute-start | bytes 921608 | tf_op jit(solution)/shard_map/ppermute | solution.py:25
  216.6 9.5 %copy-start.28 = (f32[3,50,1,512]{3,1,2,0:T(8,128)S(1)}, f32[3,50,1,512]{3,1,2,0:T(8,128)}, u32[]{:S(2)}) copy-start(f32[3,50,1,512]{3,1,2,0:T(8,128)} %copy-done.27) | copy-start | bytes 921604
  216.7 9.4 %collective-permute-start.18 = (f32[3,50,1,512]{3,1,2,0:T(8,128)S(1)}, f32[3,50,1,512]{3,1,2,0:T(8,128)S(1)}, u32[]{:S(2)}, u32[]{:S(2)}) collective-permute-start(f32[3,50,1,512]{3,1,2,0:T(8,128)S(1)} %get-tuple-element.154), channel_id=1, source_target_pairs={{2,0},{4,2},{6,4},{8,6},{10,8},{12,10},{14,12},{16,14},{18,16},{20... | collective-permute-start | bytes 921608 | tf_op jit(solution)/shard_map/ppermute | solution.py:28
  (48 other events, 185.7 us)
where the time goes:
time: 237 us; the launch traced here: 236 us
  blocking collectives  116 us (49%)
  starting transfers between devices  46.9 us (20%)
  other arithmetic  25.5 us (11%)
  waiting for transfers between devices  18.3 us (8%)
  matrix products  10.7 us (5%)
  local copies, waits for them, and re-layouts  10.5 us (4%)
  between operations  8.2 us (3%)
    psum x1, blocking collectives, body(): lax.psum(jnp.sum(weighted * weighted), 'lon')  32.7 us
    unnamed x1, blocking collectives  31.8 us
    ppermute x10, starting transfers between devices, extended(): lax.ppermute(lax.slice_in_dim(block, 0, width, axis=dim), axis, backward)  28.5 us
    all_gather x1, blocking collectives, body(): all_feats = lax.all_gather(own_feats, 'lon', axis=0, tiled=True)  19.7 us
    ppermute x10, starting transfers between devices, extended(): lax.ppermute(lax.slice_in_dim(block, block.shape[dim] - width, None, axis...  18.4 us
    all_gather x1, blocking collectives, body(): piece = lax.all_gather(packet, 'lon', axis=0, tiled=True)  17.5 us
    ppermute x10, waiting for transfers between devices, extended(): lax.ppermute(lax.slice_in_dim(block, block.shape[dim] - width, None, axis...  11.7 us
    psum x1, blocking collectives, body(): whole_column = lax.psum(column, 'rad')  9.44 us
  transfers between devices with their start and end apart: 20, of which 7 were waited for; matrix products, arithmetic and copies ran while one was open for 4% of the time, Pallas kernels for 0%

commit v1 on v0

v1 whole, which is shorter than its diff:
```python
import functools
import math

import jax
import jax.numpy as jnp
from jax import lax
from jax.experimental import pallas as pl
from jax.experimental.pallas import tpu as pltpu
from jax.sharding import PartitionSpec as P

RELAX_RATE = 0.05
KERNEL_WIDTH = 0.1
KERNEL_WAVE = 40.0
PRIOR_WEIGHT = 0.1
COLS = 8
F32 = jnp.float32
VMEM_LIMIT = 56 * 1024 * 1024


def reciprocal(x):
    r = pl.reciprocal(x, approx=True)
    return r * (2.0 - x * r)


def sub_index(width):
    return lax.broadcasted_iota(jnp.int32, (8, width), 0)


def lat_next(x):
    return pltpu.roll(x, x.shape[1] - 1, 1)


def lat_prev(x):
    return pltpu.roll(x, 1, 1)


def lon_next(x):
    return pltpu.roll(x, 7, 0)


def lon_prev(x):
    return pltpu.roll(x, 1, 0)


def swap_halves(x):
    return pltpu.roll(x, 4, 0)


def pack(low, high):
    return jnp.concatenate([low, high], axis=0)


def site_kernel(d):
    x = 1.0 + d * (1.0 / KERNEL_WIDTH)
    turns = d * (KERNEL_WAVE / (2.0 * math.pi))
    u = turns - jnp.round(turns)
    z = u * u
    p = 0.0821458866
    p = p * z - 0.599264529
    p = p * z + 2.55016404
    p = p * z - 5.16771278
    p = p * z + 3.14159265
    s = p * u
    return (reciprocal(x) + 0.5) - s * s


def weights_kernel(sites_ref, lat_ref, out_ref):
    width = lat_ref.shape[1]
    cos_lat = lat_ref[0:1, :]
    sin_lat = lat_ref[1:2, :]

    def chunk(j, carry):
        rows = pl.ds(pl.multiple_of(j * 8, 8), 8)
        cols = sites_ref[rows, :]
        a = 2.0 + cols[:, 0:1] * cos_lat
        b = cols[:, 1:2] * sin_lat
        for col in range(COLS):
            out_ref[col, rows, :] = site_kernel(a + b * cols[:, 2 + col : 3 + col])
        return carry

    lax.fori_loop(0, out_ref.shape[1] // 8, chunk, 0)


def forward_kernel(
    steps_ref, wr_ref, flag_ref, v_ref, s_ref, west_ref, east_ref, low_ref, high_ref, ice_ref, k_ref,
    fluid_ref, field_ref, fluid_side_ref, field_side_ref, next_ref, to_west_ref, to_east_ref,
    to_low_ref, to_high_ref, pred_ref,
    ge_ref, gn_ref, gw_ref, gu_ref, surf_ref,
):
    nr, nl, width = v_ref.shape
    half = nr // 2
    sub = sub_index(width)
    lon = sub % 4
    lane = lax.broadcasted_iota(jnp.int32, (8, width), 1)
    lower = sub < 4
    has_low, has_high = flag_ref[0], flag_ref[1]

    def wr_row(i):
        return jnp.where(lower, wr_ref[i + 2], wr_ref[i + half + 2])

    def side(ref, i):
        return [
            jnp.where(
                lower,
                jnp.where(lon < 2, west_ref[n, i], east_ref[n, i]),
                jnp.where(lon < 2, west_ref[n, i + half], east_ref[n, i + half]),
            )
            for n in range(4)
        ]

    def pack_row(i, carry):
        fluid_ref[i + 1] = jnp.exp(-pack(v_ref[i], v_ref[i + half]))
        sides = side(None, i)
        fluid_side_ref[i] = jnp.exp(-sides[0])
        for c in range(3):
            field_ref[c, i + 1] = pack(s_ref[c, i], s_ref[c, i + half])
            field_side_ref[c, i] = sides[1 + c]
        return carry

    lax.fori_loop(0, half, pack_row, 0)
    fluid_ref[0] = pack(has_low * jnp.exp(-low_ref[0]), jnp.exp(-v_ref[half - 1]))
    fluid_ref[half + 1] = pack(jnp.exp(-v_ref[half]), has_high * jnp.exp(-high_ref[0]))
    for c in range(3):
        field_ref[c, 0] = pack(low_ref[1 + c], s_ref[c, half - 1])
        field_ref[c, half + 1] = pack(s_ref[c, half], high_ref[1 + c])

    def face(a, b):
        return 2.0 * a * b * reciprocal(a + b)

    f_low = fluid_ref[0]
    f_first = fluid_ref[1]
    face_low = face(f_low, f_first)
    gu_ref[0] = (wr_row(0) - wr_row(-1)) * face_low

    def relax_row(i, carry):
        flux_low = carry
        f = fluid_ref[i + 1]
        f_up = fluid_ref[i + 2]
        f_side = fluid_side_ref[i]
        wr = wr_row(i)
        h_east = face(f, jnp.where(lon == 3, f_side, lon_next(f)))
        h_cut = face(f, f_side)
        h_west = jnp.where(lon == 0, h_cut, lon_prev(h_east))
        h_north = jnp.where(lane < width - 1, face(f, lat_next(f)), 0.0)
        h_up = face(f, f_up)
        ge_ref[i] = wr * h_east
        gw_ref[i] = wr * h_cut
        gn_ref[i] = wr * h_north
        gu_ref[i + 1] = (wr_row(i + 1) - wr) * h_up
        flux_out = []
        for c in range(3):
            s = field_ref[c, i + 1]
            s_side = field_side_ref[c, i]
            s_east = jnp.where(lon == 3, s_side, lon_next(s))
            s_west = jnp.where(lon == 0, s_side, lon_prev(s))
            north = h_north * (lat_next(s) - s)
            up = h_up * (field_ref[c, i + 2] - s)
            total = h_east * (s_east - s) + h_west * (s_west - s)
            total = total + (north - lat_prev(north))
            total = total + (up - flux_low[c])
            next_ref[c, i] = s + RELAX_RATE * total
            flux_out.append(up)
        return tuple(flux_out)

    first = tuple(face_low * (field_ref[c, 1] - field_ref[c, 0]) for c in range(3))
    lax.fori_loop(0, half, relax_row, first)

    load = ice_ref[steps_ref[0]] * (1.0 - has_high)
    next_ref[0, half - 1] = next_ref[0, half - 1] - pack(jnp.zeros_like(load), load)

    for c in range(3):
        top = next_ref[c, half - 1]
        to_low_ref[c] = next_ref[c, 0][0:4, :]
        to_high_ref[c] = top[4:8, :]
        below = jnp.where(lower, 0.0, swap_halves(top))

        def column_row(i, carry):
            below, column, east, north, cut = carry
            s = next_ref[c, i]
            to_west_ref[c, i] = s[0:1, :]
            to_west_ref[c, i + half] = s[4:5, :]
            to_east_ref[c, i] = s[3:4, :]
            to_east_ref[c, i + half] = s[7:8, :]
            column = column + wr_row(i) * s - RELAX_RATE * (gu_ref[i] * (s - below))
            east = east + ge_ref[i] * (jnp.where(lon == 3, 0.0, lon_next(s)) - s)
            north = north + gn_ref[i] * (lat_next(s) - s)
            cut = cut + gw_ref[i] * s
            return s, column, east, north, cut

        zero = jnp.zeros((8, width), F32)
        last, column, east, north, cut = lax.fori_loop(
            0, half, column_row, (below, zero, zero, zero, zero)
        )
        column = column + jnp.where(lower, 0.0, RELAX_RATE * (gu_ref[half] * last))
        column = column + swap_halves(column)
        east = east + swap_halves(east)
        north = north + swap_halves(north)
        cut = cut + swap_halves(cut)
        west = jnp.where(lon == 0, cut, lon_prev(east))
        own = column + RELAX_RATE * ((east - west) + (north - lat_prev(north)))
        if c == 0:
            second = ice_ref[steps_ref[1]] * ((1.0 - has_high) * wr_ref[nr + 1])
            own = own - pack(second, second)
        surf_ref[0, c : c + 1, :] = RELAX_RATE * cut[0:1, :]
        for col in range(4):
            surf_ref[col + 1, c : c + 1, :] = own[col : col + 1, :]
        surf_ref[5, c : c + 1, :] = -RELAX_RATE * east[3:4, :]

    for col in range(6):
        surf_ref[col, 3:8, :] = jnp.zeros((5, width), F32)
    total = jnp.zeros((8, k_ref.shape[1]), F32)
    for col in range(6):
        total = total + lax.dot_general(
            surf_ref[col],
            k_ref[col + 1],
            (((1,), (1,)), ((), ())),
            precision=lax.Precision.HIGHEST,
            preferred_element_type=F32,
        )

    def spread(n, carry):
        pred_ref[n] = total[0:3, :]
        return carry

    lax.fori_loop(0, pred_ref.shape[0], spread, 0)


def prepare_kernel(
    wr_ref, flag_ref, v_ref, m_ref, fluid_ref, field_ref, fluid_side_ref, field_side_ref, next_ref,
    west_ref, east_ref, low_ref, high_ref, west2_ref, east2_ref, low2_ref, high2_ref,
    d0_ref, q_ref, d0_up_ref, q_up_ref, u_ref, base_ref, own_ref, side_ref, ring_ref,
):
    nr, nl, width = v_ref.shape
    half = nr // 2
    sub = sub_index(width)
    lon = sub % 4
    lane = lax.broadcasted_iota(jnp.int32, (8, width), 1)
    lower = sub < 4
    has_low, has_high = flag_ref[0], flag_ref[1]

    def wr_row(i):
        return jnp.where(lower, wr_ref[i + 2], wr_ref[i + half + 2])

    def share(f, other):
        return other * reciprocal(f + other)

    def safe_share(f, other):
        return other * reciprocal(jnp.maximum(f + other, 1e-30))

    def pick(ref_w, ref_e, i):
        return jnp.where(
            lower,
            jnp.where(lon < 2, ref_w[i], ref_e[i]),
            jnp.where(lon < 2, ref_w[i + half], ref_e[i + half]),
        )

    def north_of(f):
        return jnp.where(lane < width - 1, lat_next(f), 0.0)

    def south_of(f):
        return jnp.where(lane > 0, lat_prev(f), 0.0)

    def coefficients(ref, f, wr, wr_up, wr_down, shares):
        scaled = (2.0 * RELAX_RATE) * f
        weighted = scaled * wr
        for n in range(4):
            ref(n, weighted * shares[n])
        ref(4, scaled * (shares[4] * (wr_up - wr) + shares[5] * (wr_down - wr)))

    def prepare_row(i, s_up, f_up):
        f = fluid_ref[i + 1]
        f_down = fluid_ref[i]
        f_side = fluid_side_ref[i]
        wr, wr_up, wr_down = wr_row(i), wr_row(i + 1), wr_row(i - 1)
        shares = [
            share(f, jnp.where(lon == 3, f_side, lon_next(f))),
            share(f, jnp.where(lon == 0, f_side, lon_prev(f))),
            share(f, north_of(f)),
            share(f, south_of(f)),
            share(f, f_up),
            share(f, f_down),
        ]

        def store_own(n, value):
            own_ref[n, i] = value

        coefficients(store_own, f, wr, wr_up, wr_down, shares)
        scaled = (-0.5 * 2.0 * RELAX_RATE) * f
        for n in range(6):
            u_ref[n, i] = scaled * (shares[n] * shares[n])
        base_ref[i] = pack(
            m_ref[i] - (0.5 * PRIOR_WEIGHT) * v_ref[i],
            m_ref[i + half] - (0.5 * PRIOR_WEIGHT) * v_ref[i + half],
        )
        f_far = jnp.exp(-pick(west2_ref, east2_ref, i))
        edge = jnp.where(lon < 2, f_far, f)
        other = jnp.where(lon < 2, f, f_far)
        up_side = fluid_side_ref[jnp.minimum(i + 1, half - 1)]
        down_side = fluid_side_ref[jnp.maximum(i - 1, 0)]
        seam_up = swap_halves(fluid_side_ref[0])
        seam_down = swap_halves(fluid_side_ref[half - 1])
        corner_low = has_low * jnp.exp(-jnp.where(lon < 2, west2_ref[nr], east2_ref[nr]))
        corner_high = has_high * jnp.exp(-jnp.where(lon < 2, west2_ref[nr + 1], east2_ref[nr + 1]))
        up_side = jnp.where(i == half - 1, jnp.where(lower, seam_up, corner_high), up_side)
        down_side = jnp.where(i == 0, jnp.where(lower, corner_low, seam_down), down_side)
        side_shares = [
            share(f_side, other),
            share(f_side, edge),
            share(f_side, north_of(f_side)),
            share(f_side, south_of(f_side)),
            share(f_side, up_side),
            share(f_side, down_side),
        ]

        def store_side(n, value):
            side_ref[n, i] = value

        coefficients(store_side, f_side, wr, wr_up, wr_down, side_shares)
        dwr = wr_up - wr
        for c in range(3):
            s0 = field_ref[c, i + 1]
            s1 = next_ref[c, i]
            s0_side = field_side_ref[c, i]
            s1_side = jnp.where(
                lower,
                jnp.where(lon < 2, west_ref[c, i], east_ref[c, i]),
                jnp.where(lon < 2, west_ref[c, i + half], east_ref[c, i + half]),
            )
            cut = s0_side - s0
            east = jnp.where(lon == 3, s0_side, lon_next(s0)) - s0
            north = lat_next(s0) - s0
            cut1 = s1_side - s1
            east1 = jnp.where(lon == 3, s1_side, lon_next(s1)) - s1
            north1 = lat_next(s1) - s1
            for n, (first, second) in enumerate(((east, east1), (cut, cut1), (north, north1))):
                d0_ref[n, c, i] = first
                q_ref[n, c, i] = wr * (first + second)
            up = field_ref[c, i + 2] - s0
            d0_up_ref[c, i + 1] = up
            q_up_ref[c, i + 1] = dwr * (up + (s_up[c] - s1))

    def loop(i, carry):
        prepare_row(i, [next_ref[c, i + 1] for c in range(3)], fluid_ref[i + 2])
        return carry

    lax.fori_loop(0, half - 1, loop, 0)
    top_rows = [pack(next_ref[c, 0][4:8, :], high_ref[c]) for c in range(3)]
    prepare_row(half - 1, top_rows, fluid_ref[half + 1])
    dwr_low = wr_row(0) - wr_row(-1)
    for c in range(3):
        low_row = pack(low_ref[c], next_ref[c, half - 1][0:4, :])
        up = field_ref[c, 1] - field_ref[c, 0]
        d0_up_ref[c, 0] = up
        q_up_ref[c, 0] = dwr_low * (up + (next_ref[c, 0] - low_row))
    ring = jnp.where(lower, fluid_ref[0], fluid_ref[half + 1])
    inner = jnp.where(lower, fluid_ref[1], fluid_ref[half])
    far = pack(has_low * jnp.exp(-low2_ref[...]), has_high * jnp.exp(-high2_ref[...]))
    corner_w = jnp.where(
        lower, has_low * jnp.exp(-west2_ref[nr]), has_high * jnp.exp(-west2_ref[nr + 1])
    )
    corner_e = jnp.where(
        lower, has_low * jnp.exp(-east2_ref[nr]), has_high * jnp.exp(-east2_ref[nr + 1])
    )
    far = jnp.where(lower, flag_ref[2] * far, flag_ref[3] * far)
    wr_ring = jnp.where(lower, wr_ref[1], wr_ref[nr + 2])
    wr_in = jnp.where(lower, wr_ref[2], wr_ref[nr + 1])
    wr_far = jnp.where(lower, wr_ref[0], wr_ref[nr + 3])
    ring_shares = [
        safe_share(ring, jnp.where(lon == 3, corner_e, lon_next(ring))),
        safe_share(ring, jnp.where(lon == 0, corner_w, lon_prev(ring))),
        safe_share(ring, north_of(ring)),
        safe_share(ring, south_of(ring)),
        safe_share(ring, far),
        safe_share(ring, inner),
    ]

    def store_ring(n, value):
        ring_ref[n] = value

    coefficients(store_ring, ring, wr_ring, wr_far, wr_in, ring_shares)


def gradient_kernel(
    v_ref, pred_ref, obs_ref, wt_ref, k_ref,
    d0_ref, q_ref, d0_up_ref, q_up_ref, u_ref, base_ref, own_ref, side_ref, ring_ref,
    new_ref, half_ref, misfit_ref,
    sa_ref, d_ref,
    *, scale,
):
    nr, nl, width = v_ref.shape
    half = nr // 2
    sites = k_ref.shape[1]
    sub = sub_index(width)
    lon = sub % 4
    lower = sub < 4

    predicted = lax.fori_loop(
        1, pred_ref.shape[0], lambda n, acc: acc + pred_ref[n], pred_ref[0]
    )
    weight = wt_ref[...]
    weighted = weight * (predicted * scale - obs_ref[...])
    squares = jnp.sum(weighted * weighted, axis=1, keepdims=True)
    squares = jnp.sum(squares, axis=0, keepdims=True)
    misfit_ref[...] = squares * (1.0 / (3 * sites))
    pulled = (weight * weighted) * scale
    pulled = jnp.concatenate([pulled, jnp.zeros((5, sites), F32)], axis=0)
    for col in range(COLS):
        spread = jnp.dot(
            pulled, k_ref[col], precision=lax.Precision.HIGHEST, preferred_element_type=F32
        )
        for c in range(3):
            sa_ref[c, col : col + 1, :] = spread[c : c + 1, :]

    for c in range(3):
        x = sa_ref[c]

        def window(start):
            return jnp.where(
                lower,
                x if start == 0 else pltpu.roll(x, 8 - start, 0),
                x if start == 4 else pltpu.roll(x, (4 - start) % 8, 0),
            )

        own = window(2)
        east = window(3)
        west = window(1)
        outside = jnp.where(lon < 2, west, east)
        d_ref[0, c] = east - own
        d_ref[1, c] = west - own
        d_ref[2, c] = lat_next(own) - own
        d_ref[3, c] = lat_prev(own) - own
        d_ref[4, c] = own
        d_ref[5, c] = jnp.where(lon < 2, own, window(4)) - outside
        d_ref[6, c] = jnp.where(lon < 2, window(0), own) - outside
        d_ref[7, c] = lat_next(outside) - outside
        d_ref[8, c] = lat_prev(outside) - outside
        d_ref[9, c] = outside

    def change(coeff, first):
        out = []
        for c in range(3):
            total = coeff(0) * d_ref[first, c]
            for n in range(1, 5):
                total = total + coeff(n) * d_ref[first + n, c]
            out.append(total)
        return out

    def own_row(i):
        return change(lambda n: own_ref[n, i], 0)

    ring = change(lambda n: ring_ref[n], 0)
    e_first = own_row(0)
    e_last = own_row(half - 1)
    e_low = [jnp.where(lower, ring[c], swap_halves(e_last[c])) for c in range(3)]
    e_high = [jnp.where(lower, swap_halves(e_first[c]), ring[c]) for c in range(3)]

    def up_product(k, e_a, e_b):
        total = None
        for c in range(3):
            term = q_up_ref[c, k] * d_ref[4, c] + d0_up_ref[c, k] * (e_b[c] - e_a[c])
            total = term if total is None else total + term
        return total

    def finish_row(i, e, e_up, p_down):
        outside = change(lambda n: side_ref[n, i], 5)
        p_up = up_product(i + 1, e, e_up)
        p_east = p_cut = p_north = None
        for c in range(3):
            to_side = outside[c] - e[c]
            to_east = jnp.where(lon == 3, outside[c], lon_next(e[c])) - e[c]
            to_north = lat_next(e[c]) - e[c]
            t_east = q_ref[0, c, i] * d_ref[0, c] + d0_ref[0, c, i] * to_east
            t_cut = q_ref[1, c, i] * d_ref[1, c] + d0_ref[1, c, i] * to_side
            t_north = q_ref[2, c, i] * d_ref[2, c] + d0_ref[2, c, i] * to_north
            p_east = t_east if p_east is None else p_east + t_east
            p_cut = t_cut if p_cut is None else p_cut + t_cut
            p_north = t_north if p_north is None else p_north + t_north
        p_west = jnp.where(lon == 0, p_cut, lon_prev(p_east))
        total = base_ref[i] + u_ref[0, i] * p_east + u_ref[1, i] * p_west
        total = total + u_ref[2, i] * p_north + u_ref[3, i] * lat_prev(p_north)
        total = total + u_ref[4, i] * p_up + u_ref[5, i] * p_down
        half_ref[i] = total[0:4, :]
        half_ref[i + half] = total[4:8, :]
        new_ref[i] = v_ref[i] + total[0:4, :]
        new_ref[i + half] = v_ref[i + half] + total[4:8, :]
        return p_up

    def loop(i, carry):
        e, p_down = carry
        e_up = own_row(i + 1)
        p_up = finish_row(i, e, e_up, p_down)
        return e_up, p_up

    e, p_down = lax.fori_loop(
        0, half - 1, loop, (e_first, up_product(0, e_low, e_first))
    )
    finish_row(half - 1, e, e_high, p_down)


def call(kernel, out_shapes, in_smem, arity, scratch=(), flops=1, name=None):
    vmem = pl.BlockSpec(memory_space=pltpu.VMEM)
    smem = pl.BlockSpec(memory_space=pltpu.SMEM)
    return pl.pallas_call(
        kernel,
        out_shape=[jax.ShapeDtypeStruct(s, F32) for s in out_shapes],
        in_specs=[smem] * in_smem + [vmem] * (arity - in_smem),
        out_specs=[vmem] * len(out_shapes),
        scratch_shapes=[pltpu.VMEM(s, F32) for s in scratch],
        compiler_params=pltpu.CompilerParams(vmem_limit_bytes=VMEM_LIMIT),
        cost_estimate=pl.CostEstimate(flops=flops, bytes_accessed=1 << 20, transcendentals=0),
        name=name,
    )


def body(
    logvisc, momentum, displacement, ice_history, load_steps, site_cells, observed, site_weight
):
    nr, nl, nlat = logvisc.shape
    own_sites = site_cells.shape[0]
    lon_n = lax.axis_size("lon")
    rad_n = lax.axis_size("rad")
    total_rad = nr * rad_n
    total_lon = nl * lon_n
    sites = own_sites * lon_n
    devices = lon_n * rad_n
    half = nr // 2
    scale = 1.0 / math.sqrt(total_lon * nlat)
    rad_at = lax.axis_index("rad")
    lon_at = lax.axis_index("lon")

    packet = jnp.concatenate(
        [site_cells.astype(F32)[None, :], observed, site_weight], axis=0
    )
    gathered = lax.all_to_all(
        jnp.broadcast_to(packet[None], (lon_n,) + packet.shape), "lon", 0, 0
    )

    fields = jnp.concatenate([logvisc[None], displacement], axis=0)
    eastward = [(i, (i + 1) % lon_n) for i in range(lon_n)]
    westward = [(t, s) for s, t in eastward]
    upward = [(i, i + 1) for i in range(rad_n - 1)]
    downward = [(t, s) for s, t in upward]
    west = lax.ppermute(fields[:, :, nl - 1 : nl, :], "lon", eastward)
    east = lax.ppermute(fields[:, :, 0:1, :], "lon", westward)
    low = lax.ppermute(
        jnp.concatenate([fields[:, nr - 1], logvisc[None, nr - 2]], axis=0), "rad", upward
    )
    high = lax.ppermute(
        jnp.concatenate([fields[:, 0], logvisc[None, 1]], axis=0), "rad", downward
    )

    layers = (rad_at * nr - 2 + jnp.arange(nr + 4)).astype(F32)
    wr = jnp.exp(4.0 * (layers - (total_rad - 1)) / total_rad)
    flags = jnp.stack(
        [rad_at > 0, rad_at < rad_n - 1, rad_at * nr > 1, rad_at * nr + nr + 1 < total_rad]
    ).astype(F32)

    lat_angle = math.pi * (jnp.arange(nlat).astype(F32) + 0.5) / nlat
    lat_rows = jnp.stack([jnp.cos(lat_angle), jnp.sin(lat_angle)])
    col_index = (lon_at * nl - 2 + jnp.arange(COLS) + total_lon) % total_lon
    col_angle = 2.0 * math.pi * col_index.astype(F32) / total_lon
    cells = gathered[:, 0].reshape(sites)
    cell_index = cells.astype(jnp.int32)
    lon_index = cell_index // nlat
    site_angle = math.pi * ((cell_index - lon_index * nlat).astype(F32) + 0.5) / nlat
    site_phi = 2.0 * math.pi * lon_index.astype(F32) / total_lon
    columns = jnp.concatenate(
        [
            (-2.0 * jnp.cos(site_angle))[:, None],
            (-2.0 * jnp.sin(site_angle))[:, None],
            jnp.cos(site_phi)[:, None] * jnp.cos(col_angle)[None, :]
            + jnp.sin(site_phi)[:, None] * jnp.sin(col_angle)[None, :],
        ],
        axis=1,
    )
    (weights,) = call(
        weights_kernel, [(COLS, sites, nlat)], 0, 2, flops=20000000, name="site_weights"
    )(columns, lat_rows)
    obs_all = gathered[:, 1:4].transpose(1, 0, 2).reshape(3, sites)
    wt_all = gathered[:, 4:7].transpose(1, 0, 2).reshape(3, sites)

    row = (8, nlat)
    (
        fluid, field, fluid_side, field_side, state, to_west, to_east, to_low, to_high, partial,
    ) = call(
        forward_kernel,
        [
            (half + 2,) + row,
            (3, half + 2) + row,
            (half,) + row,
            (3, half) + row,
            (3, half) + row,
            (3, nr, 1, nlat),
            (3, nr, 1, nlat),
            (3, nl, nlat),
            (3, nl, nlat),
            (devices, 3, sites),
        ],
        3,
        11,
        scratch=[(half,) + row, (half,) + row, (half,) + row, (half + 1,) + row, (6,) + row],
        flops=20000000,
        name="forward",
    )(
        load_steps, wr, flags, logvisc, displacement, west, east, low, high, ice_history, weights
    )

    predicted = lax.all_to_all(partial, ("lon", "rad"), 0, 0)

    west_next = lax.ppermute(to_east, "lon", eastward)
    east_next = lax.ppermute(to_west, "lon", westward)
    corners_w = jnp.stack([low[0, 0:1], high[0, 0:1]])
    corners_e = jnp.stack([low[0, nl - 1 : nl], high[0, nl - 1 : nl]])
    west_far = lax.ppermute(
        jnp.concatenate([logvisc[:, nl - 2 : nl - 1], corners_e]), "lon", eastward
    )
    east_far = lax.ppermute(jnp.concatenate([logvisc[:, 1:2], corners_w]), "lon", westward)
    low_next = lax.ppermute(to_high, "rad", upward)
    high_next = lax.ppermute(to_low, "rad", downward)

    prepared = call(
        prepare_kernel,
        [
            (3, 3, half) + row,
            (3, 3, half) + row,
            (3, half + 1) + row,
            (3, half + 1) + row,
            (6, half) + row,
            (half,) + row,
            (5, half) + row,
            (5, half) + row,
            (5,) + row,
        ],
        2,
        17,
        flops=40000000,
        name="prepare",
    )(
        wr, flags, logvisc, momentum, fluid, field, fluid_side, field_side, state,
        west_next, east_next, low_next, high_next, west_far, east_far, low[4], high[4],
    )

    new_logvisc, half_momentum, misfit = call(
        functools.partial(gradient_kernel, scale=scale),
        [(nr, nl, nlat), (nr, nl, nlat), (1, 1)],
        0,
        14,
        scratch=[(3,) + row, (10, 3) + row],
        flops=20000000,
        name="gradient",
    )(logvisc, predicted, obs_all, wt_all, weights, *prepared)
    return (new_logvisc, half_momentum, misfit.reshape(1))


def solution(mesh):
    return jax.shard_map(
        body,
        mesh=mesh,
        in_specs=(
            P("rad", "lon", None),
            P("rad", "lon", None),
            P(None, "rad", "lon", None),
            P(None, "lon", None),
            P(),
            P("lon"),
            P(None, "lon"),
            P(None, "lon"),
        ),
        out_specs=(P("rad", "lon", None), P("rad", "lon", None), P()),
        check_vma=False,
    )
```

time: 237 us -> 104 us (0.44)
  blocking collectives: 116 us -> 0 us
  Pallas kernels: 0 us -> 49.7 us
  other arithmetic: 25.5 us -> 5.87 us
  waiting for transfers between devices: 18.3 us -> 3.34 us
  starting transfers between devices: 46.9 us -> 33.1 us
  matrix products: 10.7 us -> 0 us
  between operations: 8.2 us -> 0.98 us
    pallas_call x0 -> x4, Pallas kernels: none -> 49.7 us  [the longest x1 17.3 us: body(): call(forward_kernel, [(half + 2,) + row, (3, half + 2) + row, (half,) + r...]
    psum x3 -> x0, blocking collectives: 47 us -> none  [the longest x1 32.7 us: body(): lax.psum(jnp.sum(weighted * weighted), 'lon')]
    all_gather x2 -> x0, blocking collectives: 37.2 us -> none  [the longest x1 19.7 us: body(): all_feats = lax.all_gather(own_feats, 'lon', axis=0, tiled=True)]
    unnamed x1 -> x0, blocking collectives: 31.8 us -> none
    ppermute x20 -> x10, starting transfers between devices: 46.9 us -> 23 us  [the longest x1 4.49 us: body(): lax.ppermute(jnp.concatenate([logvisc[:, 1:2], corners_w]), 'lon', westward)]
    ppermute x20 -> x10, waiting for transfers between devices: 18.3 us -> 3.34 us  [the longest x1 3.31 us: body(): high_next = lax.ppermute(to_low, 'rad', downward)]
    dot_general x4 -> x0, matrix products: 10.7 us -> none  [the longest x2 6.86 us: add_block(): jnp.einsum('sc,sm->cm', block[:, 3:], weights, precision=lax.Precision.HI...]
    all_to_all x0 -> x2, starting transfers between devices: none -> 10.1 us  [the longest x1 7.39 us: body(): lax.all_to_all(jnp.broadcast_to(packet[None], (lon_n,) + packet.shape), '...]
  transfers between devices with their start and end apart: 20 -> 12, of which waited for: 7 -> 1; matrix products, arithmetic and copies ran while one was open for 4% -> 12% of each run, Pallas kernels for 0% -> 35%
where the time goes in v1:
time: 104 us; the launch traced here: 103 us
  Pallas kernels  49.7 us (48%)
  starting transfers between devices  33.1 us (32%)
  local copies, waits for them, and re-layouts  9.95 us (10%)
  other arithmetic  5.87 us (6%)
  waiting for transfers between devices  3.34 us (3%)
    pallas_call x1, Pallas kernels, body(): call(forward_kernel, [(half + 2,) + row, (3, half + 2) + row, (half,) + r...  17.3 us
    pallas_call x1, Pallas kernels, body(): call(functools.partial(gradient_kernel, scale=scale), [(nr, nl, nlat), (n...  13.6 us
    pallas_call x1, Pallas kernels, body(): call(prepare_kernel, [(3, 3, half) + row, (3, 3, half) + row, (3, half +...  11.8 us
    all_to_all x1, starting transfers between devices, body(): lax.all_to_all(jnp.broadcast_to(packet[None], (lon_n,) + packet.shape), '...  7.39 us
    pallas_call x1, Pallas kernels, body(): call(weights_kernel, [(COLS, sites, nlat)], 0, 2, flops=20000000, name='s...  6.97 us
    ppermute x1, starting transfers between devices, body(): lax.ppermute(jnp.concatenate([logvisc[:, 1:2], corners_w]), 'lon', westward)  4.49 us
    ppermute x1, starting transfers between devices, body(): east_next = lax.ppermute(to_west, 'lon', westward)  4.43 us
    ppermute x1, starting transfers between devices, body(): east = lax.ppermute(fields[:, :, 0:1, :], 'lon', westward)  4.15 us
  transfers between devices with their start and end apart: 12, of which 1 were waited for; matrix products, arithmetic and copies ran while one was open for 12% of the time, Pallas kernels for 35%

profile of v1, /device:TPU:0, one launch (start us, length us, event | category | flops | bytes accessed | tf_op | source)
XLA Modules:
  0.0 102.9 jit_solution(6779302885573604184)
XLA Ops:
  0.7 0.8 convert_bitcast_fusion
  1.4 0.7 pad_maximum_fusion.6
  2.1 0.6 broadcast_in_dim.8
  2.8 7.4 %all-to-all-start = ((f32[16,7,12]{2,1,0:T(8,128)}), f32[16,7,12]{2,1,0:T(8,128)S(1)}, u32[]{:S(2)}, u32[]{:S(2)}) async-start(f32[16,7,12]{2,1,0:T(8,128)} %broadcast_in_dim.8), calls=%async_computation | async-start | bytes 131072 | tf_op jit(solution)/shard_map/all_to_all | solution.py:534
  10.2 0.7 fusion.15
  10.9 0.8 fusion.3
  11.7 3.4 %collective-permute-start.2 = (f32[5,4,512]{2,1,0:T(4,128)S(1)}, f32[5,4,512]{2,1,0:T(4,128)S(1)}, u32[]{:S(2)}, u32[]{:S(2)}) collective-permute-start(f32[5,4,512]{2,1,0:T(4,128)S(1)} %pad_maximum_fusion.2), channel_id=1, source_target_pairs={{0,1},{2,3},{4,5},{6,7},{8,9},{10,11},{12,13},{14,15},{16,17},{18,... | collective-permute-start | bytes 122888 | tf_op jit(solution)/shard_map/ppermute | solution.py:545
  15.1 0.6 pad_maximum_fusion.3
  15.7 1.3 %collective-permute-start.3 = (f32[5,4,512]{2,1,0:T(4,128)}, f32[5,4,512]{2,1,0:T(4,128)S(1)}, u32[]{:S(2)}, u32[]{:S(2)}) collective-permute-start(f32[5,4,512]{2,1,0:T(4,128)} %pad_maximum_fusion.3), channel_id=1, source_target_pairs={{1,0},{3,2},{5,4},{7,6},{9,8},{11,10},{13,12},{15,14},{17,16},{19,... | collective-permute-start | bytes 122888 | tf_op jit(solution)/shard_map/ppermute | solution.py:548
  17.1 0.7 fusion.1
  17.7 4.2 %collective-permute-start.1 = (f32[4,48,1,512]{3,2,0,1:T(1,128)S(1)}, f32[4,48,1,512]{3,2,0,1:T(1,128)S(1)}, u32[]{:S(2)}, u32[]{:S(2)}) collective-permute-start(f32[4,48,1,512]{3,2,0,1:T(1,128)S(1)} %get-tuple-element.53), channel_id=1, source_target_pairs={{2,0},{4,2},{6,4},{8,6},{10,8},{12,10},{14,12},{16,14},{18,16},{20... | collective-permute-start | bytes 1179656 | tf_op jit(solution)/shard_map/ppermute | solution.py:544
  22.7 0.6 pad_maximum_fusion.7.lat_ref
  23.3 0.6 add_convert_fusion.flag_ref
  24.5 0.7 reshape.157.wt_ref
  25.2 0.7 reshape.156.obs_ref
  25.9 0.8 copy.23.sites_ref
  26.6 7.0 %site_weights.1.k_ref = f32[8,192,512]{2,1,0:T(8,128)} custom-call(f32[192,10]{1,0:T(8,128)} %copy.23.sites_ref, f32[2,512]{1,0:T(2,128)} %pad_maximum_fusion.7.lat_ref), custom_call_target="tpu_custom_call" | custom-call | flops 20000000 | bytes 1048576 | tf_op jit(solution)/shard_map/site_weights/pallas_call | solution.py:576
  33.9 4.5 %collective-permute-start.9 = (f32[50,1,512]{2,1,0:T(1,128)S(1)}, f32[50,1,512]{2,1,0:T(1,128)S(1)}, u32[]{:S(2)}, u32[]{:S(2)}) collective-permute-start(f32[50,1,512]{2,1,0:T(1,128)S(1)} %pad_maximum_fusion.1), channel_id=1, source_target_pairs={{2,0},{4,2},{6,4},{8,6},{10,8},{12,10},{14,12},{16,14},{18,16},{20... | collective-permute-start | bytes 307208 | tf_op jit(solution)/shard_map/ppermute | solution.py:617
  38.4 1.0 copy.25.east_ref
  39.4 1.0 copy.24.west_ref
  40.4 17.3 %forward.1 = (f32[26,8,512]{2,1,0:T(8,128)}, f32[3,26,8,512]{3,2,1,0:T(8,128)}, f32[24,8,512]{2,1,0:T(8,128)}, f32[3,24,8,512]{3,2,1,0:T(8,128)}, f32[3,24,8,512...) custom-call(s32[2]{0:T(128)} %steps_ref.1, ...), custom_call_target="tpu_custom_call" | custom-call | flops 20000000 | bytes 1048576 | tf_op jit(solution)/shard_map/forward/pallas_call | solution.py:585
  57.8 4.4 %collective-permute-start.5 = (f32[3,48,1,512]{3,2,1,0:T(1,128)}, f32[3,48,1,512]{3,2,1,0:T(1,128)S(1)}, u32[]{:S(2)}, u32[]{:S(2)}) collective-permute-start(f32[3,48,1,512]{3,2,1,0:T(1,128)} %get-tuple-element.32), channel_id=1, source_target_pairs={{2,0},{4,2},{6,4},{8,6},{10,8},{12,10},{14,12},{16,14},{18,16},{20... | collective-permute-start | bytes 884744 | tf_op jit(solution)/shard_map/ppermute | solution.py:611
  62.2 1.3 %slice_bitcast_fusion.3.low2_ref = f32[4,512]{1,0:T(4,128)} fusion(f32[5,4,512]{2,1,0:T(4,128)} %copy-done.8), kind=kLoop, calls=%fused_computation.20 | loop fusion | bytes 16384 | tf_op jit(solution)/shard_map/squeeze | solution.py:640
  63.5 2.7 %all-to-all-start.1 = ((f32[32,3,192]{2,1,0:T(4,128)}), f32[32,3,192]{2,1,0:T(4,128)S(1)}, u32[]{:S(2)}, u32[]{:S(2)}) async-start(f32[32,3,192]{2,1,0:T(4,128)} %get-tuple-element.25), calls=%async_computation.1 | async-start | bytes 262144 | tf_op jit(solution)/shard_map/all_to_all | solution.py:608
  66.2 3.8 %collective-permute-start.6 = (f32[3,4,512]{2,1,0:T(4,128)}, f32[3,4,512]{2,1,0:T(4,128)S(1)}, u32[]{:S(2)}, u32[]{:S(2)}) collective-permute-start(f32[3,4,512]{2,1,0:T(4,128)} %get-tuple-element.33), channel_id=1, source_target_pairs={{0,1},{2,3},{4,5},{6,7},{8,9},{10,11},{12,13},{14,15},{16,17},{18,... | collective-permute-start | bytes 73736 | tf_op jit(solution)/shard_map/ppermute | solution.py:618
  70.1 1.3 %collective-permute-start.7 = (f32[3,4,512]{2,1,0:T(4,128)}, f32[3,4,512]{2,1,0:T(4,128)S(1)}, u32[]{:S(2)}, u32[]{:S(2)}) collective-permute-start(f32[3,4,512]{2,1,0:T(4,128)} %get-tuple-element.34), channel_id=1, source_target_pairs={{1,0},{3,2},{5,4},{7,6},{9,8},{11,10},{13,12},{15,14},{17,16},{19,... | collective-permute-start | bytes 73736 | tf_op jit(solution)/shard_map/ppermute | solution.py:619
  71.4 1.3 %slice_bitcast_fusion.2.high2_ref = f32[4,512]{1,0:T(4,128)} fusion(f32[5,4,512]{2,1,0:T(4,128)} %copy-done.7), kind=kLoop, calls=%fused_computation.19 | loop fusion | bytes 16384 | tf_op jit(solution)/shard_map/squeeze | solution.py:640
  72.7 3.3 %collective-permute-done.7.high_ref = f32[3,4,512]{2,1,0:T(4,128)S(1)} collective-permute-done((f32[3,4,512]{2,1,0:T(4,128)}, f32[3,4,512]{2,1,0:T(4,128)S(1)}, u32[]{:S(2)}, u32[]{:S(2)}) %collective-permute-start.7) | collective-permute-done | bytes 24608 | tf_op jit(solution)/shard_map/ppermute | solution.py:619
  76.1 0.5 copy-done.10
  76.8 11.8 %prepare.1 = (f32[3,3,24,8,512]{4,3,2,1,0:T(8,128)}, f32[3,3,24,8,512]{4,3,2,1,0:T(8,128)}, f32[3,25,8,512]{3,2,1,0:T(8,128)}, f32[3,25,8,512]{3,2,1,0:T(8,128)}...) custom-call(f32[52]{0:T(128)} %multiply_exponential_fusion.wr_ref, ...), custom_call_target="tpu_custom_call" | custom-call | flops 40000000 | bytes 1048576 | tf_op jit(solution)/shard_map/prepare/pallas_call | solution.py:621
  88.7 0.6 copy-done.2
  89.3 13.6 %gradient.1 = (f32[48,4,512]{2,1,0:T(4,128)}, f32[48,4,512]{2,1,0:T(4,128)}, f32[1,1]{1,0:T(1,128)}) custom-call(f32[48,4,512]{2,1,0:T(4,128)} %v_ref.5, f32[32,3,192]{2,1,0:T(4,128)} %copy-done.2, f32[3,192]{1,0:T(4,128)} %reshape.156.obs_ref, f32[3,192]{1,0:T(4,128)} %reshape.157.wt_ref, f32[8,192,512]{2,1,0:T(8,128)} %site_weights.1.k_ref, ...), custom_call_target="tpu_custom_call" | custom-call | flops 20000000 | bytes 1048576 | tf_op jit(solution)/shard_map/gradient/pallas_call | solution.py:643
  (56 shorter events, 1.9 us)
Async XLA Ops:
  0.6 16.4 %copy-start = (f32[48,4,512]{2,1,0:T(4,128)S(1)}, f32[48,4,512]{2,1,0:T(4,128)}, u32[]{:S(2)}) copy-start(f32[48,4,512]{2,1,0:T(4,128)} %v_ref.5) | copy-start | bytes 1179652
  0.6 16.4 %copy-start.1 = (f32[3,48,4,512]{3,2,1,0:T(4,128)S(1)}, f32[3,48,4,512]{3,2,1,0:T(4,128)}, u32[]{:S(2)}) copy-start(f32[3,48,4,512]{3,2,1,0:T(4,128)} %s_ref.1) | copy-start | bytes 3538948
  2.8 21.1 %all-to-all-start = ((f32[16,7,12]{2,1,0:T(8,128)}), f32[16,7,12]{2,1,0:T(8,128)S(1)}, u32[]{:S(2)}, u32[]{:S(2)}) async-start(f32[16,7,12]{2,1,0:T(8,128)} %broadcast_in_dim.8), calls=%async_computation | async-start | bytes 131072 | tf_op jit(solution)/shard_map/all_to_all | solution.py:534
  11.7 21.9 %collective-permute-start.2 = (f32[5,4,512]{2,1,0:T(4,128)S(1)}, f32[5,4,512]{2,1,0:T(4,128)S(1)}, u32[]{:S(2)}, u32[]{:S(2)}) collective-permute-start(f32[5,4,512]{2,1,0:T(4,128)S(1)} %pad_maximum_fusion.2), channel_id=1, source_target_pairs={{0,1},{2,3},{4,5},{6,7},{8,9},{10,11},{12,13},{14,15},{16,17},{18,... | collective-permute-start | bytes 122888 | tf_op jit(solution)/shard_map/ppermute | solution.py:545
  15.7 17.8 %collective-permute-start.3 = (f32[5,4,512]{2,1,0:T(4,128)}, f32[5,4,512]{2,1,0:T(4,128)S(1)}, u32[]{:S(2)}, u32[]{:S(2)}) collective-permute-start(f32[5,4,512]{2,1,0:T(4,128)} %pad_maximum_fusion.3), channel_id=1, source_target_pairs={{1,0},{3,2},{5,4},{7,6},{9,8},{11,10},{13,12},{15,14},{17,16},{19,... | collective-permute-start | bytes 122888 | tf_op jit(solution)/shard_map/ppermute | solution.py:548
  17.7 20.7 %collective-permute-start.1 = (f32[4,48,1,512]{3,2,0,1:T(1,128)S(1)}, f32[4,48,1,512]{3,2,0,1:T(1,128)S(1)}, u32[]{:S(2)}, u32[]{:S(2)}) collective-permute-start(f32[4,48,1,512]{3,2,0,1:T(1,128)S(1)} %get-tuple-element.53), channel_id=1, source_target_pairs={{2,0},{4,2},{6,4},{8,6},{10,8},{12,10},{14,12},{16,14},{18,16},{20... | collective-permute-start | bytes 1179656 | tf_op jit(solution)/shard_map/ppermute | solution.py:544
  21.9 17.5 %collective-permute-start = (f32[4,48,1,512]{3,2,0,1:T(1,128)S(1)}, f32[4,48,1,512]{3,2,0,1:T(1,128)S(1)}, u32[]{:S(2)}, u32[]{:S(2)}) collective-permute-start(f32[4,48,1,512]{3,2,0,1:T(1,128)S(1)} %get-tuple-element.54), channel_id=1, source_target_pairs={{0,2},{2,4},{4,6},{6,8},{8,10},{10,12},{12,14},{14,16},{16,18},{18... | collective-permute-start | bytes 1179656 | tf_op jit(solution)/shard_map/ppermute | solution.py:543
  33.6 6.8 %copy-start.8 = (f32[5,4,512]{2,1,0:T(4,128)}, f32[5,4,512]{2,1,0:T(4,128)S(1)}, u32[]{:S(2)}) copy-start(f32[5,4,512]{2,1,0:T(4,128)S(1)} %collective-permute-done.2.low_ref) | copy-start | bytes 122884
  33.6 6.8 %copy-start.7 = (f32[5,4,512]{2,1,0:T(4,128)}, f32[5,4,512]{2,1,0:T(4,128)S(1)}, u32[]{:S(2)}) copy-start(f32[5,4,512]{2,1,0:T(4,128)S(1)} %collective-permute-done.3.high_ref) | copy-start | bytes 122884
  33.7 36.3 %collective-permute-start.8 = (f32[50,1,512]{2,1,0:T(1,128)S(1)}, f32[50,1,512]{2,1,0:T(1,128)S(1)}, u32[]{:S(2)}, u32[]{:S(2)}) collective-permute-start(f32[50,1,512]{2,1,0:T(1,128)S(1)} %pad_maximum_fusion), channel_id=1, source_target_pairs={{0,2},{2,4},{4,6},{6,8},{8,10},{10,12},{12,14},{14,16},{16,18},{18... | collective-permute-start | bytes 307208 | tf_op jit(solution)/shard_map/ppermute | solution.py:614
  33.9 38.8 %collective-permute-start.9 = (f32[50,1,512]{2,1,0:T(1,128)S(1)}, f32[50,1,512]{2,1,0:T(1,128)S(1)}, u32[]{:S(2)}, u32[]{:S(2)}) collective-permute-start(f32[50,1,512]{2,1,0:T(1,128)S(1)} %pad_maximum_fusion.1), channel_id=1, source_target_pairs={{2,0},{4,2},{6,4},{8,6},{10,8},{12,10},{14,12},{16,14},{18,16},{20... | collective-permute-start | bytes 307208 | tf_op jit(solution)/shard_map/ppermute | solution.py:617
  57.7 18.3 %collective-permute-start.4 = (f32[3,48,1,512]{3,2,1,0:T(1,128)}, f32[3,48,1,512]{3,2,1,0:T(1,128)S(1)}, u32[]{:S(2)}, u32[]{:S(2)}) collective-permute-start(f32[3,48,1,512]{3,2,1,0:T(1,128)} %get-tuple-element.31), channel_id=1, source_target_pairs={{0,2},{2,4},{4,6},{6,8},{8,10},{10,12},{12,14},{14,16},{16,18},{18... | collective-permute-start | bytes 884744 | tf_op jit(solution)/shard_map/ppermute | solution.py:610
  57.8 18.3 %collective-permute-start.5 = (f32[3,48,1,512]{3,2,1,0:T(1,128)}, f32[3,48,1,512]{3,2,1,0:T(1,128)S(1)}, u32[]{:S(2)}, u32[]{:S(2)}) collective-permute-start(f32[3,48,1,512]{3,2,1,0:T(1,128)} %get-tuple-element.32), channel_id=1, source_target_pairs={{2,0},{4,2},{6,4},{8,6},{10,8},{12,10},{14,12},{16,14},{18,16},{20... | collective-permute-start | bytes 884744 | tf_op jit(solution)/shard_map/ppermute | solution.py:611
  63.5 25.2 %all-to-all-start.1 = ((f32[32,3,192]{2,1,0:T(4,128)}), f32[32,3,192]{2,1,0:T(4,128)S(1)}, u32[]{:S(2)}, u32[]{:S(2)}) async-start(f32[32,3,192]{2,1,0:T(4,128)} %get-tuple-element.25), calls=%async_computation.1 | async-start | bytes 262144 | tf_op jit(solution)/shard_map/all_to_all | solution.py:608
  66.2 6.5 %collective-permute-start.6 = (f32[3,4,512]{2,1,0:T(4,128)}, f32[3,4,512]{2,1,0:T(4,128)S(1)}, u32[]{:S(2)}, u32[]{:S(2)}) collective-permute-start(f32[3,4,512]{2,1,0:T(4,128)} %get-tuple-element.33), channel_id=1, source_target_pairs={{0,1},{2,3},{4,5},{6,7},{8,9},{10,11},{12,13},{14,15},{16,17},{18,... | collective-permute-start | bytes 73736 | tf_op jit(solution)/shard_map/ppermute | solution.py:618
  70.1 6.0 %copy-start.5 = (f32[50,1,512]{2,1,0:T(1,128)}, f32[50,1,512]{2,1,0:T(1,128)S(1)}, u32[]{:S(2)}) copy-start(f32[50,1,512]{2,1,0:T(1,128)S(1)} %collective-permute-done.8.west2_ref) | copy-start | bytes 307204
  70.1 5.9 %collective-permute-start.7 = (f32[3,4,512]{2,1,0:T(4,128)}, f32[3,4,512]{2,1,0:T(4,128)S(1)}, u32[]{:S(2)}, u32[]{:S(2)}) collective-permute-start(f32[3,4,512]{2,1,0:T(4,128)} %get-tuple-element.34), channel_id=1, source_target_pairs={{1,0},{3,2},{5,4},{7,6},{9,8},{11,10},{13,12},{15,14},{17,16},{19,... | collective-permute-start | bytes 73736 | tf_op jit(solution)/shard_map/ppermute | solution.py:619
  72.7 3.4 %copy-start.6 = (f32[50,1,512]{2,1,0:T(1,128)}, f32[50,1,512]{2,1,0:T(1,128)S(1)}, u32[]{:S(2)}) copy-start(f32[50,1,512]{2,1,0:T(1,128)S(1)} %collective-permute-done.9.east2_ref) | copy-start | bytes 307204
  72.7 3.4 %copy-start.9 = (f32[3,4,512]{2,1,0:T(4,128)}, f32[3,4,512]{2,1,0:T(4,128)S(1)}, u32[]{:S(2)}) copy-start(f32[3,4,512]{2,1,0:T(4,128)S(1)} %collective-permute-done.6.low_ref) | copy-start | bytes 73732
  76.0 0.6 copy-start.10
  76.0 0.7 copy-start.3
  76.0 0.8 copy-start.4
  88.6 0.6 copy-start.2

commit v2 on v0

v2 whole, which is shorter than its diff:
```python
import functools
import math

import jax
import jax.numpy as jnp
from jax import lax
from jax.experimental import pallas as pl
from jax.experimental.pallas import tpu as pltpu
from jax.sharding import PartitionSpec as P

RELAX_RATE = 0.05
KERNEL_WIDTH = 0.1
KERNEL_WAVE = 40.0
PRIOR_WEIGHT = 0.1
COLS = 8
F32 = jnp.float32
BF16 = jnp.bfloat16
VMEM_LIMIT = 40 * 1024 * 1024


def reciprocal(x):
    r = pl.reciprocal(x, approx=True)
    return r * (2.0 - x * r)


def lat_next(x):
    return pltpu.roll(x, x.shape[1] - 1, 1)


def lat_prev(x):
    return pltpu.roll(x, 1, 1)


def lon_next(x):
    return pltpu.roll(x, 7, 0)


def lon_prev(x):
    return pltpu.roll(x, 1, 0)


def swap_halves(x):
    return pltpu.roll(x, 4, 0)


def pack(low, high):
    return jnp.concatenate([low, high], axis=0)


class Shape:
    def __init__(self, nr, width, rad_n):
        self.nr, self.width, self.half = nr, width, nr // 2
        sub = lax.broadcasted_iota(jnp.int32, (8, width), 0)
        lane = lax.broadcasted_iota(jnp.int32, (8, width), 1)
        self.lon = sub % 4
        self.lower = sub < 4
        self.upper = sub >= 4
        self.western = self.lon < 2
        self.not_last = lane < width - 1
        self.not_first = lane > 0
        self.rate = 4.0 / (nr * rad_n)
        at = lax.axis_index("rad")
        self.has_low = (at > 0).astype(F32)
        self.has_high = (at < rad_n - 1).astype(F32)
        layer = jnp.where(self.lower, 0, self.half) + (at * nr - (nr * rad_n - 1))
        self.first_weight = jnp.exp(layer.astype(F32) * self.rate)

    def step(self, i):
        return math.exp(self.rate * i)

    def sides(self, west, east):
        return jnp.where(
            self.lower,
            jnp.where(self.western, west[0], east[0]),
            jnp.where(self.western, west[1], east[1]),
        )


def face(a, b):
    return 2.0 * a * b * reciprocal(a + b)


def sin_pi(u):
    z = u * u
    p = 0.0772201269865036
    p = p * z - 0.5980451703071594
    p = p * z + 2.5500314235687256
    p = p * z - 5.1677069664001465
    p = p * z + 3.141592502593994
    return p * u


def site_kernel(d):
    turns = d * (KERNEL_WAVE / (2.0 * math.pi))
    s = sin_pi(turns - jnp.round(turns))
    return (reciprocal(1.0 + d * (1.0 / KERNEL_WIDTH)) + 0.5) - s * s


def message_kernel(
    steps_ref, v_ref, s_ref, ice_ref, cells_ref, obs_ref, wt_ref,
    west_ref, east_ref, west2_ref, east2_ref, low_ref, high_ref, packet_ref,
):
    nr, nl, width = v_ref.shape
    packet = jnp.concatenate(
        [
            cells_ref[...].astype(F32),
            obs_ref[...],
            wt_ref[...],
            jnp.zeros((1, obs_ref.shape[1]), F32),
        ],
        axis=0,
    )
    for n in range(packet_ref.shape[0]):
        packet_ref[n] = packet

    def field(n, r):
        return v_ref[r] if n == 0 else s_ref[n - 1, r]

    for r in range(nr):
        for n in range(4):
            x = field(n, r)
            west_ref[n * nr + r] = x[0:1, :]
            east_ref[n * nr + r] = x[nl - 1 : nl, :]
            west2_ref[n * nr + r] = x[1:2, :]
            east2_ref[n * nr + r] = x[nl - 2 : nl - 1, :]
    load = ice_ref[steps_ref[0]]
    west_ref[4 * nr] = load[0:1, :]
    east_ref[4 * nr] = load[nl - 1 : nl, :]
    for n in range(4):
        low_ref[n] = field(n, 0)
        low_ref[4 + n] = field(n, 1)
        high_ref[n] = field(n, nr - 1)
        high_ref[4 + n] = field(n, nr - 2)


def weights_kernel(gathered_ref, high_ref, low_ref, data_ref, rows_ref, *, total_lon):
    devices, _, own = gathered_ref.shape
    sites = high_ref.shape[1]
    width = high_ref.shape[2]
    for d in range(devices):
        data_ref[:, d * own : (d + 1) * own] = gathered_ref[d]
    cells = data_ref[0:1, :]
    lon = jnp.floor((cells + 0.5) * (1.0 / width))
    theta = (cells - lon * width + 0.5) * (1.0 / width)
    phi = lon * (1.0 / total_lon)

    def sin_whole(t):
        return sin_pi(jnp.minimum(t, 1.0 - t))

    def circle(t):
        u = t - jnp.round(t)
        s = sin_pi(u)
        y = jnp.abs(2.0 * u)
        wave = sin_pi(jnp.minimum(y, 1.0 - y))
        return 1.0 - 2.0 * s * s, jnp.where(u < 0, -wave, wave)

    site_cos, site_sin = circle(phi)
    first = lax.axis_index("lon") * 4 - 2 + total_lon
    col = (lax.broadcasted_iota(jnp.int32, (COLS, sites), 0) + first).astype(F32)
    turns = col * (1.0 / total_lon)
    col_cos, col_sin = circle(turns - jnp.floor(turns))
    rows_ref[0:8, :] = col_cos * site_cos + col_sin * site_sin
    rows_ref[8:9, :] = -2.0 * sin_pi(0.5 - theta)
    rows_ref[9:10, :] = -2.0 * sin_whole(theta)
    rows_ref[10:16, :] = jnp.zeros((6, sites), F32)
    columns = jnp.transpose(rows_ref[...])
    lat = (lax.broadcasted_iota(jnp.int32, (16, width), 1).astype(F32) + 0.5) * (1.0 / width)
    cos_lat = sin_pi(0.5 - lat)
    sin_lat = sin_whole(lat)
    for at in range(0, sites, 16):
        part = columns[at : at + 16, :]
        a = 2.0 + part[:, 8:9] * cos_lat
        b = part[:, 9:10] * sin_lat
        for n in range(COLS):
            k = site_kernel(a + b * part[:, n : n + 1])
            high = k.astype(BF16)
            high_ref[n, at : at + 16, :] = high
            low_ref[n, at : at + 16, :] = (k - high.astype(F32)).astype(BF16)


def two_parts(x):
    high = x.astype(BF16).astype(F32)
    return jnp.concatenate([high, x - high], axis=0).astype(BF16)


def product(x, high, low, contract):
    dims = (((1,), (contract,)), ((), ()))
    parts = two_parts(x)
    both = lax.dot_general(parts, high, dims, preferred_element_type=F32)
    rest = lax.dot_general(parts, low, dims, preferred_element_type=F32)
    return both[0:8, :] + (both[8:16, :] + rest[0:8, :])


class Rows:
    def __init__(self, half):
        self.fluid = 1
        self.field = [half + 3 + c * (half + 2) for c in range(3)]
        self.next = [4 * (half + 2) + c * half for c in range(3)]
        self.count = 4 * (half + 2) + 3 * half


def interior_kernel(v_ref, s_ref, out_ref, *, rad_n):
    nr, nl, width = v_ref.shape
    shape = Shape(nr, width, rad_n)
    half = shape.half
    at = Rows(half)
    for i in range(half):
        out_ref[at.fluid + i] = jnp.exp(-pack(v_ref[i], v_ref[i + half]))
        for c in range(3):
            out_ref[at.field[c] + i] = pack(s_ref[c, i], s_ref[c, i + half])

    def fluid(i):
        return out_ref[at.fluid + i]

    for base in [at.fluid] + at.field:
        out_ref[base - 1] = swap_halves(out_ref[base + half - 1])
        out_ref[base + half] = swap_halves(out_ref[base])
    seam = jnp.where(shape.upper, face(fluid(-1), fluid(0)), 0.0)
    carry = [seam * (out_ref[at.field[c]] - out_ref[at.field[c] - 1]) for c in range(3)]
    for i in range(half):
        f = fluid(i)
        h_east = jnp.where(shape.lon < 3, face(f, lon_next(f)), 0.0)
        h_north = jnp.where(shape.not_last, face(f, lat_next(f)), 0.0)
        h_up = face(f, fluid(i + 1))
        if i == half - 1:
            h_up = jnp.where(shape.lower, h_up, 0.0)
        for c in range(3):
            s = out_ref[at.field[c] + i]
            east = h_east * (lon_next(s) - s)
            north = h_north * (lat_next(s) - s)
            up = h_up * (out_ref[at.field[c] + i + 1] - s)
            total = (east - lon_prev(east)) + (north - lat_prev(north)) + (up - carry[c])
            out_ref[at.next[c] + i] = s + RELAX_RATE * total
            carry[c] = up


def forward_kernel(
    steps_ref, rows_ref, west_ref, east_ref, low_ref, high_ref, ice_ref, k_high_ref, k_low_ref,
    pred_ref, next_ref, surf_ref, *, rad_n,
):
    width = rows_ref.shape[2]
    nr = west_ref.shape[0] // 4
    shape = Shape(nr, width, rad_n)
    half = shape.half
    at = Rows(half)
    lower, lon = shape.lower, shape.lon
    ends = (lon == 0) | (lon == 3)

    def fluid(i):
        return rows_ref[at.fluid + i]

    ring = pack(shape.has_low * jnp.exp(-low_ref[0]), shape.has_high * jnp.exp(-high_ref[0]))
    h_ring = face(ring, jnp.where(lower, fluid(0), fluid(half - 1)))
    load = ice_ref[steps_ref[0]] * (1.0 - shape.has_high)
    load = pack(jnp.zeros_like(load), load)
    h_cuts = []
    for i in range(half):

        def side(n):
            return shape.sides(
                (west_ref[n * nr + i], west_ref[n * nr + i + half]),
                (east_ref[n * nr + i], east_ref[n * nr + i + half]),
            )

        h_cut = jnp.where(ends, face(fluid(i), jnp.exp(-side(0))), 0.0)
        h_cuts.append(h_cut)
        for c in range(3):
            s = rows_ref[at.field[c] + i]
            total = h_cut * (side(1 + c) - s)
            if i in (0, half - 1):
                beyond = h_ring * (pack(low_ref[1 + c], high_ref[1 + c]) - s)
                if i == 0:
                    total = total + jnp.where(lower, beyond, 0.0)
                if i == half - 1:
                    total = total + jnp.where(lower, 0.0, beyond)
            s1 = rows_ref[at.next[c] + i] + RELAX_RATE * total
            if c == 0 and i == half - 1:
                s1 = s1 - load
            next_ref[c, i] = s1

    zero = jnp.zeros((8, width), F32)
    column, east, north, cut = [zero] * 3, [zero] * 3, [zero] * 3, [zero] * 3
    below = [None] * 3
    for i in range(half):
        f = fluid(i)
        weight = shape.step(i)
        g_east = weight * face(f, lon_next(f))
        g_north = weight * face(f, lat_next(f))
        g_cut = weight * h_cuts[i]
        g_low = (RELAX_RATE * (weight - shape.step(i - 1))) * face(fluid(i - 1), f)
        if i == 0:
            g_low = jnp.where(lower, 0.0, g_low)
        for c in range(3):
            s = next_ref[c, i]
            if i == 0:
                below[c] = swap_halves(next_ref[c, half - 1])
            column[c] = column[c] + (weight * s - g_low * (s - below[c]))
            east[c] = east[c] + g_east * (lon_next(s) - s)
            north[c] = north[c] + g_north * (lat_next(s) - s)
            cut[c] = cut[c] + g_cut * s
            below[c] = s
    top = shape.step(half - 1)
    g_ring = (RELAX_RATE * h_ring) * jnp.where(
        lower, shape.step(-1) - 1.0, shape.step(half) - top
    )
    for c in range(3):
        inner = jnp.where(lower, next_ref[c, 0], next_ref[c, half - 1])

        def folded(x):
            x = shape.first_weight * x
            return x + swap_halves(x)

        sum_east = jnp.where(lon < 3, folded(east[c]), 0.0)
        sum_north = jnp.where(shape.not_last, folded(north[c]), 0.0)
        sum_cut = folded(cut[c])
        own = folded(column[c] + g_ring * inner)
        spread = (sum_east - lon_prev(sum_east)) + (sum_north - lat_prev(sum_north)) - sum_cut
        own = own + RELAX_RATE * spread
        if c == 0:
            second = ice_ref[steps_ref[1]] * (1.0 - shape.has_high)
            own = own - pack(second, second)
        surf_ref[0, c : c + 1, :] = RELAX_RATE * sum_cut[0:1, :]
        for col in range(4):
            surf_ref[col + 1, c : c + 1, :] = own[col : col + 1, :]
        surf_ref[5, c : c + 1, :] = RELAX_RATE * sum_cut[3:4, :]
    total = None
    for col in range(6):
        surf_ref[col, 3:8, :] = jnp.zeros((5, width), F32)
        term = product(surf_ref[col], k_high_ref[col + 1], k_low_ref[col + 1], 1)
        total = term if total is None else total + term
    for n in range(pred_ref.shape[0]):
        pred_ref[n] = total[0:3, :]


EAST, CUT, NORTH, UP = 0, 1, 2, 3
D0, Q, U, BASE, OWN, SIDE, BLOCK = 0, 12, 24, 30, 31, 36, 41
RING, LAST, D0_LOW, Q_LOW, ENDS = 0, 5, 10, 13, 16


def prepare_kernel(
    steps_ref, v_ref, m_ref, s_ref, ice_ref, west_ref, east_ref, west2_ref, east2_ref, low_ref,
    high_ref, corner_low_ref, corner_high_ref, blocks_ref, ends_ref,
    fluid_ref, field_ref, fluid_side_ref, field_side_ref, next_ref, next_side_ref, out_ref, sems,
    *, rad_n,
):
    nr, nl, width = v_ref.shape
    shape = Shape(nr, width, rad_n)
    half = shape.half
    lower, lon, western = shape.lower, shape.lon, shape.western

    def share(f, other):
        return other * reciprocal(f + other)

    def safe_share(f, other):
        return other * reciprocal(jnp.maximum(f + other, 1e-30))

    def north_of(f):
        return jnp.where(shape.not_last, lat_next(f), 0.0)

    def south_of(f):
        return jnp.where(shape.not_first, lat_prev(f), 0.0)

    def two(ref, n, i):
        return ref[n * nr + i], ref[n * nr + i + half]

    def corner(ref, n):
        return jnp.where(western, ref[n, 0], ref[n, 1])

    def weight(i):
        return shape.step(i) * shape.first_weight

    for i in range(half):
        fluid_ref[i + 1] = jnp.exp(-pack(v_ref[i], v_ref[i + half]))
        fluid_side_ref[i + 1] = jnp.exp(-shape.sides(two(west_ref, 0, i), two(east_ref, 0, i)))
        for c in range(3):
            field_ref[c, i + 1] = pack(s_ref[c, i], s_ref[c, i + half])
            field_side_ref[c, i + 1] = shape.sides(
                two(west_ref, 1 + c, i), two(east_ref, 1 + c, i)
            )
    ring = pack(shape.has_low * jnp.exp(-low_ref[0]), shape.has_high * jnp.exp(-high_ref[0]))
    ring_side = jnp.where(
        lower,
        shape.has_low * jnp.exp(-corner(corner_low_ref, 0)),
        shape.has_high * jnp.exp(-corner(corner_high_ref, 0)),
    )
    ring_field = [pack(low_ref[1 + c], high_ref[1 + c]) for c in range(3)]
    ring_field_side = [
        jnp.where(lower, corner(corner_low_ref, 1 + c), corner(corner_high_ref, 1 + c))
        for c in range(3)
    ]

    def close(ref, ring):
        ref[0] = jnp.where(lower, ring, swap_halves(ref[half]))
        ref[half + 1] = jnp.where(lower, swap_halves(ref[1]), ring)

    close(fluid_ref, ring)
    close(fluid_side_ref, ring_side)
    for c in range(3):
        close(field_ref.at[c], ring_field[c])
        close(field_side_ref.at[c], ring_field_side[c])

    def coefficients(ref, first, f, shares, here, above, below):
        scaled = (2.0 * RELAX_RATE) * f
        weighted = scaled * here
        for n in range(4):
            ref[first + n] = weighted * shares[n]
        ref[first + 4] = scaled * (shares[4] * (above - here) + shares[5] * (below - here))

    def relaxed(f, shares, s, others):
        total = shares[0] * (others[0] - s)
        for n in range(1, 6):
            total = total + shares[n] * (others[n] - s)
        return s + (2.0 * RELAX_RATE) * (f * total)

    outer = pack(shape.has_low * jnp.exp(-low_ref[4]), shape.has_high * jnp.exp(-high_ref[4]))
    inner = jnp.where(lower, fluid_ref[1], fluid_ref[half])
    ring_shares = [
        safe_share(ring, jnp.where(lon == 3, ring_side, lon_next(ring))),
        safe_share(ring, jnp.where(lon == 0, ring_side, lon_prev(ring))),
        safe_share(ring, north_of(ring)),
        safe_share(ring, south_of(ring)),
        safe_share(ring, outer),
        safe_share(ring, inner),
    ]
    coefficients(
        ends_ref,
        RING,
        ring,
        ring_shares,
        jnp.where(lower, weight(-1), weight(half)),
        jnp.where(lower, weight(-2), weight(half + 1)),
        jnp.where(lower, weight(0), weight(half - 1)),
    )
    ring_next = []
    for c in range(3):
        s, s_side = ring_field[c], ring_field_side[c]
        others = [
            jnp.where(lon == 3, s_side, lon_next(s)),
            jnp.where(lon == 0, s_side, lon_prev(s)),
            lat_next(s),
            lat_prev(s),
            pack(low_ref[5 + c], high_ref[5 + c]),
            jnp.where(lower, field_ref[c, 1], field_ref[c, half]),
        ]
        ring_next.append(relaxed(ring, ring_shares, s, others))
    load = ice_ref[steps_ref[0]]
    load = (1.0 - shape.has_high) * pack(jnp.zeros_like(load), load)
    load_side = jnp.where(western, west_ref[4 * nr], east_ref[4 * nr])
    load_side = (1.0 - shape.has_high) * jnp.where(lower, 0.0, load_side)

    def first_pass(i):
        f, f_side = fluid_ref[i + 1], fluid_side_ref[i + 1]
        here, above, below = weight(i), weight(i + 1), weight(i - 1)
        shares = [
            share(f, jnp.where(lon == 3, f_side, lon_next(f))),
            share(f, jnp.where(lon == 0, f_side, lon_prev(f))),
            share(f, north_of(f)),
            share(f, south_of(f)),
            share(f, fluid_ref[i + 2]),
            share(f, fluid_ref[i]),
        ]
        coefficients(out_ref.at[i], OWN, f, shares, here, above, below)
        scaled = (-0.5 * 2.0 * RELAX_RATE) * f
        for n in range(6):
            out_ref[i, U + n] = scaled * (shares[n] * shares[n])
        out_ref[i, BASE] = pack(
            m_ref[i] - (0.5 * PRIOR_WEIGHT) * v_ref[i],
            m_ref[i + half] - (0.5 * PRIOR_WEIGHT) * v_ref[i + half],
        )
        f_far = jnp.exp(-shape.sides(two(west2_ref, 0, i), two(east2_ref, 0, i)))
        side_shares = [
            share(f_side, jnp.where(western, f, f_far)),
            share(f_side, jnp.where(western, f_far, f)),
            share(f_side, north_of(f_side)),
            share(f_side, south_of(f_side)),
            share(f_side, fluid_side_ref[i + 2]),
            share(f_side, fluid_side_ref[i]),
        ]
        coefficients(out_ref.at[i], SIDE, f_side, side_shares, here, above, below)
        for c in range(3):
            s, s_side = field_ref[c, i + 1], field_side_ref[c, i + 1]
            s_far = shape.sides(two(west2_ref, 1 + c, i), two(east2_ref, 1 + c, i))
            others = [
                jnp.where(lon == 3, s_side, lon_next(s)),
                jnp.where(lon == 0, s_side, lon_prev(s)),
                lat_next(s),
                lat_prev(s),
                field_ref[c, i + 2],
                field_ref[c, i],
            ]
            out_ref[i, D0 + 3 * EAST + c] = others[0] - s
            out_ref[i, D0 + 3 * CUT + c] = s_side - s
            out_ref[i, D0 + 3 * NORTH + c] = others[2] - s
            out_ref[i, D0 + 3 * UP + c] = others[4] - s
            s1 = relaxed(f, shares, s, others)
            others = [
                jnp.where(western, s, s_far),
                jnp.where(western, s_far, s),
                lat_next(s_side),
                lat_prev(s_side),
                field_side_ref[c, i + 2],
                field_side_ref[c, i],
            ]
            s1_side = relaxed(f_side, side_shares, s_side, others)
            if c == 0 and i == half - 1:
                s1 = s1 - load
                s1_side = s1_side - load_side
            next_ref[c, i] = s1
            next_side_ref[c, i] = s1_side

    def second_pass(i):
        here = weight(i)
        step = weight(i + 1) - here
        for c in range(3):
            s, s_side = next_ref[c, i], next_side_ref[c, i]
            if i < half - 1:
                s_up = next_ref[c, i + 1]
            else:
                s_up = jnp.where(lower, swap_halves(next_ref[c, 0]), ring_next[c])
            ones = [jnp.where(lon == 3, s_side, lon_next(s)), s_side, lat_next(s)]
            for n, other in enumerate(ones):
                out_ref[i, Q + 3 * n + c] = here * (out_ref[i, D0 + 3 * n + c] + (other - s))
            out_ref[i, Q + 3 * UP + c] = step * (out_ref[i, D0 + 3 * UP + c] + (s_up - s))
        copies.append(
            pltpu.make_async_copy(out_ref.at[i], blocks_ref.at[i], sems.at[i])
        )
        copies[-1].start()

    copies = []
    for i in range(half):
        first_pass(i)
        if i > 0:
            second_pass(i - 1)
    second_pass(half - 1)
    for n in range(5):
        ends_ref[LAST + n] = out_ref[half - 1, OWN + n]
    step = weight(0) - weight(-1)
    for c in range(3):
        up = field_ref[c, 1] - field_ref[c, 0]
        low_state = jnp.where(lower, ring_next[c], swap_halves(next_ref[c, half - 1]))
        ends_ref[D0_LOW + c] = up
        ends_ref[Q_LOW + c] = step * (up + (next_ref[c, 0] - low_state))
    for copy in copies:
        copy.wait()


def gradient_kernel(
    v_ref, pred_ref, data_ref, k_high_ref, k_low_ref, ends_ref, blocks_ref,
    new_ref, half_ref, misfit_ref, sa_ref, d_ref, in_ref, sems, *, scale,
):
    nr, nl, width = v_ref.shape
    half = nr // 2
    sites = k_high_ref.shape[1]
    sub = lax.broadcasted_iota(jnp.int32, (8, width), 0)
    lon = sub % 4
    lower = sub < 4
    copies = [
        pltpu.make_async_copy(blocks_ref.at[i], in_ref.at[i], sems.at[i]) for i in range(half)
    ]
    for copy in copies:
        copy.start()

    predicted = pred_ref[0]
    for n in range(1, pred_ref.shape[0]):
        predicted = predicted + pred_ref[n]
    weight = data_ref[4:7, :]
    weighted = weight * (predicted * scale - data_ref[1:4, :])
    squares = jnp.sum(weighted * weighted, axis=1, keepdims=True)
    misfit_ref[...] = jnp.sum(squares, axis=0, keepdims=True) * (1.0 / (3 * sites))
    pulled = (weight * weighted) * scale
    pulled = jnp.concatenate([pulled, jnp.zeros((5, sites), F32)], axis=0)
    for col in range(COLS):
        spread = product(pulled, k_high_ref[col], k_low_ref[col], 0)
        for c in range(3):
            sa_ref[c, col : col + 1, :] = spread[c : c + 1, :]

    for c in range(3):
        x = sa_ref[c]

        def window(start):
            return jnp.where(
                lower,
                x if start == 0 else pltpu.roll(x, 8 - start, 0),
                x if start == 4 else pltpu.roll(x, (4 - start) % 8, 0),
            )

        own = window(2)
        east = window(3)
        west = window(1)
        outside = jnp.where(lon < 2, west, east)
        d_ref[0, c] = east - own
        d_ref[1, c] = west - own
        d_ref[2, c] = lat_next(own) - own
        d_ref[3, c] = lat_prev(own) - own
        d_ref[4, c] = own
        d_ref[5, c] = jnp.where(lon < 2, own, window(4)) - outside
        d_ref[6, c] = jnp.where(lon < 2, window(0), own) - outside
        d_ref[7, c] = lat_next(outside) - outside
        d_ref[8, c] = lat_prev(outside) - outside
        d_ref[9, c] = outside

    def change(ref, at, first):
        coeffs = [ref[at + n] for n in range(5)]
        out = []
        for c in range(3):
            total = coeffs[0] * d_ref[first, c]
            for n in range(1, 5):
                total = total + coeffs[n] * d_ref[first + n, c]
            out.append(total)
        return out

    def up_product(ref, d0, q, e_a, e_b):
        total = None
        for c in range(3):
            term = ref[q + c] * d_ref[4, c] + ref[d0 + c] * (e_b[c] - e_a[c])
            total = term if total is None else total + term
        return total

    ring = change(ends_ref, RING, 0)
    e_last = change(ends_ref, LAST, 0)
    copies[0].wait()
    e_first = e = change(in_ref.at[0], OWN, 0)
    e_low = [jnp.where(lower, ring[c], swap_halves(e_last[c])) for c in range(3)]
    p_down = up_product(ends_ref, D0_LOW, Q_LOW, e_low, e)
    for i in range(half):
        block = in_ref.at[i]
        if i < half - 1:
            copies[i + 1].wait()
            e_up = change(in_ref.at[i + 1], OWN, 0)
        else:
            e_up = [jnp.where(lower, swap_halves(e_first[c]), ring[c]) for c in range(3)]
        outside = change(block, SIDE, 5)
        p_up = up_product(block, D0 + 3 * UP, Q + 3 * UP, e, e_up)
        sums = [None, None, None]
        for c in range(3):
            others = [
                jnp.where(lon == 3, outside[c], lon_next(e[c])), outside[c], lat_next(e[c])
            ]
            slopes = [d_ref[0, c], d_ref[1, c], d_ref[2, c]]
            for n in range(3):
                term = block[Q + 3 * n + c] * slopes[n]
                term = term + block[D0 + 3 * n + c] * (others[n] - e[c])
                sums[n] = term if sums[n] is None else sums[n] + term
        p_east, p_cut, p_north = sums
        p_west = jnp.where(lon == 0, p_cut, lon_prev(p_east))
        total = block[BASE] + block[U] * p_east + block[U + 1] * p_west
        total = total + block[U + 2] * p_north + block[U + 3] * lat_prev(p_north)
        total = total + block[U + 4] * p_up + block[U + 5] * p_down
        half_ref[i] = total[0:4, :]
        half_ref[i + half] = total[4:8, :]
        new_ref[i] = v_ref[i] + total[0:4, :]
        new_ref[i + half] = v_ref[i + half] + total[4:8, :]
        e, p_down = e_up, p_up


def call(
    kernel, outs, ins, scratch=(), flops=1, name=None, held_in=(), held_out=(), far_out=()
):
    spaces = {"s": pltpu.SMEM, "v": pltpu.VMEM, "a": pl.ANY}
    made = pl.pallas_call(
        kernel,
        out_shape=[
            pltpu.VMEM(shape, dtype) if n in held_out else jax.ShapeDtypeStruct(shape, dtype)
            for n, (shape, dtype) in enumerate(outs)
        ],
        in_specs=[pl.BlockSpec(memory_space=spaces[k]) for k in ins],
        out_specs=[
            pl.BlockSpec(memory_space=pl.ANY if n in far_out else pltpu.VMEM)
            for n in range(len(outs))
        ],
        scratch_shapes=list(scratch),
        compiler_params=pltpu.CompilerParams(vmem_limit_bytes=VMEM_LIMIT),
        cost_estimate=pl.CostEstimate(flops=flops, bytes_accessed=1 << 20, transcendentals=0),
        name=name,
    )

    def run(*args):
        return made(
            *[
                pltpu.with_memory_space_constraint(a, pltpu.VMEM if n in held_in else pltpu.HBM)
                if ins[n] != "s"
                else a
                for n, a in enumerate(args)
            ]
        )

    return run


def body(
    logvisc, momentum, displacement, ice_history, load_steps, site_cells, observed, site_weight
):
    nr, nl, nlat = logvisc.shape
    own_sites = site_cells.shape[0]
    lon_n = lax.axis_size("lon")
    rad_n = lax.axis_size("rad")
    total_lon = nl * lon_n
    sites = own_sites * lon_n
    devices = lon_n * rad_n
    half = nr // 2
    scale = 1.0 / math.sqrt(total_lon * nlat)
    rad_at = lax.axis_index("rad")
    row = (8, nlat)

    column, first_column, layers = (4 * nr, 1, nlat), (4 * nr + 1, 1, nlat), (8, nl, nlat)
    to_west, to_east, to_west2, to_east2, to_low, to_high, packets = call(
        message_kernel,
        [
            (shape, F32)
            for shape in [first_column] * 2 + [column] * 2 + [layers] * 2 + [(lon_n, 8, own_sites)]
        ],
        "svvvvvv",
        name="messages",
    )(
        load_steps, logvisc, displacement, ice_history, site_cells[None], observed, site_weight
    )
    gathered = lax.all_to_all(packets, "lon", 0, 0)

    eastward = [(i, (i + 1) % lon_n) for i in range(lon_n)]
    westward = [(t, s) for s, t in eastward]
    upward = [(i, i + 1) for i in range(rad_n - 1)]
    downward = [(t, s) for s, t in upward]

    def across_rad(down, up):
        if rad_n == 2:
            both = lax.ppermute(jnp.where(rad_at == 0, up, down), "rad", [(0, 1), (1, 0)])
            return both, both
        return lax.ppermute(up, "rad", upward), lax.ppermute(down, "rad", downward)

    west = lax.ppermute(to_east, "lon", eastward)
    east = lax.ppermute(to_west, "lon", westward)
    low, high = across_rad(to_low, to_high)

    (rows,) = call(
        functools.partial(interior_kernel, rad_n=rad_n),
        [((Rows(half).count,) + row, F32)],
        "vv",
        flops=20000000,
        name="interior",
        held_out=(0,),
    )(logvisc, displacement)

    k_high, k_low, data = call(
        functools.partial(weights_kernel, total_lon=total_lon),
        [((COLS, sites, nlat), BF16)] * 2 + [((8, sites), F32)],
        "v",
        scratch=[pltpu.VMEM((16, sites), F32)],
        flops=20000000,
        name="site_weights",
        held_out=(0, 1, 2),
    )(gathered)

    (partial,) = call(
        functools.partial(forward_kernel, rad_n=rad_n),
        [((devices, 3, sites), F32)],
        "svvvvvvvv",
        scratch=[pltpu.VMEM((3, half) + row, F32), pltpu.VMEM((6,) + row, F32)],
        flops=20000000,
        name="forward",
        held_in=(1, 7, 8),
    )(load_steps, rows, west, east, low, high, ice_history, k_high, k_low)
    predicted = lax.all_to_all(partial, ("lon", "rad"), 0, 0)

    west2 = lax.ppermute(to_east2, "lon", eastward)
    east2 = lax.ppermute(to_west2, "lon", westward)
    ends = [
        jnp.stack([x[: 4 * nr].reshape(4, nr, 1, nlat)[:, r] for x in (west, east)], axis=1)
        for r in (0, nr - 1)
    ]
    corner_low, corner_high = across_rad(*ends)

    blocks, ends = call(
        functools.partial(prepare_kernel, rad_n=rad_n),
        [((half, BLOCK) + row, F32), ((ENDS,) + row, F32)],
        "s" + "v" * 12,
        scratch=[
            pltpu.VMEM((half + 2,) + row, F32),
            pltpu.VMEM((3, half + 2) + row, F32),
            pltpu.VMEM((half + 2,) + row, F32),
            pltpu.VMEM((3, half + 2) + row, F32),
            pltpu.VMEM((3, half) + row, F32),
            pltpu.VMEM((3, half) + row, F32),
            pltpu.VMEM((half, BLOCK) + row, F32),
            pltpu.SemaphoreType.DMA((half,)),
        ],
        flops=40000000,
        name="prepare",
        far_out=(0,),
    )(
        load_steps, logvisc, momentum, displacement, ice_history, west, east, west2, east2, low,
        high, corner_low, corner_high,
    )

    new_logvisc, half_momentum, misfit = call(
        functools.partial(gradient_kernel, scale=scale),
        [((nr, nl, nlat), F32), ((nr, nl, nlat), F32), ((1, 1), F32)],
        "vvvvvva",
        scratch=[
            pltpu.VMEM((3,) + row, F32),
            pltpu.VMEM((10, 3) + row, F32),
            pltpu.VMEM((half, BLOCK) + row, F32),
            pltpu.SemaphoreType.DMA((half,)),
        ],
        flops=20000000,
        name="gradient",
        held_in=(2, 3, 4),
    )(logvisc, predicted, data, k_high, k_low, ends, blocks)
    return (new_logvisc, half_momentum, misfit.reshape(1))


def solution(mesh):
    return jax.shard_map(
        body,
        mesh=mesh,
        in_specs=(
            P("rad", "lon", None),
            P("rad", "lon", None),
            P(None, "rad", "lon", None),
            P(None, "lon", None),
            P(),
            P("lon"),
            P(None, "lon"),
            P(None, "lon"),
        ),
        out_specs=(P("rad", "lon", None), P("rad", "lon", None), P()),
        check_vma=False,
    )
```

time: 237 us -> 69.6 us (0.29)
  blocking collectives: 116 us -> 0 us
  Pallas kernels: 0 us -> 33.3 us
  other arithmetic: 25.5 us -> 0.04 us
  starting transfers between devices: 46.9 us -> 21.5 us
  waiting for transfers between devices: 18.3 us -> 4.6 us
  matrix products: 10.7 us -> 0 us
  between operations: 8.2 us -> 0.94 us
    psum x3 -> x0, blocking collectives: 47 us -> none  [the longest x1 32.7 us: body(): lax.psum(jnp.sum(weighted * weighted), 'lon')]
    all_gather x2 -> x0, blocking collectives: 37.2 us -> none  [the longest x1 19.7 us: body(): all_feats = lax.all_gather(own_feats, 'lon', axis=0, tiled=True)]
    ppermute x20 -> x6, starting transfers between devices: 46.9 us -> 13.5 us  [the longest x1 5.05 us: body(): east = lax.ppermute(to_west, 'lon', westward)]
    pallas_call x0 -> x6, Pallas kernels: none -> 33.3 us  [run(): made(*[pltpu.with_memory_space_constraint(a, pltpu.VMEM if n in held_in e...]
    unnamed x1 -> x0, blocking collectives: 31.8 us -> none
    ppermute x20 -> x6, waiting for transfers between devices: 18.3 us -> 2.15 us  [the longest x2 2.14 us: across_rad(): lax.ppermute(jnp.where(rad_at == 0, up, down), 'rad', [(0, 1), (1, 0)])]
    dot_general x4 -> x0, matrix products: 10.7 us -> none  [the longest x2 6.86 us: add_block(): jnp.einsum('sc,sm->cm', block[:, 3:], weights, precision=lax.Precision.HI...]
    reduce_sum x6 -> x0, other arithmetic: 10 us -> none  [the longest x4 7.54 us: fluid_gradient(): jnp.sum((state_side - state_mid) * (adjoint_side - adjoint_mid), axis=0,...]
  transfers between devices with their start and end apart: 20 -> 8, of which waited for: 7 -> 2; matrix products, arithmetic and copies ran while one was open for 4% -> 4% of each run, Pallas kernels for 0% -> 32%
where the time goes in v2:
time: 69.6 us; the launch traced here: 69.1 us
  Pallas kernels  33.3 us (48%)
  starting transfers between devices  21.5 us (31%)
  local copies, waits for them, and re-layouts  8.7 us (12%)
  waiting for transfers between devices  4.6 us (7%)
  between operations  0.94 us (1%)
    pallas_call x6, Pallas kernels, run(): made(*[pltpu.with_memory_space_constraint(a, pltpu.VMEM if n in held_in e...  33.3 us
    unnamed x22, local copies, waits for them, and re-layouts  6.16 us
    ppermute x1, starting transfers between devices, body(): east = lax.ppermute(to_west, 'lon', westward)  5.05 us
    all_to_all x1, starting transfers between devices, body(): predicted = lax.all_to_all(partial, ('lon', 'rad'), 0, 0)  4.49 us
    ppermute x1, starting transfers between devices, body(): east2 = lax.ppermute(to_west2, 'lon', westward)  4.44 us
    ppermute x2, starting transfers between devices, across_rad(): lax.ppermute(jnp.where(rad_at == 0, up, down), 'rad', [(0, 1), (1, 0)])  3.6 us
    all_to_all x1, starting transfers between devices, body(): gathered = lax.all_to_all(packets, 'lon', 0, 0)  3.49 us
    slice x3, local copies, waits for them, and re-layouts, body(): x[:4 * nr].reshape(4, nr, 1, nlat)[:, r]  2.54 us
  transfers between devices with their start and end apart: 8, of which 2 were waited for; matrix products, arithmetic and copies ran while one was open for 4% of the time, Pallas kernels for 32%

profile of v2, /device:TPU:0, one launch (start us, length us, event | category | flops | bytes accessed | tf_op | source)
XLA Modules:
  0.0 69.1 jit_solution(11569319967173312195)
XLA Ops:
  0.6 0.0 copy-start.5
  0.6 0.6 copy-done.5
  1.3 2.7 %messages.1 = (f32[193,1,512]{2,1,0:T(1,128)S(1)}, f32[193,1,512]{2,1,0:T(1,128)}, f32[192,1,512]{2,1,0:T(1,128)}, f32[192,1,512]{2,1,0:T(1,128)}, f32[8,4,512]{...) custom-call(s32[2]{0:T(128)S(1)} %copy-done.5, f32[48,4,512]{2,1,0:T(4,128)} %v_ref.7, ...), custom_call_target="tpu_custom_call" | custom-call | flops 1 | bytes 1048576 | tf_op jit(solution)/shard_map/messages/pallas_call | solution.py:678
  3.9 0.5 collective-permute-start
  4.4 5.0 %collective-permute-start.1 = (f32[193,1,512]{2,1,0:T(1,128)S(1)}, f32[193,1,512]{2,1,0:T(1,128)}, u32[]{:S(2)}, u32[]{:S(2)}) collective-permute-start(f32[193,1,512]{2,1,0:T(1,128)S(1)} %get-tuple-element.19), channel_id=1, source_target_pairs={{2,0},{4,2},{6,4},{8,6},{10,8},{12,10},{14,12},{16,14},{18,16},{20... | collective-permute-start | bytes 1185800 | tf_op jit(solution)/shard_map/ppermute | solution.py:731
  9.5 1.9 %collective-permute-start.2 = (f32[8,4,512]{2,1,0:T(4,128)S(1)}, f32[8,4,512]{2,1,0:T(4,128)S(1)}, u32[]{:S(2)}, u32[]{:S(2)}) collective-permute-start(f32[8,4,512]{2,1,0:T(4,128)S(1)} %bitcast.11), channel_id=1, source_target_pairs={{0,1},{1,0},{2,3},{3,2},{4,5},{5,4},{6,7},{7,6},{8,9},{9,8},{10,11... | collective-permute-start | bytes 196616 | tf_op jit(solution)/shard_map/ppermute | solution.py:726
  11.4 0.0 collective-permute-start.3
  11.4 4.4 %collective-permute-start.4 = (f32[192,1,512]{2,1,0:T(1,128)}, f32[192,1,512]{2,1,0:T(1,128)}, u32[]{:S(2)}, u32[]{:S(2)}) collective-permute-start(f32[192,1,512]{2,1,0:T(1,128)} %get-tuple-element.27), channel_id=1, source_target_pairs={{2,0},{4,2},{6,4},{8,6},{10,8},{12,10},{14,12},{16,14},{18,16},{20... | collective-permute-start | bytes 1179656 | tf_op jit(solution)/shard_map/ppermute | solution.py:765
  15.9 3.5 %all-to-all-start = ((f32[16,8,12]{2,1,0:T(8,128)}), f32[16,8,12]{2,1,0:T(8,128)S(1)}, u32[]{:S(2)}, u32[]{:S(2)}) async-start(f32[16,8,12]{2,1,0:T(8,128)} %get-tuple-element.22), calls=%async_computation | async-start | bytes 131072 | tf_op jit(solution)/shard_map/all_to_all | solution.py:717
  19.3 0.0 copy-start.6
  19.4 5.9 %interior.1.rows_ref = f32[176,8,512]{2,1,0:T(8,128)S(1)} custom-call(f32[48,4,512]{2,1,0:T(4,128)} %v_ref.7, f32[3,48,4,512]{3,2,1,0:T(4,128)} %s_ref.5), custom_call_target="tpu_custom_call" | custom-call | flops 20000000 | bytes 1048576 | tf_op jit(solution)/shard_map/interior/pallas_call | solution.py:678
  25.3 2.5 %all-to-all-done.gathered_ref = f32[16,8,12]{2,1,0:T(8,128)S(1)} async-done(((f32[16,8,12]{2,1,0:T(8,128)}), f32[16,8,12]{2,1,0:T(8,128)S(1)}, u32[]{:S(2)}, u32[]{:S(2)}) %all-to-all-start) | async-done | bytes 6176 | tf_op jit(solution)/shard_map/all_to_all | solution.py:717
  27.8 0.6 copy-done.10
  28.4 4.1 %site_weights.1 = (bf16[8,192,512]{2,1,0:T(8,128)(2,1)S(1)}, bf16[8,192,512]{2,1,0:T(8,128)(2,1)S(1)}, f32[8,192]{1,0:T(8,128)S(1)}) custom-call(f32[16,8,12]{2,1,0:T(8,128)} %copy-done.10), custom_call_target="tpu_custom_call" | custom-call | flops 20000000 | bytes 1048576 | tf_op jit(solution)/shard_map/site_weights/pallas_call | solution.py:678
  32.5 0.0 collective-permute-done.west_ref
  32.5 0.0 collective-permute-done.1.east_ref
  32.5 0.6 copy-done.7
  33.1 4.0 %forward.1 = f32[32,3,192]{2,1,0:T(4,128)} custom-call(s32[2]{0:T(128)S(1)} %copy-done.6, f32[176,8,512]{2,1,0:T(8,128)S(1)} %interior.1.rows_ref, f32[193,1,512]{2,1,0:T(1,128)} %collective-permute-done.west_ref, f32[193,1,512]{2,1,0:T(1,128)} %collective-permute-done.1.east_ref, f32[8,4,512]{2,1,0:T(4,128)} %copy-done.7, f32[8,4,512]{2,1,0:T(4,128)} %copy-done.7, ...), custom_call_target="tpu_custom_call" | custom-call | flops 20000000 | bytes 1048576 | tf_op jit(solution)/shard_map/forward/pallas_call | solution.py:678
  37.1 1.1 %copy-done = bf16[8,192,512]{2,1,0:T(8,128)(2,1)} copy-done((bf16[8,192,512]{2,1,0:T(8,128)(2,1)}, bf16[8,192,512]{2,1,0:T(8,128)(2,1)S(1)}, u32[]{:S(2)}) %copy-start) | copy-done | bytes 1572888
  38.3 1.2 %copy-done.2 = bf16[8,192,512]{2,1,0:T(8,128)(2,1)} copy-done((bf16[8,192,512]{2,1,0:T(8,128)(2,1)}, bf16[8,192,512]{2,1,0:T(8,128)(2,1)S(1)}, u32[]{:S(2)}) %copy-start.2) | copy-done | bytes 1572888
  39.4 4.5 %all-to-all-start.1 = ((f32[32,3,192]{2,1,0:T(4,128)}), f32[32,3,192]{2,1,0:T(4,128)S(1)}, u32[]{:S(2)}, u32[]{:S(2)}) async-start(f32[32,3,192]{2,1,0:T(4,128)} %forward.1), calls=%async_computation.1 | async-start | bytes 262144 | tf_op jit(solution)/shard_map/all_to_all | solution.py:762
  43.9 1.3 %slice.26 = f32[192,1,512]{2,1,0:T(1,128)S(1)} slice(f32[193,1,512]{2,1,0:T(1,128)} %collective-permute-done.west_ref), slice={[0:192], [0:1], [0:512]} | slice | bytes 786432 | tf_op jit(solution)/shard_map/slice | solution.py:767
  45.2 1.3 %slice.28 = f32[192,1,512]{2,1,0:T(1,128)S(1)} slice(f32[193,1,512]{2,1,0:T(1,128)} %collective-permute-done.1.east_ref), slice={[0:192], [0:1], [0:512]} | slice | bytes 786432 | tf_op jit(solution)/shard_map/slice | solution.py:767
  46.5 1.7 %collective-permute-start.5 = (f32[4,2,1,512]{3,2,1,0:T(1,128)S(1)}, f32[4,2,1,512]{3,2,1,0:T(1,128)S(1)}, u32[]{:S(2)}, u32[]{:S(2)}) collective-permute-start(f32[4,2,1,512]{3,2,1,0:T(1,128)S(1)} %broadcast_select_fusion), channel_id=1, source_target_pairs={{0,1},{1,0},{2,3},{3,2},{4,5},{5,4},{6,7},{7,6},{8,9},{9,8},{10,11... | collective-permute-start | bytes 49160 | tf_op jit(solution)/shard_map/ppermute | solution.py:726
  48.2 0.0 collective-permute-done.3.west2_ref
  48.2 0.0 collective-permute-done.4.east2_ref
  48.2 2.1 %collective-permute-done.5.corner_low_ref.corner_high_ref = f32[4,2,1,512]{3,2,1,0:T(1,128)S(1)} collective-permute-done((f32[4,2,1,512]{3,2,1,0:T(1,128)S(1)}, f32[4,2,1,512]{3,2,1,0:T(1,128)S(1)}, u32[]{:S(2)}, u32[]{:S(2)}) %collective-permute-start.5) | collective-permute-done | bytes 16416 | tf_op jit(solution)/shard_map/ppermute | solution.py:726
  50.4 0.6 copy-done.9
  51.0 8.4 %prepare.1 = (f32[24,41,8,512]{3,2,1,0:T(8,128)}, f32[16,8,512]{2,1,0:T(8,128)S(1)}) custom-call(s32[2]{0:T(128)S(1)} %copy-done.6, f32[48,4,512]{2,1,0:T(4,128)} %v_ref.7, f32[48,4,512]{2,1,0:T(4,128)} %m_ref.1, f32[3,48,4,512]{3,2,1,0:T(4,128)} %s_ref.5, f32[8,4,512]{2,1,0:T(4,128)} %ice_ref.5, f32[193,1,512]{2,1,0:T(1,128)} %collective-permute-done.west_ref, ...), custom_call_target="tpu_custom_call" | custom-call | flops 40000000 | bytes 1048576 | tf_op jit(solution)/shard_map/prepare/pallas_call | solution.py:678
  59.4 0.7 %copy-done.4 = f32[16,8,512]{2,1,0:T(8,128)} copy-done((f32[16,8,512]{2,1,0:T(8,128)}, f32[16,8,512]{2,1,0:T(8,128)S(1)}, u32[]{:S(2)}) %copy-start.4) | copy-done | bytes 262168
  60.1 0.6 copy-done.8
  60.7 8.2 %gradient.1 = (f32[48,4,512]{2,1,0:T(4,128)}, f32[48,4,512]{2,1,0:T(4,128)}, f32[1,1]{1,0:T(1,128)}) custom-call(f32[48,4,512]{2,1,0:T(4,128)} %v_ref.7, f32[32,3,192]{2,1,0:T(4,128)} %copy-done.8, f32[8,192]{1,0:T(8,128)S(1)} %get-tuple-element.25.data_ref, bf16[8,192,512]{2,1,0:T(8,128)(2,1)S(1)} %copy-done.1, bf16[8,192,512]{2,1,0:T(8,128)(2,1)S(1)} %copy-done.3, ...), custom_call_target="tpu_custom_call" | custom-call | flops 20000000 | bytes 1048576 | tf_op jit(solution)/shard_map/gradient/pallas_call | solution.py:678
  (17 shorter events, 0.1 us)
Async XLA Ops:
  0.6 0.7 copy-start.5
  3.9 28.5 %collective-permute-start = (f32[193,1,512]{2,1,0:T(1,128)}, f32[193,1,512]{2,1,0:T(1,128)}, u32[]{:S(2)}, u32[]{:S(2)}) collective-permute-start(f32[193,1,512]{2,1,0:T(1,128)} %get-tuple-element.18), channel_id=1, source_target_pairs={{0,2},{2,4},{4,6},{6,8},{8,10},{10,12},{12,14},{14,16},{16,18},{18... | collective-permute-start | bytes 1185800 | tf_op jit(solution)/shard_map/ppermute | solution.py:730
  4.4 28.1 %collective-permute-start.1 = (f32[193,1,512]{2,1,0:T(1,128)S(1)}, f32[193,1,512]{2,1,0:T(1,128)}, u32[]{:S(2)}, u32[]{:S(2)}) collective-permute-start(f32[193,1,512]{2,1,0:T(1,128)S(1)} %get-tuple-element.19), channel_id=1, source_target_pairs={{2,0},{4,2},{6,4},{8,6},{10,8},{12,10},{14,12},{16,14},{18,16},{20... | collective-permute-start | bytes 1185800 | tf_op jit(solution)/shard_map/ppermute | solution.py:731
  9.5 23.0 %collective-permute-start.2 = (f32[8,4,512]{2,1,0:T(4,128)S(1)}, f32[8,4,512]{2,1,0:T(4,128)S(1)}, u32[]{:S(2)}, u32[]{:S(2)}) collective-permute-start(f32[8,4,512]{2,1,0:T(4,128)S(1)} %bitcast.11), channel_id=1, source_target_pairs={{0,1},{1,0},{2,3},{3,2},{4,5},{5,4},{6,7},{7,6},{8,9},{9,8},{10,11... | collective-permute-start | bytes 196616 | tf_op jit(solution)/shard_map/ppermute | solution.py:726
  11.4 36.8 %collective-permute-start.3 = (f32[192,1,512]{2,1,0:T(1,128)}, f32[192,1,512]{2,1,0:T(1,128)}, u32[]{:S(2)}, u32[]{:S(2)}) collective-permute-start(f32[192,1,512]{2,1,0:T(1,128)} %get-tuple-element.26), channel_id=1, source_target_pairs={{0,2},{2,4},{4,6},{6,8},{8,10},{10,12},{12,14},{14,16},{16,18},{18... | collective-permute-start | bytes 1179656 | tf_op jit(solution)/shard_map/ppermute | solution.py:764
  11.4 36.8 %collective-permute-start.4 = (f32[192,1,512]{2,1,0:T(1,128)}, f32[192,1,512]{2,1,0:T(1,128)}, u32[]{:S(2)}, u32[]{:S(2)}) collective-permute-start(f32[192,1,512]{2,1,0:T(1,128)} %get-tuple-element.27), channel_id=1, source_target_pairs={{2,0},{4,2},{6,4},{8,6},{10,8},{12,10},{14,12},{16,14},{18,16},{20... | collective-permute-start | bytes 1179656 | tf_op jit(solution)/shard_map/ppermute | solution.py:765
  15.9 11.9 %all-to-all-start = ((f32[16,8,12]{2,1,0:T(8,128)}), f32[16,8,12]{2,1,0:T(8,128)S(1)}, u32[]{:S(2)}, u32[]{:S(2)}) async-start(f32[16,8,12]{2,1,0:T(8,128)} %get-tuple-element.22), calls=%async_computation | async-start | bytes 131072 | tf_op jit(solution)/shard_map/all_to_all | solution.py:717
  19.3 13.7 %copy-start.6 = (s32[2]{0:T(128)S(1)}, s32[2]{0:T(128)}, u32[]{:S(2)}) copy-start(s32[2]{0:T(128)} %steps_ref.5) | copy-start | bytes 28
  27.8 0.6 copy-start.10
  32.5 0.6 copy-start.7
  37.1 1.1 %copy-start = (bf16[8,192,512]{2,1,0:T(8,128)(2,1)}, bf16[8,192,512]{2,1,0:T(8,128)(2,1)S(1)}, u32[]{:S(2)}) copy-start(bf16[8,192,512]{2,1,0:T(8,128)(2,1)S(1)} %get-tuple-element.23.k_high_ref) | copy-start | bytes 4718596
  38.3 1.2 %copy-start.2 = (bf16[8,192,512]{2,1,0:T(8,128)(2,1)}, bf16[8,192,512]{2,1,0:T(8,128)(2,1)S(1)}, u32[]{:S(2)}) copy-start(bf16[8,192,512]{2,1,0:T(8,128)(2,1)S(1)} %get-tuple-element.24.k_low_ref) | copy-start | bytes 4718596
  39.4 20.7 %all-to-all-start.1 = ((f32[32,3,192]{2,1,0:T(4,128)}), f32[32,3,192]{2,1,0:T(4,128)S(1)}, u32[]{:S(2)}, u32[]{:S(2)}) async-start(f32[32,3,192]{2,1,0:T(4,128)} %forward.1), calls=%async_computation.1 | async-start | bytes 262144 | tf_op jit(solution)/shard_map/all_to_all | solution.py:762
  46.5 14.2 %copy-start.1 = (bf16[8,192,512]{2,1,0:T(8,128)(2,1)S(1)}, bf16[8,192,512]{2,1,0:T(8,128)(2,1)}, u32[]{:S(2)}) copy-start(bf16[8,192,512]{2,1,0:T(8,128)(2,1)} %copy-done) | copy-start | bytes 4718596
  46.5 14.2 %copy-start.3 = (bf16[8,192,512]{2,1,0:T(8,128)(2,1)S(1)}, bf16[8,192,512]{2,1,0:T(8,128)(2,1)}, u32[]{:S(2)}) copy-start(bf16[8,192,512]{2,1,0:T(8,128)(2,1)} %copy-done.2) | copy-start | bytes 4718596
  46.5 3.8 %collective-permute-start.5 = (f32[4,2,1,512]{3,2,1,0:T(1,128)S(1)}, f32[4,2,1,512]{3,2,1,0:T(1,128)S(1)}, u32[]{:S(2)}, u32[]{:S(2)}) collective-permute-start(f32[4,2,1,512]{3,2,1,0:T(1,128)S(1)} %broadcast_select_fusion), channel_id=1, source_target_pairs={{0,1},{1,0},{2,3},{3,2},{4,5},{5,4},{6,7},{7,6},{8,9},{9,8},{10,11... | collective-permute-start | bytes 49160 | tf_op jit(solution)/shard_map/ppermute | solution.py:726
  50.3 0.6 copy-start.9
  59.4 0.7 %copy-start.4 = (f32[16,8,512]{2,1,0:T(8,128)}, f32[16,8,512]{2,1,0:T(8,128)S(1)}, u32[]{:S(2)}) copy-start(f32[16,8,512]{2,1,0:T(8,128)S(1)} %get-tuple-element.28.ends_ref) | copy-start | bytes 786436
  60.1 0.6 copy-start.8

commit v3 on v2

v3 whole, which is shorter than its diff:
```python
import functools
import math

import jax
import jax.numpy as jnp
from jax import lax
from jax.experimental import pallas as pl
from jax.experimental.pallas import tpu as pltpu
from jax.sharding import PartitionSpec as P

RELAX_RATE = 0.05
KERNEL_WIDTH = 0.1
KERNEL_WAVE = 40.0
PRIOR_WEIGHT = 0.1
COLS = 8
F32 = jnp.float32
BF16 = jnp.bfloat16
VMEM_LIMIT = 40 * 1024 * 1024


def reciprocal(x):
    r = pl.reciprocal(x, approx=True)
    return r * (2.0 - x * r)


def lat_next(x):
    return pltpu.roll(x, x.shape[1] - 1, 1)


def lat_prev(x):
    return pltpu.roll(x, 1, 1)


def lon_next(x):
    return pltpu.roll(x, 7, 0)


def lon_prev(x):
    return pltpu.roll(x, 1, 0)


def swap_halves(x):
    return pltpu.roll(x, 4, 0)


def pack(low, high):
    return jnp.concatenate([low, high], axis=0)


class Shape:
    def __init__(self, nr, width, rad_n):
        self.nr, self.width, self.half = nr, width, nr // 2
        sub = lax.broadcasted_iota(jnp.int32, (8, width), 0)
        lane = lax.broadcasted_iota(jnp.int32, (8, width), 1)
        self.lon = sub % 4
        self.lower = sub < 4
        self.upper = sub >= 4
        self.western = self.lon < 2
        self.not_last = lane < width - 1
        self.not_first = lane > 0
        self.rate = 4.0 / (nr * rad_n)
        at = lax.axis_index("rad")
        self.has_low = (at > 0).astype(F32)
        self.has_high = (at < rad_n - 1).astype(F32)
        layer = jnp.where(self.lower, 0, self.half) + (at * nr - (nr * rad_n - 1))
        self.first_weight = jnp.exp(layer.astype(F32) * self.rate)

    def step(self, i):
        return math.exp(self.rate * i)

    def sides(self, west, east):
        return jnp.where(
            self.lower,
            jnp.where(self.western, west[0], east[0]),
            jnp.where(self.western, west[1], east[1]),
        )


def face(a, b):
    return 2.0 * a * b * reciprocal(a + b)


def sin_pi(u):
    z = u * u
    p = 0.0772201269865036
    p = p * z - 0.5980451703071594
    p = p * z + 2.5500314235687256
    p = p * z - 5.1677069664001465
    p = p * z + 3.141592502593994
    return p * u


def site_kernel(d):
    turns = d * (KERNEL_WAVE / (2.0 * math.pi))
    s = sin_pi(turns - jnp.round(turns))
    return (reciprocal(1.0 + d * (1.0 / KERNEL_WIDTH)) + 0.5) - s * s


def packet_kernel(cells_ref, obs_ref, wt_ref, packet_ref):
    packet = jnp.concatenate(
        [
            cells_ref[...].astype(F32),
            obs_ref[...],
            wt_ref[...],
            jnp.zeros((1, obs_ref.shape[1]), F32),
        ],
        axis=0,
    )
    for n in range(packet_ref.shape[0]):
        packet_ref[n] = packet


def message_kernel(
    v_ref, s_ref, ice_ref, west_ref, east_ref, west2_ref, east2_ref, low_ref, high_ref, *, rad_n
):
    nr, nl, width = v_ref.shape

    def field(n, r):
        return v_ref[r] if n == 0 else s_ref[n - 1, r]

    for r in range(nr):
        for n in range(4):
            x = field(n, r)
            west_ref[n * nr + r] = x[0:1, :]
            east_ref[n * nr + r] = x[nl - 1 : nl, :]
            west2_ref[n * nr + r] = x[1:2, :]
            east2_ref[n * nr + r] = x[nl - 2 : nl - 1, :]
    for n in range(ice_ref.shape[0]):
        west_ref[4 * nr + n] = ice_ref[n, 0:1, :]
        east_ref[4 * nr + n] = ice_ref[n, nl - 1 : nl, :]
    bottom = lax.axis_index("rad") == 0
    for n in range(4):
        for k in range(2):
            down, up = field(n, k), field(n, nr - 1 - k)
            if rad_n == 2:
                low_ref[n + 4 * k] = jnp.where(bottom, up, down)
            else:
                low_ref[n + 4 * k] = down
                high_ref[n + 4 * k] = up
    if rad_n == 2:
        high_ref[...] = jnp.zeros_like(high_ref)


def weights_kernel(gathered_ref, high_ref, low_ref, data_ref, rows_ref, *, total_lon):
    devices, _, own = gathered_ref.shape
    sites = high_ref.shape[1]
    width = high_ref.shape[2]
    for d in range(devices):
        data_ref[:, d * own : (d + 1) * own] = gathered_ref[d]
    cells = data_ref[0:1, :]
    lon = jnp.floor((cells + 0.5) * (1.0 / width))
    theta = (cells - lon * width + 0.5) * (1.0 / width)
    phi = lon * (1.0 / total_lon)

    def sin_whole(t):
        return sin_pi(jnp.minimum(t, 1.0 - t))

    def circle(t):
        u = t - jnp.round(t)
        s = sin_pi(u)
        y = jnp.abs(2.0 * u)
        wave = sin_pi(jnp.minimum(y, 1.0 - y))
        return 1.0 - 2.0 * s * s, jnp.where(u < 0, -wave, wave)

    site_cos, site_sin = circle(phi)
    first = lax.axis_index("lon") * 4 - 2 + total_lon
    col = (lax.broadcasted_iota(jnp.int32, (COLS, sites), 0) + first).astype(F32)
    turns = col * (1.0 / total_lon)
    col_cos, col_sin = circle(turns - jnp.floor(turns))
    rows_ref[0:8, :] = col_cos * site_cos + col_sin * site_sin
    rows_ref[8:9, :] = -2.0 * sin_pi(0.5 - theta)
    rows_ref[9:10, :] = -2.0 * sin_whole(theta)
    rows_ref[10:16, :] = jnp.zeros((6, sites), F32)
    columns = jnp.transpose(rows_ref[...])
    lat = (lax.broadcasted_iota(jnp.int32, (16, width), 1).astype(F32) + 0.5) * (1.0 / width)
    cos_lat = sin_pi(0.5 - lat)
    sin_lat = sin_whole(lat)
    for at in range(0, sites, 16):
        part = columns[at : at + 16, :]
        a = 2.0 + part[:, 8:9] * cos_lat
        b = part[:, 9:10] * sin_lat
        for n in range(COLS):
            k = site_kernel(a + b * part[:, n : n + 1])
            high = k.astype(BF16)
            high_ref[n, at : at + 16, :] = high
            low_ref[n, at : at + 16, :] = (k - high.astype(F32)).astype(BF16)


def two_parts(x):
    high = x.astype(BF16).astype(F32)
    return jnp.concatenate([high, x - high], axis=0).astype(BF16)


def product(x, high, low, contract):
    dims = (((1,), (contract,)), ((), ()))
    parts = two_parts(x)
    both = lax.dot_general(parts, high, dims, preferred_element_type=F32)
    rest = lax.dot_general(parts, low, dims, preferred_element_type=F32)
    return both[0:8, :] + (both[8:16, :] + rest[0:8, :])


def forward_kernel(
    steps_ref, v_ref, s_ref, west_ref, east_ref, low_ref, high_ref, ice_ref, k_high_ref, k_low_ref,
    pred_ref, corner_low_ref, corner_high_ref,
    fluid_ref, fluid_north_ref, field_ref, north_ref, south_ref, h_east_ref, h_north_ref,
    h_south_ref, h_up_ref, h_cut_ref, next_ref, next_north_ref, surf_ref, *, rad_n,
):
    nr, nl, width = v_ref.shape
    shape = Shape(nr, width, rad_n)
    half = shape.half
    lower, lon = shape.lower, shape.lon
    ends = (lon == 0) | (lon == 3)

    bottom = lax.axis_index("rad") == 0
    for n in range(4):
        for k, ref in enumerate((west_ref, east_ref)):
            down, up = ref[n * nr], ref[n * nr + nr - 1]
            if rad_n == 2:
                corner_low_ref[2 * n + k] = jnp.where(bottom, up, down)
            else:
                corner_low_ref[2 * n + k] = down
                corner_high_ref[2 * n + k] = up
    if rad_n == 2:
        corner_high_ref[...] = jnp.zeros_like(corner_high_ref)

    for i in range(half):
        f = jnp.exp(-pack(v_ref[i], v_ref[i + half]))
        fluid_ref[i] = f
        fluid_north_ref[i] = lat_next(f)
        for c in range(3):
            x = pack(s_ref[c, i], s_ref[c, i + half])
            field_ref[c, i] = x
            north_ref[c, i] = lat_next(x)
            south_ref[c, i] = lat_prev(x)
    for i in range(half):
        h_north = jnp.where(shape.not_last, face(fluid_ref[i], fluid_north_ref[i]), 0.0)
        h_north_ref[i] = h_north
        h_south_ref[i] = lat_prev(h_north)

    ring = pack(shape.has_low * jnp.exp(-low_ref[0]), shape.has_high * jnp.exp(-high_ref[0]))
    h_ring = face(ring, jnp.where(lower, fluid_ref[0], fluid_ref[half - 1]))
    seam = face(swap_halves(fluid_ref[0]), fluid_ref[half - 1])
    h_up_ref[half] = jnp.where(lower, seam, 0.0)
    h_up_ref[0] = swap_halves(h_up_ref[half])
    load = ice_ref[steps_ref[0]] * (1.0 - shape.has_high)
    load = pack(jnp.zeros_like(load), load)
    carry = [h_up_ref[0] * (field_ref[c, 0] - swap_halves(field_ref[c, half - 1])) for c in range(3)]
    for i in range(half):

        def side(n):
            return shape.sides(
                (west_ref[n * nr + i], west_ref[n * nr + i + half]),
                (east_ref[n * nr + i], east_ref[n * nr + i + half]),
            )

        f = fluid_ref[i]
        h_cut = jnp.where(ends, face(f, jnp.exp(-side(0))), 0.0)
        h_cut_ref[i] = h_cut
        h_east = jnp.where(lon < 3, face(f, lon_next(f)), 0.0)
        h_east_ref[i] = h_east
        if i < half - 1:
            h_up_ref[i + 1] = face(f, fluid_ref[i + 1])
        h_north, h_south, h_up = h_north_ref[i], h_south_ref[i], h_up_ref[i + 1]
        for c in range(3):
            x = field_ref[c, i]
            above = field_ref[c, i + 1] if i < half - 1 else swap_halves(field_ref[c, 0])
            east = h_east * (lon_next(x) - x)
            up = h_up * (above - x)
            total = (east - lon_prev(east)) + (up - carry[c]) + h_cut * (side(1 + c) - x)
            total = total + h_north * (north_ref[c, i] - x) + h_south * (south_ref[c, i] - x)
            if i in (0, half - 1):
                beyond = h_ring * (pack(low_ref[1 + c], high_ref[1 + c]) - x)
                if i == 0:
                    total = total + jnp.where(lower, beyond, 0.0)
                if i == half - 1:
                    total = total + jnp.where(lower, 0.0, beyond)
            s1 = x + RELAX_RATE * total
            if c == 0 and i == half - 1:
                s1 = s1 - load
            next_ref[c, i] = s1
            next_north_ref[c, i] = lat_next(s1)
            carry[c] = up

    zero = jnp.zeros((8, width), F32)
    column, east, north, cut = [zero] * 3, [zero] * 3, [zero] * 3, [zero] * 3
    below = [swap_halves(next_ref[c, half - 1]) for c in range(3)]
    for i in range(half):
        weight = shape.step(i)
        g_east = weight * h_east_ref[i]
        g_north = weight * h_north_ref[i]
        g_cut = weight * h_cut_ref[i]
        g_low = (RELAX_RATE * (weight - shape.step(i - 1))) * h_up_ref[i]
        for c in range(3):
            x = next_ref[c, i]
            column[c] = column[c] + (weight * x - g_low * (x - below[c]))
            east[c] = east[c] + g_east * (lon_next(x) - x)
            north[c] = north[c] + g_north * (next_north_ref[c, i] - x)
            cut[c] = cut[c] + g_cut * x
            below[c] = x
    top = shape.step(half - 1)
    g_ring = (RELAX_RATE * h_ring) * jnp.where(
        lower, shape.step(-1) - 1.0, shape.step(half) - top
    )
    for c in range(3):
        inner = jnp.where(lower, next_ref[c, 0], next_ref[c, half - 1])

        def folded(x):
            x = shape.first_weight * x
            return x + swap_halves(x)

        sum_east = folded(east[c])
        sum_north = folded(north[c])
        sum_cut = folded(cut[c])
        own = folded(column[c] + g_ring * inner)
        spread = (sum_east - lon_prev(sum_east)) + (sum_north - lat_prev(sum_north)) - sum_cut
        own = own + RELAX_RATE * spread
        if c == 0:
            second = ice_ref[steps_ref[1]] * (1.0 - shape.has_high)
            own = own - pack(second, second)
        surf_ref[0, c : c + 1, :] = RELAX_RATE * sum_cut[0:1, :]
        for col in range(4):
            surf_ref[col + 1, c : c + 1, :] = own[col : col + 1, :]
        surf_ref[5, c : c + 1, :] = RELAX_RATE * sum_cut[3:4, :]
    total = None
    for col in range(6):
        surf_ref[col, 3:8, :] = jnp.zeros((5, width), F32)
        term = product(surf_ref[col], k_high_ref[col + 1], k_low_ref[col + 1], 1)
        total = term if total is None else total + term
    sites = total.shape[1]
    spare = pred_ref.shape[2] - 3 * sites
    flat = [total[c : c + 1, :] for c in range(3)]
    if spare > 0:
        flat.append(jnp.zeros((1, spare), F32))
    flat = jnp.concatenate(flat, axis=1)
    for n in range(pred_ref.shape[0]):
        pred_ref[n] = flat


FIELD, FIELD_SIDE, BOTH, BOTH_SIDE, SHARE, FLUID, SIDE, BASE, BLOCK = 0, 3, 6, 9, 12, 18, 19, 24, 25
RING, LAST, LOW, LOW_BOTH, HIGH, HIGH_BOTH, ENDS = 0, 5, 12, 15, 18, 21, 24


def prepare_kernel(
    steps_ref, v_ref, m_ref, s_ref, ice_ref, west_ref, east_ref, west2_ref, east2_ref, low_ref,
    high_ref, corner_low_ref, corner_high_ref, blocks_ref,
    fluid_ref, field_ref, fluid_side_ref, field_side_ref, north_ref, south_ref, out_ref, sems,
    *, rad_n,
):
    nr, nl, width = v_ref.shape
    shape = Shape(nr, width, rad_n)
    half = shape.half
    lower, lon, western = shape.lower, shape.lon, shape.western

    def share(f, other):
        return other * reciprocal(f + other)

    def safe_share(f, other):
        return other * reciprocal(jnp.maximum(f + other, 1e-30))

    def north_of(f):
        return jnp.where(shape.not_last, lat_next(f), 0.0)

    def south_of(f):
        return jnp.where(shape.not_first, lat_prev(f), 0.0)

    def two(ref, n, i):
        return ref[n * nr + i], ref[n * nr + i + half]

    def corner(ref, n):
        return jnp.where(western, ref[2 * n], ref[2 * n + 1])

    for i in range(half):
        f = jnp.exp(-pack(v_ref[i], v_ref[i + half]))
        f_side = jnp.exp(-shape.sides(two(west_ref, 0, i), two(east_ref, 0, i)))
        fluid_ref[i + 1] = f
        fluid_side_ref[i + 1] = f_side
        north_ref[0, i], south_ref[0, i] = north_of(f), south_of(f)
        north_ref[1, i], south_ref[1, i] = north_of(f_side), south_of(f_side)
        for c in range(3):
            x = pack(s_ref[c, i], s_ref[c, i + half])
            x_side = shape.sides(two(west_ref, 1 + c, i), two(east_ref, 1 + c, i))
            field_ref[c, i + 1] = x
            field_side_ref[c, i + 1] = x_side
            north_ref[2 + c, i], south_ref[2 + c, i] = lat_next(x), lat_prev(x)
            north_ref[5 + c, i], south_ref[5 + c, i] = lat_next(x_side), lat_prev(x_side)
    ring = pack(shape.has_low * jnp.exp(-low_ref[0]), shape.has_high * jnp.exp(-high_ref[0]))
    ring_side = jnp.where(
        lower,
        shape.has_low * jnp.exp(-corner(corner_low_ref, 0)),
        shape.has_high * jnp.exp(-corner(corner_high_ref, 0)),
    )
    ring_field = [pack(low_ref[1 + c], high_ref[1 + c]) for c in range(3)]
    ring_field_side = [
        jnp.where(lower, corner(corner_low_ref, 1 + c), corner(corner_high_ref, 1 + c))
        for c in range(3)
    ]

    def close(ref, ring):
        ref[0] = jnp.where(lower, ring, swap_halves(ref[half]))
        ref[half + 1] = jnp.where(lower, swap_halves(ref[1]), ring)

    close(fluid_ref, ring)
    close(fluid_side_ref, ring_side)
    for c in range(3):
        close(field_ref.at[c], ring_field[c])
        close(field_side_ref.at[c], ring_field_side[c])

    def coefficients(f, shares, here, above, below):
        scaled = (2.0 * RELAX_RATE) * f
        weighted = scaled * here
        radial = scaled * (shares[4] * (above - here) + shares[5] * (below - here))
        return [weighted * shares[n] for n in range(4)] + [radial]

    def relaxed(f, shares, s, others):
        total = shares[0] * (others[0] - s)
        for n in range(1, 6):
            total = total + shares[n] * (others[n] - s)
        return s + (2.0 * RELAX_RATE) * (f * total)

    outer = pack(shape.has_low * jnp.exp(-low_ref[4]), shape.has_high * jnp.exp(-high_ref[4]))
    inner = jnp.where(lower, fluid_ref[1], fluid_ref[half])
    ring_shares = [
        safe_share(ring, jnp.where(lon == 3, ring_side, lon_next(ring))),
        safe_share(ring, jnp.where(lon == 0, ring_side, lon_prev(ring))),
        safe_share(ring, north_of(ring)),
        safe_share(ring, south_of(ring)),
        safe_share(ring, outer),
        safe_share(ring, inner),
    ]
    ring_coefficients = coefficients(
        ring,
        ring_shares,
        jnp.where(lower, shape.step(-1), shape.step(half)),
        jnp.where(lower, shape.step(-2), shape.step(half + 1)),
        jnp.where(lower, shape.step(0), shape.step(half - 1)),
    )
    for n in range(5):
        out_ref[half, RING + n] = ring_coefficients[n]
    ring_both = []
    for c in range(3):
        s, s_side = ring_field[c], ring_field_side[c]
        others = [
            jnp.where(lon == 3, s_side, lon_next(s)),
            jnp.where(lon == 0, s_side, lon_prev(s)),
            lat_next(s),
            lat_prev(s),
            pack(low_ref[5 + c], high_ref[5 + c]),
            jnp.where(lower, field_ref[c, 1], field_ref[c, half]),
        ]
        ring_both.append(s + relaxed(ring, ring_shares, s, others))
    load = ice_ref[steps_ref[0]]
    load = (1.0 - shape.has_high) * pack(jnp.zeros_like(load), load)
    load_side = jnp.where(
        western, west_ref[4 * nr + steps_ref[0]], east_ref[4 * nr + steps_ref[0]]
    )
    load_side = (1.0 - shape.has_high) * jnp.where(lower, 0.0, load_side)

    copies = []
    both_ends = {}

    def send(i):
        copies.append(pltpu.make_async_copy(out_ref.at[i], blocks_ref.at[i], sems.at[i]))
        copies[-1].start()

    for i in range(half):
        f, f_side = fluid_ref[i + 1], fluid_side_ref[i + 1]
        shares = [
            share(f, jnp.where(lon == 3, f_side, lon_next(f))),
            share(f, jnp.where(lon == 0, f_side, lon_prev(f))),
            share(f, north_ref[0, i]),
            share(f, south_ref[0, i]),
            share(f, fluid_ref[i + 2]),
            share(f, fluid_ref[i]),
        ]
        for n in range(6):
            out_ref[i, SHARE + n] = shares[n]
        out_ref[i, FLUID] = f
        if i == half - 1:
            for n in range(6):
                out_ref[half, LAST + n] = shares[n]
            out_ref[half, LAST + 6] = f
        out_ref[i, BASE] = pack(
            m_ref[i] - (0.5 * PRIOR_WEIGHT) * v_ref[i],
            m_ref[i + half] - (0.5 * PRIOR_WEIGHT) * v_ref[i + half],
        )
        f_far = jnp.exp(-shape.sides(two(west2_ref, 0, i), two(east2_ref, 0, i)))
        side_shares = [
            share(f_side, jnp.where(western, f, f_far)),
            share(f_side, jnp.where(western, f_far, f)),
            share(f_side, north_ref[1, i]),
            share(f_side, south_ref[1, i]),
            share(f_side, fluid_side_ref[i + 2]),
            share(f_side, fluid_side_ref[i]),
        ]
        side = coefficients(
            f_side, side_shares, shape.step(i), shape.step(i + 1), shape.step(i - 1)
        )
        for n in range(5):
            out_ref[i, SIDE + n] = side[n]
        for c in range(3):
            s, s_side = field_ref[c, i + 1], field_side_ref[c, i + 1]
            s_far = shape.sides(two(west2_ref, 1 + c, i), two(east2_ref, 1 + c, i))
            others = [
                jnp.where(lon == 3, s_side, lon_next(s)),
                jnp.where(lon == 0, s_side, lon_prev(s)),
                north_ref[2 + c, i],
                south_ref[2 + c, i],
                field_ref[c, i + 2],
                field_ref[c, i],
            ]
            both = s + relaxed(f, shares, s, others)
            others = [
                jnp.where(western, s, s_far),
                jnp.where(western, s_far, s),
                north_ref[5 + c, i],
                south_ref[5 + c, i],
                field_side_ref[c, i + 2],
                field_side_ref[c, i],
            ]
            both_side = s_side + relaxed(f_side, side_shares, s_side, others)
            if c == 0 and i == half - 1:
                both = both - load
                both_side = both_side - load_side
            out_ref[i, FIELD + c] = s
            out_ref[i, FIELD_SIDE + c] = s_side
            out_ref[i, BOTH + c] = both
            out_ref[i, BOTH_SIDE + c] = both_side
            if i in (0, half - 1):
                both_ends[c, i] = both
        send(i)
    low_step = shape.step(0) - shape.step(-1)
    high_step = shape.step(half) - shape.step(half - 1)
    for c in range(3):
        first, last = both_ends[c, 0], both_ends[c, half - 1]
        out_ref[half, LOW + c] = field_ref[c, 1] - field_ref[c, 0]
        out_ref[half, LOW_BOTH + c] = low_step * (
            first - jnp.where(lower, ring_both[c], swap_halves(last))
        )
        out_ref[half, HIGH + c] = field_ref[c, half + 1] - field_ref[c, half]
        out_ref[half, HIGH_BOTH + c] = high_step * (
            jnp.where(lower, swap_halves(first), ring_both[c]) - last
        )
    out_ref[half, ENDS:BLOCK] = jnp.zeros((BLOCK - ENDS, 8, width), F32)
    send(half)
    for copy in copies:
        copy.wait()


def gradient_kernel(
    v_ref, pred_ref, data_ref, k_high_ref, k_low_ref, blocks_ref,
    new_ref, half_ref, misfit_ref, sa_ref, d_ref, in_ref, e_ref, side_ref, north_ref, product_ref,
    total_ref, sems, *, scale, rad_n,
):
    nr, nl, width = v_ref.shape
    shape = Shape(nr, width, rad_n)
    half = shape.half
    sites = k_high_ref.shape[1]
    lon, lower = shape.lon, shape.lower
    copies = [
        pltpu.make_async_copy(blocks_ref.at[i], in_ref.at[i], sems.at[i]) for i in range(half + 1)
    ]
    copies[half].start()
    for i in range(half):
        copies[i].start()
    ends_ref = in_ref.at[half]

    flat = pred_ref[0]
    for n in range(1, pred_ref.shape[0]):
        flat = flat + pred_ref[n]
    predicted = jnp.concatenate(
        [flat[:, c * sites : (c + 1) * sites] for c in range(3)], axis=0
    )
    weight = data_ref[4:7, :]
    weighted = weight * (predicted * scale - data_ref[1:4, :])
    squares = jnp.sum(weighted * weighted, axis=1, keepdims=True)
    misfit_ref[...] = jnp.sum(squares, axis=0, keepdims=True) * (1.0 / (3 * sites))
    pulled = (weight * weighted) * scale
    pulled = jnp.concatenate([pulled, jnp.zeros((5, sites), F32)], axis=0)
    for col in range(COLS):
        spread = product(pulled, k_high_ref[col], k_low_ref[col], 0)
        for c in range(3):
            sa_ref[c, col : col + 1, :] = spread[c : c + 1, :]

    for c in range(3):
        x = sa_ref[c]

        def window(start):
            return shape.first_weight * jnp.where(
                lower,
                x if start == 0 else pltpu.roll(x, 8 - start, 0),
                x if start == 4 else pltpu.roll(x, (4 - start) % 8, 0),
            )

        own = window(2)
        east = window(3)
        west = window(1)
        outside = jnp.where(lon < 2, west, east)
        d_ref[0, c] = east - own
        d_ref[1, c] = west - own
        d_ref[2, c] = lat_next(own) - own
        d_ref[3, c] = lat_prev(own) - own
        d_ref[4, c] = own
        d_ref[5, c] = jnp.where(lon < 2, own, window(4)) - outside
        d_ref[6, c] = jnp.where(lon < 2, window(0), own) - outside
        d_ref[7, c] = lat_next(outside) - outside
        d_ref[8, c] = lat_prev(outside) - outside
        d_ref[9, c] = outside

    def change(coeffs, first):
        out = []
        for c in range(3):
            total = coeffs[0] * d_ref[first, c]
            for n in range(1, 5):
                total = total + coeffs[n] * d_ref[first + n, c]
            out.append(total)
        return out

    above, below = shape.step(1) - 1.0, shape.step(-1) - 1.0

    def own_change(ref, at, fluid, i):
        shares = [ref[at + n] for n in range(6)]
        scaled = (2.0 * RELAX_RATE * shape.step(i)) * fluid
        coeffs = shares[:4] + [above * shares[4] + below * shares[5]]
        return [scaled * x for x in change(coeffs, 0)]

    def first_pass(i):
        copies[i].wait()
        e = own_change(in_ref.at[i], SHARE, in_ref[i, FLUID], i)
        side = change([in_ref[i, SIDE + n] for n in range(5)], 5)
        for c in range(3):
            e_ref[c, i] = e[c]
            side_ref[c, i] = side[c]
            north_ref[c, i] = lat_next(in_ref[i, FIELD + c])
            north_ref[3 + c, i] = lat_next(in_ref[i, BOTH + c])
            north_ref[6 + c, i] = lat_next(e[c])

    def second_pass(i, p_down):
        here, step = shape.step(i), shape.step(i + 1) - shape.step(i)
        weighted = [0.0] * 4
        plain = [0.0] * 4
        for c in range(3):
            s, s_side = in_ref[i, FIELD + c], in_ref[i, FIELD_SIDE + c]
            both, both_side = in_ref[i, BOTH + c], in_ref[i, BOTH_SIDE + c]
            e, e_side = e_ref[c, i], side_ref[c, i]

            def differences(x, x_side, x_north):
                return [jnp.where(lon == 3, x_side, lon_next(x)) - x, x_side - x, x_north - x]

            d_field = differences(s, s_side, north_ref[c, i])
            d_both = differences(both, both_side, north_ref[3 + c, i])
            d_e = differences(e, e_side, north_ref[6 + c, i])
            if i < half - 1:
                d_field.append(in_ref[i + 1, FIELD + c] - s)
                d_both.append(step * (in_ref[i + 1, BOTH + c] - both))
                d_e.append(e_ref[c, i + 1] - e)
            else:
                d_field.append(ends_ref[HIGH + c])
                d_both.append(ends_ref[HIGH_BOTH + c])
                d_e.append(jnp.where(lower, swap_halves(e_ref[c, 0]), ring[c]) - e)
            slopes = [d_ref[0, c], d_ref[1, c], d_ref[2, c], d_ref[4, c]]
            for n in range(4):
                weighted[n] = weighted[n] + d_both[n] * slopes[n]
                plain[n] = plain[n] + d_field[n] * d_e[n]
        p_east, p_cut, p_north = [here * weighted[n] + plain[n] for n in range(3)]
        p_up = weighted[3] + plain[3]
        p_west = jnp.where(lon == 0, p_cut, lon_prev(p_east))
        product_ref[i] = lat_prev(p_north)
        total = None
        for n, x in ((0, p_east), (1, p_west), (2, p_north), (4, p_up), (5, p_down)):
            share = in_ref[i, SHARE + n]
            term = (share * share) * x
            total = term if total is None else total + term
        total_ref[i] = total
        return p_up

    def third_pass(i):
        share = in_ref[i, SHARE + 3]
        total = total_ref[i] + (share * share) * product_ref[i]
        total = in_ref[i, BASE] - RELAX_RATE * (in_ref[i, FLUID] * total)
        half_ref[i] = total[0:4, :]
        half_ref[i + half] = total[4:8, :]
        new_ref[i] = v_ref[i] + total[0:4, :]
        new_ref[i + half] = v_ref[i + half] + total[4:8, :]

    copies[half].wait()
    ring = change([ends_ref[RING + n] for n in range(5)], 0)
    e_last = own_change(ends_ref, LAST, ends_ref[LAST + 6], half - 1)
    lead = min(2, half)
    for i in range(lead):
        first_pass(i)
    p_down = None
    for c in range(3):
        e_low = jnp.where(lower, ring[c], swap_halves(e_last[c]))
        term = ends_ref[LOW_BOTH + c] * d_ref[4, c] + ends_ref[LOW + c] * (e_ref[c, 0] - e_low)
        p_down = term if p_down is None else p_down + term
    for i in range(half):
        if i + lead < half:
            first_pass(i + lead)
        p_down = second_pass(i, p_down)
        if i > 0:
            third_pass(i - 1)
    third_pass(half - 1)


def call(
    kernel, outs, ins, scratch=(), flops=1, name=None, held_in=(), held_out=(), far_in=(),
    far_out=(), near_out=(),
):
    spaces = {"s": pltpu.SMEM, "v": pltpu.VMEM, "h": pltpu.HBM}
    made = pl.pallas_call(
        kernel,
        out_shape=[
            pltpu.VMEM(shape, dtype)
            if n in held_out
            else pltpu.HBM(shape, dtype)
            if n in far_out or n in near_out
            else jax.ShapeDtypeStruct(shape, dtype)
            for n, (shape, dtype) in enumerate(outs)
        ],
        in_specs=[pl.BlockSpec(memory_space=spaces[k]) for k in ins],
        out_specs=[
            pl.BlockSpec(memory_space=pltpu.HBM if n in far_out else pltpu.VMEM)
            for n in range(len(outs))
        ],
        scratch_shapes=list(scratch),
        compiler_params=pltpu.CompilerParams(vmem_limit_bytes=VMEM_LIMIT),
        cost_estimate=pl.CostEstimate(flops=flops, bytes_accessed=1 << 20, transcendentals=0),
        name=name,
    )

    def run(*args):
        return made(
            *[
                pltpu.with_memory_space_constraint(a, pltpu.VMEM if n in held_in else pltpu.HBM)
                if n in held_in or n in far_in
                else a
                for n, a in enumerate(args)
            ]
        )

    return run


def body(
    logvisc, momentum, displacement, ice_history, load_steps, site_cells, observed, site_weight
):
    nr, nl, nlat = logvisc.shape
    own_sites = site_cells.shape[0]
    lon_n = lax.axis_size("lon")
    rad_n = lax.axis_size("rad")
    total_lon = nl * lon_n
    sites = own_sites * lon_n
    devices = lon_n * rad_n
    half = nr // 2
    scale = 1.0 / math.sqrt(total_lon * nlat)
    row = (8, nlat)

    def across_rad(down, up):
        if rad_n == 2:
            both = lax.ppermute(down, "rad", [(0, 1), (1, 0)])
            return both, both
        upward = [(i, i + 1) for i in range(rad_n - 1)]
        downward = [(t, s) for s, t in upward]
        return lax.ppermute(up, "rad", upward), lax.ppermute(down, "rad", downward)

    eastward = [(i, (i + 1) % lon_n) for i in range(lon_n)]
    westward = [(t, s) for s, t in eastward]
    column, layers = (4 * nr, 1, nlat), (8, nl, nlat)
    first_column = (4 * nr + ice_history.shape[0], 1, nlat)
    (packets,) = call(
        packet_kernel,
        [((lon_n, 8, own_sites), F32)],
        "vvv",
        name="packet",
        flops=575000000,
        far_in=(0, 1, 2),
    )(site_cells[None], observed, site_weight)
    gathered = lax.all_to_all(packets, "lon", 0, 0)
    to_west, to_east, to_west2, to_east2, to_low, to_high = call(
        functools.partial(message_kernel, rad_n=rad_n),
        [(shape, F32) for shape in [first_column] * 2 + [column] * 2 + [layers] * 2],
        "vvv",
        name="messages",
        flops=2875000000,
        far_in=(0, 1, 2),
    )(logvisc, displacement, ice_history)
    west = lax.ppermute(to_east, "lon", eastward)
    east = lax.ppermute(to_west, "lon", westward)
    low, high = across_rad(to_low, to_high)
    west2 = lax.ppermute(to_east2, "lon", eastward)
    east2 = lax.ppermute(to_west2, "lon", westward)

    k_high, k_low, data = call(
        functools.partial(weights_kernel, total_lon=total_lon),
        [((COLS, sites, nlat), BF16)] * 2 + [((8, sites), F32)],
        "v",
        scratch=[pltpu.VMEM((16, sites), F32)],
        name="site_weights",
        flops=3680000000,
        held_out=(0, 1, 2),
    )(gathered)

    padded = -(-3 * sites // 128) * 128
    partial, to_corner_low, to_corner_high = call(
        functools.partial(forward_kernel, rad_n=rad_n),
        [((devices, 1, padded), F32), ((8, 1, nlat), F32), ((8, 1, nlat), F32)],
        "s" + "v" * 9,
        scratch=[
            pltpu.VMEM(shape + row, F32)
            for shape in [(half,)] * 2 + [(3, half)] * 3 + [(half,)] * 3 + [(half + 1,), (half,)]
            + [(3, half)] * 2 + [(6,)]
        ],
        name="forward",
        flops=6325000000,
        held_in=(8, 9),
        far_in=(1, 2, 7),
        near_out=(0, 1, 2),
    )(load_steps, logvisc, displacement, west, east, low, high, ice_history, k_high, k_low)
    predicted = lax.all_to_all(partial, ("lon", "rad"), 0, 0)

    corner_low, corner_high = across_rad(to_corner_low, to_corner_high)
    (blocks,) = call(
        functools.partial(prepare_kernel, rad_n=rad_n),
        [((half + 1, BLOCK) + row, F32)],
        "s" + "v" * 12,
        scratch=[
            pltpu.VMEM(shape + row, F32)
            for shape in [(half + 2,), (3, half + 2)] * 2 + [(8, half)] * 2 + [(half + 1, BLOCK)]
        ]
        + [pltpu.SemaphoreType.DMA((half + 1,))],
        name="prepare",
        flops=8050000000,
        far_in=(1, 2, 3, 4),
        far_out=(0,),
    )(
        load_steps, logvisc, momentum, displacement, ice_history, west, east, west2, east2, low,
        high, corner_low, corner_high,
    )

    new_logvisc, half_momentum, misfit = call(
        functools.partial(gradient_kernel, scale=scale, rad_n=rad_n),
        [((nr, nl, nlat), F32), ((nr, nl, nlat), F32), ((1, 1), F32)],
        "vvvvvh",
        scratch=[
            pltpu.VMEM(shape + row, F32)
            for shape in [(3,), (10, 3), (half + 1, BLOCK), (3, half), (3, half), (9, half)]
            + [(half,)] * 2
        ]
        + [pltpu.SemaphoreType.DMA((half + 1,))],
        name="gradient",
        flops=6900000000,
        held_in=(2, 3, 4),
        far_in=(0, 5),
    )(logvisc, predicted, data, k_high, k_low, blocks)
    return (new_logvisc, half_momentum, misfit.reshape(1))


def solution(mesh):
    return jax.shard_map(
        body,
        mesh=mesh,
        in_specs=(
            P("rad", "lon", None),
            P("rad", "lon", None),
            P(None, "rad", "lon", None),
            P(None, "lon", None),
            P(),
            P("lon"),
            P(None, "lon"),
            P(None, "lon"),
        ),
        out_specs=(P("rad", "lon", None), P("rad", "lon", None), P()),
        check_vma=False,
    )
```

time: 69.6 us -> 54.4 us (0.78)
  local copies, waits for them, and re-layouts: 8.7 us -> 1.42 us
  waiting for transfers between devices: 4.6 us -> 0.66 us
  Pallas kernels: 33.3 us -> 30.6 us
  starting transfers between devices: 21.5 us -> 20.4 us
    unnamed x22 -> x10, local copies, waits for them, and re-layouts: 6.16 us -> 1.42 us
    pallas_call x6, Pallas kernels: 33.3 us -> 30.6 us  [run(): made(*[pltpu.with_memory_space_constraint(a, pltpu.VMEM if n in held_in e...]
    slice x3 -> x0, local copies, waits for them, and re-layouts: 2.54 us -> none  [body(): x[:4 * nr].reshape(4, nr, 1, nlat)[:, r]]
    ppermute x2, waiting for transfers between devices: 2.14 us -> 0.01 us  [across_rad(): both = lax.ppermute(down, 'rad', [(0, 1), (1, 0)])]
    all_to_all x1, waiting for transfers between devices: 2.45 us -> 0.64 us  [body(): gathered = lax.all_to_all(packets, 'lon', 0, 0)]
    all_to_all x1, starting transfers between devices: 4.49 us -> 2.75 us  [body(): predicted = lax.all_to_all(partial, ('lon', 'rad'), 0, 0)]
  transfers between devices with their start and end apart: 8 -> 8, of which waited for: 2 -> 1; matrix products, arithmetic and copies ran while one was open for 4% -> 0% of each run, Pallas kernels for 32% -> 38%
where the time goes in v3:
time: 54.4 us; the launch traced here: 54 us
  Pallas kernels  30.6 us (56%)
  starting transfers between devices  20.4 us (38%)
  local copies, waits for them, and re-layouts  1.42 us (3%)
  between operations  0.93 us (2%)
  waiting for transfers between devices  0.66 us (1%)
    pallas_call x6, Pallas kernels, run(): made(*[pltpu.with_memory_space_constraint(a, pltpu.VMEM if n in held_in e...  30.6 us
    ppermute x1, starting transfers between devices, body(): east = lax.ppermute(to_west, 'lon', westward)  4.99 us
    ppermute x1, starting transfers between devices, body(): east2 = lax.ppermute(to_west2, 'lon', westward)  4.44 us
    ppermute x2, starting transfers between devices, across_rad(): both = lax.ppermute(down, 'rad', [(0, 1), (1, 0)])  4.06 us
    all_to_all x1, starting transfers between devices, body(): gathered = lax.all_to_all(packets, 'lon', 0, 0)  3.68 us
    all_to_all x1, starting transfers between devices, body(): predicted = lax.all_to_all(partial, ('lon', 'rad'), 0, 0)  2.75 us
    unnamed x10, local copies, waits for them, and re-layouts  1.42 us
  transfers between devices with their start and end apart: 8, of which 1 were waited for; matrix products, arithmetic and copies ran while one was open for 0% of the time, Pallas kernels for 38%

profile of v3, /device:TPU:0, one launch (start us, length us, event | category | flops | bytes accessed | tf_op | source)
XLA Modules:
  0.0 54.0 jit_solution(12835543870447831744)
XLA Ops:
  0.6 2.3 %messages.1 = (f32[200,1,512]{2,1,0:T(1,128)S(1)}, f32[200,1,512]{2,1,0:T(1,128)S(1)}, f32[192,1,512]{2,1,0:T(1,128)S(1)}, f32[192,1,512]{2,1,0:T(1,128)S(1)}, f...) custom-call(f32[48,4,512]{2,1,0:T(4,128)} %v_ref.7, f32[3,48,4,512]{3,2,1,0:T(4,128)} %s_ref.5, f32[8,4,512]{2,1,0:T(4,128)} %ice_ref.5), custom_call_target="tpu_custom_call" | custom-call | flops 2875000064 | bytes 1048576 | tf_op jit(solution)/shard_map/messages/pallas_call | solution.py:732
  2.9 0.5 collective-permute-start
  3.4 5.0 %collective-permute-start.1 = (f32[200,1,512]{2,1,0:T(1,128)S(1)}, f32[200,1,512]{2,1,0:T(1,128)S(1)}, u32[]{:S(2)}, u32[]{:S(2)}) collective-permute-start(f32[200,1,512]{2,1,0:T(1,128)S(1)} %get-tuple-element.17), channel_id=1, source_target_pairs={{2,0},{4,2},{6,4},{8,6},{10,8},{12,10},{14,12},{16,14},{18,16},{20... | collective-permute-start | bytes 1228808 | tf_op jit(solution)/shard_map/ppermute | solution.py:788
  8.4 1.4 %packet.1 = f32[16,8,12]{2,1,0:T(8,128)} custom-call(s32[1,12]{1,0:T(1,128)} %bitcast.2, f32[3,12]{1,0:T(4,128)} %obs_ref.1, f32[3,12]{1,0:T(4,128)} %wt_ref.1), custom_call_target="tpu_custom_call" | custom-call | flops 575000000 | bytes 1048576 | tf_op jit(solution)/shard_map/packet/pallas_call | solution.py:732
  9.7 3.7 %all-to-all-start = ((f32[16,8,12]{2,1,0:T(8,128)}), f32[16,8,12]{2,1,0:T(8,128)S(1)}, u32[]{:S(2)}, u32[]{:S(2)}) async-start(f32[16,8,12]{2,1,0:T(8,128)} %packet.1), calls=%async_computation | async-start | bytes 131072 | tf_op jit(solution)/shard_map/all_to_all | solution.py:778
  13.4 1.8 %collective-permute-start.2 = (f32[8,4,512]{2,1,0:T(4,128)S(1)}, f32[8,4,512]{2,1,0:T(4,128)S(1)}, u32[]{:S(2)}, u32[]{:S(2)}) collective-permute-start(f32[8,4,512]{2,1,0:T(4,128)S(1)} %get-tuple-element.18), channel_id=1, source_target_pairs={{0,1},{1,0},{2,3},{3,2},{4,5},{5,4},{6,7},{7,6},{8,9},{9,8},{10,11... | collective-permute-start | bytes 196616 | tf_op jit(solution)/shard_map/ppermute | solution.py:760
  15.2 0.0 collective-permute-start.3
  15.2 0.0 copy-start
  15.2 4.4 %collective-permute-start.4 = (f32[192,1,512]{2,1,0:T(1,128)S(1)}, f32[192,1,512]{2,1,0:T(1,128)S(1)}, u32[]{:S(2)}, u32[]{:S(2)}) collective-permute-start(f32[192,1,512]{2,1,0:T(1,128)S(1)} %get-tuple-element.24), channel_id=1, source_target_pairs={{2,0},{4,2},{6,4},{8,6},{10,8},{12,10},{14,12},{16,14},{18,16},{20... | collective-permute-start | bytes 1179656 | tf_op jit(solution)/shard_map/ppermute | solution.py:791
  19.7 0.6 %all-to-all-done.gathered_ref = f32[16,8,12]{2,1,0:T(8,128)S(1)} async-done(((f32[16,8,12]{2,1,0:T(8,128)}), f32[16,8,12]{2,1,0:T(8,128)S(1)}, u32[]{:S(2)}, u32[]{:S(2)}) %all-to-all-start) | async-done | bytes 6176 | tf_op jit(solution)/shard_map/all_to_all | solution.py:778
  20.3 3.2 %site_weights.1 = (bf16[8,192,512]{2,1,0:T(8,128)(2,1)S(1)}, bf16[8,192,512]{2,1,0:T(8,128)(2,1)S(1)}, f32[8,192]{1,0:T(8,128)S(1)}) custom-call(f32[16,8,12]{2,1,0:T(8,128)S(1)} %all-to-all-done.gathered_ref), custom_call_target="tpu_custom_call" | custom-call | flops 3680000000 | bytes 1048576 | tf_op jit(solution)/shard_map/site_weights/pallas_call | solution.py:732
  23.5 0.0 copy-start.1
  23.5 0.0 copy-start.3
  23.6 0.0 collective-permute-done.2.low_ref.high_ref
  23.6 0.0 collective-permute-done.west_ref
  23.6 0.0 collective-permute-done.1.east_ref
  23.6 0.0 copy-done
  23.6 6.4 %forward.1 = (f32[32,1,640]{2,1,0:T(1,128)}, f32[8,1,512]{2,1,0:T(1,128)}, f32[8,1,512]{2,1,0:T(1,128)}) custom-call(s32[2]{0:T(128)S(1)} %copy-done, f32[48,4,512]{2,1,0:T(4,128)} %v_ref.7, f32[3,48,4,512]{3,2,1,0:T(4,128)} %s_ref.5, f32[200,1,512]{2,1,0:T(1,128)S(1)} %collective-permute-done.west_ref, f32[200,1,512]{2,1,0:T(1,128)S(1)} %collective-permute-done.1.east_ref, ...), custom_call_target="tpu_custom_call" | custom-call | flops 6325000192 | bytes 1048576 | tf_op jit(solution)/shard_map/forward/pallas_call | solution.py:732
  30.0 0.0 copy-done.1
  30.0 0.0 copy-done.3
  30.0 2.2 %collective-permute-start.5 = (f32[8,1,512]{2,1,0:T(1,128)}, f32[8,1,512]{2,1,0:T(1,128)S(1)}, u32[]{:S(2)}, u32[]{:S(2)}) collective-permute-start(f32[8,1,512]{2,1,0:T(1,128)} %get-tuple-element.25), channel_id=1, source_target_pairs={{0,1},{1,0},{2,3},{3,2},{4,5},{5,4},{6,7},{7,6},{8,9},{9,8},{10,11... | collective-permute-start | bytes 49160 | tf_op jit(solution)/shard_map/ppermute | solution.py:760
  32.2 2.8 %all-to-all-start.1 = ((f32[32,1,640]{2,1,0:T(1,128)}), f32[32,1,640]{2,1,0:T(1,128)S(1)}, u32[]{:S(2)}, u32[]{:S(2)}) async-start(f32[32,1,640]{2,1,0:T(1,128)} %get-tuple-element.21), calls=%async_computation.1 | async-start | bytes 163840 | tf_op jit(solution)/shard_map/all_to_all | solution.py:819
  35.0 0.0 collective-permute-done.3.west2_ref
  35.0 0.0 collective-permute-done.4.east2_ref
  35.0 0.0 copy-start.2
  35.0 0.0 collective-permute-done.5.corner_low_ref.corner_high_ref
  35.0 9.4 %prepare.1.blocks_ref = f32[25,25,8,512]{3,2,1,0:T(8,128)} custom-call(s32[2]{0:T(128)S(1)} %copy-done, f32[48,4,512]{2,1,0:T(4,128)} %v_ref.7, f32[48,4,512]{2,1,0:T(4,128)} %m_ref.1, f32[3,48,4,512]{3,2,1,0:T(4,128)} %s_ref.5, f32[8,4,512]{2,1,0:T(4,128)} %ice_ref.5, f32[200,1,512]{2,1,0:T(1,128)S(1)} %collective-permute-done.west_ref, ...), custom_call_target="tpu_custom_call" | custom-call | flops 8049999872 | bytes 1048576 | tf_op jit(solution)/shard_map/prepare/pallas_call | solution.py:732
  44.5 0.0 all-to-all-done.1.pred_ref
  44.5 0.0 copy-done.2
  44.5 0.0 copy-start.4
  44.5 1.4 %copy-done.4 = bf16[8,192,512]{2,1,0:T(8,128)(2,1)S(1)} copy-done((bf16[8,192,512]{2,1,0:T(8,128)(2,1)S(1)}, bf16[8,192,512]{2,1,0:T(8,128)(2,1)}, u32[]{:S(2)}) %copy-start.4) | copy-done | bytes 1572888
  45.9 7.9 %gradient.1 = (f32[48,4,512]{2,1,0:T(4,128)}, f32[48,4,512]{2,1,0:T(4,128)}, f32[1,1]{1,0:T(1,128)}) custom-call(f32[48,4,512]{2,1,0:T(4,128)} %v_ref.7, f32[32,1,640]{2,1,0:T(1,128)S(1)} %all-to-all-done.1.pred_ref, f32[8,192]{1,0:T(8,128)S(1)} %get-tuple-element.22.data_ref, bf16[8,192,512]{2,1,0:T(8,128)(2,1)S(1)} %copy-done.2, ...), custom_call_target="tpu_custom_call" | custom-call | flops 6899999744 | bytes 1048576 | tf_op jit(solution)/shard_map/gradient/pallas_call | solution.py:732
Async XLA Ops:
  2.9 20.7 %collective-permute-start = (f32[200,1,512]{2,1,0:T(1,128)S(1)}, f32[200,1,512]{2,1,0:T(1,128)S(1)}, u32[]{:S(2)}, u32[]{:S(2)}) collective-permute-start(f32[200,1,512]{2,1,0:T(1,128)S(1)} %get-tuple-element.16), channel_id=1, source_target_pairs={{0,2},{2,4},{4,6},{6,8},{8,10},{10,12},{12,14},{14,16},{16,18},{18... | collective-permute-start | bytes 1228808 | tf_op jit(solution)/shard_map/ppermute | solution.py:787
  3.4 20.2 %collective-permute-start.1 = (f32[200,1,512]{2,1,0:T(1,128)S(1)}, f32[200,1,512]{2,1,0:T(1,128)S(1)}, u32[]{:S(2)}, u32[]{:S(2)}) collective-permute-start(f32[200,1,512]{2,1,0:T(1,128)S(1)} %get-tuple-element.17), channel_id=1, source_target_pairs={{2,0},{4,2},{6,4},{8,6},{10,8},{12,10},{14,12},{16,14},{18,16},{20... | collective-permute-start | bytes 1228808 | tf_op jit(solution)/shard_map/ppermute | solution.py:788
  9.7 10.6 %all-to-all-start = ((f32[16,8,12]{2,1,0:T(8,128)}), f32[16,8,12]{2,1,0:T(8,128)S(1)}, u32[]{:S(2)}, u32[]{:S(2)}) async-start(f32[16,8,12]{2,1,0:T(8,128)} %packet.1), calls=%async_computation | async-start | bytes 131072 | tf_op jit(solution)/shard_map/all_to_all | solution.py:778
  13.4 10.1 %collective-permute-start.2 = (f32[8,4,512]{2,1,0:T(4,128)S(1)}, f32[8,4,512]{2,1,0:T(4,128)S(1)}, u32[]{:S(2)}, u32[]{:S(2)}) collective-permute-start(f32[8,4,512]{2,1,0:T(4,128)S(1)} %get-tuple-element.18), channel_id=1, source_target_pairs={{0,1},{1,0},{2,3},{3,2},{4,5},{5,4},{6,7},{7,6},{8,9},{9,8},{10,11... | collective-permute-start | bytes 196616 | tf_op jit(solution)/shard_map/ppermute | solution.py:760
  15.2 19.8 %collective-permute-start.3 = (f32[192,1,512]{2,1,0:T(1,128)S(1)}, f32[192,1,512]{2,1,0:T(1,128)S(1)}, u32[]{:S(2)}, u32[]{:S(2)}) collective-permute-start(f32[192,1,512]{2,1,0:T(1,128)S(1)} %get-tuple-element.23), channel_id=1, source_target_pairs={{0,2},{2,4},{4,6},{6,8},{8,10},{10,12},{12,14},{14,16},{16,18},{18... | collective-permute-start | bytes 1179656 | tf_op jit(solution)/shard_map/ppermute | solution.py:790
  15.2 8.4 %copy-start = (s32[2]{0:T(128)S(1)}, s32[2]{0:T(128)}, u32[]{:S(2)}) copy-start(s32[2]{0:T(128)} %steps_ref.3) | copy-start | bytes 28
  15.2 19.8 %collective-permute-start.4 = (f32[192,1,512]{2,1,0:T(1,128)S(1)}, f32[192,1,512]{2,1,0:T(1,128)S(1)}, u32[]{:S(2)}, u32[]{:S(2)}) collective-permute-start(f32[192,1,512]{2,1,0:T(1,128)S(1)} %get-tuple-element.24), channel_id=1, source_target_pairs={{2,0},{4,2},{6,4},{8,6},{10,8},{12,10},{14,12},{16,14},{18,16},{20... | collective-permute-start | bytes 1179656 | tf_op jit(solution)/shard_map/ppermute | solution.py:791
  23.5 6.5 %copy-start.1 = (bf16[8,192,512]{2,1,0:T(8,128)(2,1)}, bf16[8,192,512]{2,1,0:T(8,128)(2,1)S(1)}, u32[]{:S(2)}) copy-start(bf16[8,192,512]{2,1,0:T(8,128)(2,1)S(1)} %get-tuple-element.19.k_high_ref) | copy-start | bytes 4718596
  23.5 6.5 %copy-start.3 = (bf16[8,192,512]{2,1,0:T(8,128)(2,1)}, bf16[8,192,512]{2,1,0:T(8,128)(2,1)S(1)}, u32[]{:S(2)}) copy-start(bf16[8,192,512]{2,1,0:T(8,128)(2,1)S(1)} %get-tuple-element.20.k_low_ref) | copy-start | bytes 4718596
  30.0 5.0 %collective-permute-start.5 = (f32[8,1,512]{2,1,0:T(1,128)}, f32[8,1,512]{2,1,0:T(1,128)S(1)}, u32[]{:S(2)}, u32[]{:S(2)}) collective-permute-start(f32[8,1,512]{2,1,0:T(1,128)} %get-tuple-element.25), channel_id=1, source_target_pairs={{0,1},{1,0},{2,3},{3,2},{4,5},{5,4},{6,7},{7,6},{8,9},{9,8},{10,11... | collective-permute-start | bytes 49160 | tf_op jit(solution)/shard_map/ppermute | solution.py:760
  32.2 12.3 %all-to-all-start.1 = ((f32[32,1,640]{2,1,0:T(1,128)}), f32[32,1,640]{2,1,0:T(1,128)S(1)}, u32[]{:S(2)}, u32[]{:S(2)}) async-start(f32[32,1,640]{2,1,0:T(1,128)} %get-tuple-element.21), calls=%async_computation.1 | async-start | bytes 163840 | tf_op jit(solution)/shard_map/all_to_all | solution.py:819
  35.0 9.5 %copy-start.2 = (bf16[8,192,512]{2,1,0:T(8,128)(2,1)S(1)}, bf16[8,192,512]{2,1,0:T(8,128)(2,1)}, u32[]{:S(2)}) copy-start(bf16[8,192,512]{2,1,0:T(8,128)(2,1)} %copy-done.1) | copy-start | bytes 4718596
  44.5 1.4 %copy-start.4 = (bf16[8,192,512]{2,1,0:T(8,128)(2,1)S(1)}, bf16[8,192,512]{2,1,0:T(8,128)(2,1)}, u32[]{:S(2)}) copy-start(bf16[8,192,512]{2,1,0:T(8,128)(2,1)} %copy-done.3) | copy-start | bytes 4718596

commit v4 on v3

--- a/solution.py
+++ b/solution.py
@@ -90,13 +90,19 @@
     return p * u
 
 
-def site_kernel(d):
-    turns = d * (KERNEL_WAVE / (2.0 * math.pi))
+TURNS = KERNEL_WAVE / (2.0 * math.pi)
+
+
+def site_kernel(turns):
     s = sin_pi(turns - jnp.round(turns))
-    return (reciprocal(1.0 + d * (1.0 / KERNEL_WIDTH)) + 0.5) - s * s
-
-
-def packet_kernel(cells_ref, obs_ref, wt_ref, packet_ref):
+    return (reciprocal(1.0 + turns * (1.0 / (KERNEL_WIDTH * TURNS))) + 0.5) - s * s
+
+
+def message_kernel(
+    v_ref, s_ref, ice_ref, cells_ref, obs_ref, wt_ref,
+    west_ref, east_ref, west2_ref, east2_ref, low_ref, high_ref, packet_ref, *, rad_n,
+):
+    nr, nl, width = v_ref.shape
     packet = jnp.concatenate(
         [
             cells_ref[...].astype(F32),
@@ -108,12 +114,6 @@
     )
     for n in range(packet_ref.shape[0]):
         packet_ref[n] = packet
-
-
-def message_kernel(
-    v_ref, s_ref, ice_ref, west_ref, east_ref, west2_ref, east2_ref, low_ref, high_ref, *, rad_n
-):
-    nr, nl, width = v_ref.shape
 
     def field(n, r):
         return v_ref[r] if n == 0 else s_ref[n - 1, r]
@@ -168,8 +168,8 @@
     turns = col * (1.0 / total_lon)
     col_cos, col_sin = circle(turns - jnp.floor(turns))
     rows_ref[0:8, :] = col_cos * site_cos + col_sin * site_sin
-    rows_ref[8:9, :] = -2.0 * sin_pi(0.5 - theta)
-    rows_ref[9:10, :] = -2.0 * sin_whole(theta)
+    rows_ref[8:9, :] = (-2.0 * TURNS) * sin_pi(0.5 - theta)
+    rows_ref[9:10, :] = (-2.0 * TURNS) * sin_whole(theta)
     rows_ref[10:16, :] = jnp.zeros((6, sites), F32)
     columns = jnp.transpose(rows_ref[...])
     lat = (lax.broadcasted_iota(jnp.int32, (16, width), 1).astype(F32) + 0.5) * (1.0 / width)
@@ -177,7 +177,7 @@
     sin_lat = sin_whole(lat)
     for at in range(0, sites, 16):
         part = columns[at : at + 16, :]
-        a = 2.0 + part[:, 8:9] * cos_lat
+        a = 2.0 * TURNS + part[:, 8:9] * cos_lat
         b = part[:, 9:10] * sin_lat
         for n in range(COLS):
             k = site_kernel(a + b * part[:, n : n + 1])
@@ -369,7 +369,7 @@
     def corner(ref, n):
         return jnp.where(western, ref[2 * n], ref[2 * n + 1])
 
-    for i in range(half):
+    def pack_row(i):
         f = jnp.exp(-pack(v_ref[i], v_ref[i + half]))
         f_side = jnp.exp(-shape.sides(two(west_ref, 0, i), two(east_ref, 0, i)))
         fluid_ref[i + 1] = f
@@ -383,6 +383,10 @@
             field_side_ref[c, i + 1] = x_side
             north_ref[2 + c, i], south_ref[2 + c, i] = lat_next(x), lat_prev(x)
             north_ref[5 + c, i], south_ref[5 + c, i] = lat_next(x_side), lat_prev(x_side)
+
+    lead = min(2, half - 1)
+    for i in [half - 1] + list(range(lead)):
+        pack_row(i)
     ring = pack(shape.has_low * jnp.exp(-low_ref[0]), shape.has_high * jnp.exp(-high_ref[0]))
     ring_side = jnp.where(
         lower,
@@ -417,37 +421,6 @@
             total = total + shares[n] * (others[n] - s)
         return s + (2.0 * RELAX_RATE) * (f * total)
 
-    outer = pack(shape.has_low * jnp.exp(-low_ref[4]), shape.has_high * jnp.exp(-high_ref[4]))
-    inner = jnp.where(lower, fluid_ref[1], fluid_ref[half])
-    ring_shares = [
-        safe_share(ring, jnp.where(lon == 3, ring_side, lon_next(ring))),
-        safe_share(ring, jnp.where(lon == 0, ring_side, lon_prev(ring))),
-        safe_share(ring, north_of(ring)),
-        safe_share(ring, south_of(ring)),
-        safe_share(ring, outer),
-        safe_share(ring, inner),
-    ]
-    ring_coefficients = coefficients(
-        ring,
-        ring_shares,
-        jnp.where(lower, shape.step(-1), shape.step(half)),
-        jnp.where(lower, shape.step(-2), shape.step(half + 1)),
-        jnp.where(lower, shape.step(0), shape.step(half - 1)),
-    )
-    for n in range(5):
-        out_ref[half, RING + n] = ring_coefficients[n]
-    ring_both = []
-    for c in range(3):
-        s, s_side = ring_field[c], ring_field_side[c]
-        others = [
-            jnp.where(lon == 3, s_side, lon_next(s)),
-            jnp.where(lon == 0, s_side, lon_prev(s)),
-            lat_next(s),
-            lat_prev(s),
-            pack(low_ref[5 + c], high_ref[5 + c]),
-            jnp.where(lower, field_ref[c, 1], field_ref[c, half]),
-        ]
-        ring_both.append(s + relaxed(ring, ring_shares, s, others))
     load = ice_ref[steps_ref[0]]
     load = (1.0 - shape.has_high) * pack(jnp.zeros_like(load), load)
     load_side = jnp.where(
@@ -463,6 +436,8 @@
         copies[-1].start()
 
     for i in range(half):
+        if i + lead < half - 1:
+            pack_row(i + lead)
         f, f_side = fluid_ref[i + 1], fluid_side_ref[i + 1]
         shares = [
             share(f, jnp.where(lon == 3, f_side, lon_next(f))),
@@ -528,6 +503,37 @@
             if i in (0, half - 1):
                 both_ends[c, i] = both
         send(i)
+    outer = pack(shape.has_low * jnp.exp(-low_ref[4]), shape.has_high * jnp.exp(-high_ref[4]))
+    inner = jnp.where(lower, fluid_ref[1], fluid_ref[half])
+    ring_shares = [
+        safe_share(ring, jnp.where(lon == 3, ring_side, lon_next(ring))),
+        safe_share(ring, jnp.where(lon == 0, ring_side, lon_prev(ring))),
+        safe_share(ring, north_of(ring)),
+        safe_share(ring, south_of(ring)),
+        safe_share(ring, outer),
+        safe_share(ring, inner),
+    ]
+    ring_coefficients = coefficients(
+        ring,
+        ring_shares,
+        jnp.where(lower, shape.step(-1), shape.step(half)),
+        jnp.where(lower, shape.step(-2), shape.step(half + 1)),
+        jnp.where(lower, shape.step(0), shape.step(half - 1)),
+    )
+    for n in range(5):
+        out_ref[half, RING + n] = ring_coefficients[n]
+    ring_both = []
+    for c in range(3):
+        s, s_side = ring_field[c], ring_field_side[c]
+        others = [
+            jnp.where(lon == 3, s_side, lon_next(s)),
+            jnp.where(lon == 0, s_side, lon_prev(s)),
+            lat_next(s),
+            lat_prev(s),
+            pack(low_ref[5 + c], high_ref[5 + c]),
+            jnp.where(lower, field_ref[c, 1], field_ref[c, half]),
+        ]
+        ring_both.append(s + relaxed(ring, ring_shares, s, others))
     low_step = shape.step(0) - shape.step(-1)
     high_step = shape.step(half) - shape.step(half - 1)
     for c in range(3):
@@ -546,10 +552,13 @@
         copy.wait()
 
 
+AHEAD = 8
+
+
 def gradient_kernel(
     v_ref, pred_ref, data_ref, k_high_ref, k_low_ref, blocks_ref,
-    new_ref, half_ref, misfit_ref, sa_ref, d_ref, in_ref, e_ref, side_ref, north_ref, product_ref,
-    total_ref, sems, *, scale, rad_n,
+    new_ref, half_ref, misfit_ref, v_in_ref, new_out_ref, half_out_ref, sa_ref, d_ref, in_ref, e_ref, side_ref, north_ref, product_ref,
+    total_ref, k_low_in_ref, sems, out_sems, *, scale, rad_n,
 ):
     nr, nl, width = v_ref.shape
     shape = Shape(nr, width, rad_n)
@@ -559,9 +568,22 @@
     copies = [
         pltpu.make_async_copy(blocks_ref.at[i], in_ref.at[i], sems.at[i]) for i in range(half + 1)
     ]
+    low_copy = pltpu.make_async_copy(k_low_ref, k_low_in_ref, sems.at[half + 1])
+    low_copy.start()
     copies[half].start()
-    for i in range(half):
+    for i in range(min(AHEAD, half)):
         copies[i].start()
+    v_copy = pltpu.make_async_copy(v_ref, v_in_ref, sems.at[half + 2])
+    v_copy.start()
+    groups = []
+    for first in range(0, half, 6):
+        group = []
+        for at in (first, first + half):
+            for inner, outer in ((half_out_ref, half_ref), (new_out_ref, new_ref)):
+                rows = slice(at, at + min(6, half - first))
+                sem = out_sems.at[4 * len(groups) + len(group)]
+                group.append(pltpu.make_async_copy(inner.at[rows], outer.at[rows], sem))
+        groups.append(group)
     ends_ref = in_ref.at[half]
 
     flat = pred_ref[0]
@@ -577,7 +599,9 @@
     pulled = (weight * weighted) * scale
     pulled = jnp.concatenate([pulled, jnp.zeros((5, sites), F32)], axis=0)
     for col in range(COLS):
-        spread = product(pulled, k_high_ref[col], k_low_ref[col], 0)
+        if col == 0:
+            low_copy.wait()
+        spread = product(pulled, k_high_ref[col], k_low_in_ref[col], 0)
         for c in range(3):
             sa_ref[c, col : col + 1, :] = spread[c : c + 1, :]
 
@@ -624,7 +648,15 @@
         return [scaled * x for x in change(coeffs, 0)]
 
     def first_pass(i):
-        copies[i].wait()
+        if i % 2 == 0:
+
+            @pl.when(lax.axis_index("rad") >= 0)
+            def _():
+                for n in range(i, min(i + 2, half)):
+                    copies[n].wait()
+                    if n + AHEAD < half:
+                        copies[n + AHEAD].start()
+
         e = own_change(in_ref.at[i], SHARE, in_ref[i, FLUID], i)
         side = change([in_ref[i, SIDE + n] for n in range(5)], 5)
         for c in range(3):
@@ -677,10 +709,10 @@
         share = in_ref[i, SHARE + 3]
         total = total_ref[i] + (share * share) * product_ref[i]
         total = in_ref[i, BASE] - RELAX_RATE * (in_ref[i, FLUID] * total)
-        half_ref[i] = total[0:4, :]
-        half_ref[i + half] = total[4:8, :]
-        new_ref[i] = v_ref[i] + total[0:4, :]
-        new_ref[i + half] = v_ref[i + half] + total[4:8, :]
+        half_out_ref[i] = total[0:4, :]
+        half_out_ref[i + half] = total[4:8, :]
+        new_out_ref[i] = v_in_ref[i] + total[0:4, :]
+        new_out_ref[i + half] = v_in_ref[i + half] + total[4:8, :]
 
     copies[half].wait()
     ring = change([ends_ref[RING + n] for n in range(5)], 0)
@@ -697,9 +729,25 @@
         if i + lead < half:
             first_pass(i + lead)
         p_down = second_pass(i, p_down)
+        if i == 1:
+            v_copy.wait()
         if i > 0:
             third_pass(i - 1)
+        if i % 6 == 0 and i > 0:
+
+            @pl.when(lax.axis_index("rad") >= 0)
+            def _():
+                for copy in groups[i // 6 - 1]:
+                    copy.start()
+
+    if half == 1:
+        v_copy.wait()
     third_pass(half - 1)
+    for copy in groups[-1]:
+        copy.start()
+    for group in groups:
+        for copy in group:
+            copy.wait()
 
 
 def call(
@@ -767,23 +815,18 @@
     westward = [(t, s) for s, t in eastward]
     column, layers = (4 * nr, 1, nlat), (8, nl, nlat)
     first_column = (4 * nr + ice_history.shape[0], 1, nlat)
-    (packets,) = call(
-        packet_kernel,
-        [((lon_n, 8, own_sites), F32)],
-        "vvv",
-        name="packet",
-        flops=575000000,
-        far_in=(0, 1, 2),
-    )(site_cells[None], observed, site_weight)
-    gathered = lax.all_to_all(packets, "lon", 0, 0)
-    to_west, to_east, to_west2, to_east2, to_low, to_high = call(
+    to_west, to_east, to_west2, to_east2, to_low, to_high, packets = call(
         functools.partial(message_kernel, rad_n=rad_n),
-        [(shape, F32) for shape in [first_column] * 2 + [column] * 2 + [layers] * 2],
-        "vvv",
+        [
+            (shape, F32)
+            for shape in [first_column] * 2 + [column] * 2 + [layers] * 2 + [(lon_n, 8, own_sites)]
+        ],
+        "vvvvvv",
         name="messages",
         flops=2875000000,
-        far_in=(0, 1, 2),
-    )(logvisc, displacement, ice_history)
+        far_in=(0, 1, 2, 3, 4, 5),
+    )(logvisc, displacement, ice_history, site_cells[None], observed, site_weight)
+    gathered = lax.all_to_all(packets, "lon", 0, 0)
     west = lax.ppermute(to_east, "lon", eastward)
     east = lax.ppermute(to_west, "lon", westward)
     low, high = across_rad(to_low, to_high)
@@ -840,17 +883,23 @@
     new_logvisc, half_momentum, misfit = call(
         functools.partial(gradient_kernel, scale=scale, rad_n=rad_n),
         [((nr, nl, nlat), F32), ((nr, nl, nlat), F32), ((1, 1), F32)],
-        "vvvvvh",
-        scratch=[
+        "hvvvhh",
+        scratch=[pltpu.VMEM((nr, nl, nlat), F32)] * 3
+        + [
             pltpu.VMEM(shape + row, F32)
             for shape in [(3,), (10, 3), (half + 1, BLOCK), (3, half), (3, half), (9, half)]
             + [(half,)] * 2
         ]
-        + [pltpu.SemaphoreType.DMA((half + 1,))],
+        + [
+            pltpu.VMEM((COLS, sites, nlat), BF16),
+            pltpu.SemaphoreType.DMA((half + 3,)),
+            pltpu.SemaphoreType.DMA((4 * -(-half // 6),)),
+        ],
         name="gradient",
         flops=6900000000,
-        held_in=(2, 3, 4),
-        far_in=(0, 5),
+        held_in=(2, 3),
+        far_in=(0, 4, 5),
+        far_out=(0, 1),
     )(logvisc, predicted, data, k_high, k_low, blocks)
     return (new_logvisc, half_momentum, misfit.reshape(1))
 

time: 54.4 us -> 53.2 us (0.978)
  Pallas kernels: 30.6 us -> 26.5 us
  starting transfers between devices: 20.4 us -> 24 us
  local copies, waits for them, and re-layouts: 1.42 us -> 0.02 us
  waiting for transfers between devices: 0.66 us -> 1.36 us
    pallas_call x6 -> x5, Pallas kernels: 30.6 us -> 26.5 us  [run(): made(*[pltpu.with_memory_space_constraint(a, pltpu.VMEM if n in held_in e...]
    all_to_all x1, starting transfers between devices: 2.75 us -> 6.41 us  [body(): predicted = lax.all_to_all(partial, ('lon', 'rad'), 0, 0)]
    unnamed x10 -> x8, local copies, waits for them, and re-layouts: 1.42 us -> 0.02 us
    all_to_all x1, waiting for transfers between devices: 0.01 us -> 0.71 us  [body(): predicted = lax.all_to_all(partial, ('lon', 'rad'), 0, 0)]
  transfers between devices with their start and end apart: 8 -> 8, of which waited for: 1 -> 2; matrix products, arithmetic and copies ran while one was open for 0% -> 0% of each run, Pallas kernels for 38% -> 31%
where the time goes in v4:
time: 53.2 us; the launch traced here: 52.8 us
  Pallas kernels  26.5 us (50%)
  starting transfers between devices  24 us (45%)
  waiting for transfers between devices  1.36 us (3%)
  between operations  0.91 us (2%)
    pallas_call x5, Pallas kernels, run(): made(*[pltpu.with_memory_space_constraint(a, pltpu.VMEM if n in held_in e...  26.5 us
    all_to_all x1, starting transfers between devices, body(): predicted = lax.all_to_all(partial, ('lon', 'rad'), 0, 0)  6.41 us
    ppermute x1, starting transfers between devices, body(): east = lax.ppermute(to_west, 'lon', westward)  4.99 us
    ppermute x1, starting transfers between devices, body(): east2 = lax.ppermute(to_west2, 'lon', westward)  4.44 us
    ppermute x2, starting transfers between devices, across_rad(): both = lax.ppermute(down, 'rad', [(0, 1), (1, 0)])  4.06 us
    all_to_all x1, starting transfers between devices, body(): gathered = lax.all_to_all(packets, 'lon', 0, 0)  3.68 us
  transfers between devices with their start and end apart: 8, of which 2 were waited for; matrix products, arithmetic and copies ran while one was open for 0% of the time, Pallas kernels for 31%

profile of v4, /device:TPU:0, one launch (start us, length us, event | category | flops | bytes accessed | tf_op | source)
XLA Modules:
  0.0 52.8 jit_solution(15192224388071566028)
XLA Ops:
  0.6 2.3 %messages.1 = (f32[200,1,512]{2,1,0:T(1,128)S(1)}, f32[200,1,512]{2,1,0:T(1,128)S(1)}, f32[192,1,512]{2,1,0:T(1,128)S(1)}, f32[192,1,512]{2,1,0:T(1,128)S(1)}, f...) custom-call(f32[48,4,512]{2,1,0:T(4,128)} %v_ref.7, f32[3,48,4,512]{3,2,1,0:T(4,128)} %s_ref.5, ...), custom_call_target="tpu_custom_call" | custom-call | flops 2875000064 | bytes 1048576 | tf_op jit(solution)/shard_map/messages/pallas_call | solution.py:780
  3.0 0.5 collective-permute-start
  3.4 5.0 %collective-permute-start.1 = (f32[200,1,512]{2,1,0:T(1,128)S(1)}, f32[200,1,512]{2,1,0:T(1,128)S(1)}, u32[]{:S(2)}, u32[]{:S(2)}) collective-permute-start(f32[200,1,512]{2,1,0:T(1,128)S(1)} %get-tuple-element.18), channel_id=1, source_target_pairs={{2,0},{4,2},{6,4},{8,6},{10,8},{12,10},{14,12},{16,14},{18,16},{20... | collective-permute-start | bytes 1228808 | tf_op jit(solution)/shard_map/ppermute | solution.py:831
  8.4 3.7 %all-to-all-start = ((f32[16,8,12]{2,1,0:T(8,128)}), f32[16,8,12]{2,1,0:T(8,128)S(1)}, u32[]{:S(2)}, u32[]{:S(2)}) async-start(f32[16,8,12]{2,1,0:T(8,128)} %get-tuple-element.20), calls=%async_computation | async-start | bytes 131072 | tf_op jit(solution)/shard_map/all_to_all | solution.py:829
  12.1 1.8 %collective-permute-start.2 = (f32[8,4,512]{2,1,0:T(4,128)S(1)}, f32[8,4,512]{2,1,0:T(4,128)S(1)}, u32[]{:S(2)}, u32[]{:S(2)}) collective-permute-start(f32[8,4,512]{2,1,0:T(4,128)S(1)} %get-tuple-element.19), channel_id=1, source_target_pairs={{0,1},{1,0},{2,3},{3,2},{4,5},{5,4},{6,7},{7,6},{8,9},{9,8},{10,11... | collective-permute-start | bytes 196616 | tf_op jit(solution)/shard_map/ppermute | solution.py:808
  13.9 0.0 collective-permute-start.3
  13.9 0.0 copy-start
  13.9 4.4 %collective-permute-start.4 = (f32[192,1,512]{2,1,0:T(1,128)S(1)}, f32[192,1,512]{2,1,0:T(1,128)S(1)}, u32[]{:S(2)}, u32[]{:S(2)}) collective-permute-start(f32[192,1,512]{2,1,0:T(1,128)S(1)} %get-tuple-element.26), channel_id=1, source_target_pairs={{2,0},{4,2},{6,4},{8,6},{10,8},{12,10},{14,12},{16,14},{18,16},{20... | collective-permute-start | bytes 1179656 | tf_op jit(solution)/shard_map/ppermute | solution.py:834
  18.4 0.6 %all-to-all-done.gathered_ref = f32[16,8,12]{2,1,0:T(8,128)S(1)} async-done(((f32[16,8,12]{2,1,0:T(8,128)}), f32[16,8,12]{2,1,0:T(8,128)S(1)}, u32[]{:S(2)}, u32[]{:S(2)}) %all-to-all-start) | async-done | bytes 6176 | tf_op jit(solution)/shard_map/all_to_all | solution.py:829
  19.0 3.1 %site_weights.1 = (bf16[8,192,512]{2,1,0:T(8,128)(2,1)S(1)}, bf16[8,192,512]{2,1,0:T(8,128)(2,1)S(1)}, f32[8,192]{1,0:T(8,128)S(1)}) custom-call(f32[16,8,12]{2,1,0:T(8,128)S(1)} %all-to-all-done.gathered_ref), custom_call_target="tpu_custom_call" | custom-call | flops 3680000000 | bytes 1048576 | tf_op jit(solution)/shard_map/site_weights/pallas_call | solution.py:780
  22.1 0.0 copy-start.1
  22.1 0.0 copy-start.3
  22.1 0.0 collective-permute-done.2.low_ref.high_ref
  22.1 0.0 collective-permute-done.west_ref
  22.2 0.0 collective-permute-done.1.east_ref
  22.2 0.0 copy-done
  22.2 6.4 %forward.1 = (f32[32,1,640]{2,1,0:T(1,128)}, f32[8,1,512]{2,1,0:T(1,128)}, f32[8,1,512]{2,1,0:T(1,128)}) custom-call(s32[2]{0:T(128)S(1)} %copy-done, f32[48,4,512]{2,1,0:T(4,128)} %v_ref.7, f32[3,48,4,512]{3,2,1,0:T(4,128)} %s_ref.5, f32[200,1,512]{2,1,0:T(1,128)S(1)} %collective-permute-done.west_ref, f32[200,1,512]{2,1,0:T(1,128)S(1)} %collective-permute-done.1.east_ref, ...), custom_call_target="tpu_custom_call" | custom-call | flops 6325000192 | bytes 1048576 | tf_op jit(solution)/shard_map/forward/pallas_call | solution.py:780
  28.6 0.0 copy-done.1
  28.6 0.0 copy-done.3
  28.6 2.2 %collective-permute-start.5 = (f32[8,1,512]{2,1,0:T(1,128)}, f32[8,1,512]{2,1,0:T(1,128)S(1)}, u32[]{:S(2)}, u32[]{:S(2)}) collective-permute-start(f32[8,1,512]{2,1,0:T(1,128)} %get-tuple-element.27), channel_id=1, source_target_pairs={{0,1},{1,0},{2,3},{3,2},{4,5},{5,4},{6,7},{7,6},{8,9},{9,8},{10,11... | collective-permute-start | bytes 49160 | tf_op jit(solution)/shard_map/ppermute | solution.py:808
  30.8 6.4 %all-to-all-start.1 = ((f32[32,1,640]{2,1,0:T(1,128)}), f32[32,1,640]{2,1,0:T(1,128)S(1)}, u32[]{:S(2)}, u32[]{:S(2)}) async-start(f32[32,1,640]{2,1,0:T(1,128)} %get-tuple-element.23), calls=%async_computation.1 | async-start | bytes 163840 | tf_op jit(solution)/shard_map/all_to_all | solution.py:862
  37.2 0.0 collective-permute-done.3.west2_ref
  37.3 0.0 collective-permute-done.4.east2_ref
  37.3 0.0 copy-start.2
  37.3 0.0 collective-permute-done.5.corner_low_ref.corner_high_ref
  37.3 6.9 %prepare.1.blocks_ref = f32[25,25,8,512]{3,2,1,0:T(8,128)} custom-call(s32[2]{0:T(128)S(1)} %copy-done, f32[48,4,512]{2,1,0:T(4,128)} %v_ref.7, f32[48,4,512]{2,1,0:T(4,128)} %m_ref.1, f32[3,48,4,512]{3,2,1,0:T(4,128)} %s_ref.5, f32[8,4,512]{2,1,0:T(4,128)} %ice_ref.5, f32[200,1,512]{2,1,0:T(1,128)S(1)} %collective-permute-done.west_ref, ...), custom_call_target="tpu_custom_call" | custom-call | flops 8049999872 | bytes 1048576 | tf_op jit(solution)/shard_map/prepare/pallas_call | solution.py:780
  44.2 0.7 %all-to-all-done.1.pred_ref = f32[32,1,640]{2,1,0:T(1,128)S(1)} async-done(((f32[32,1,640]{2,1,0:T(1,128)}), f32[32,1,640]{2,1,0:T(1,128)S(1)}, u32[]{:S(2)}, u32[]{:S(2)}) %all-to-all-start.1) | async-done | bytes 81952 | tf_op jit(solution)/shard_map/all_to_all | solution.py:862
  44.9 0.0 copy-done.2
  44.9 7.7 %gradient.1 = (f32[48,4,512]{2,1,0:T(4,128)}, f32[48,4,512]{2,1,0:T(4,128)}, f32[1,1]{1,0:T(1,128)}) custom-call(f32[48,4,512]{2,1,0:T(4,128)} %v_ref.7, f32[32,1,640]{2,1,0:T(1,128)S(1)} %all-to-all-done.1.pred_ref, f32[8,192]{1,0:T(8,128)S(1)} %get-tuple-element.24.data_ref, bf16[8,192,512]{2,1,0:T(8,128)(2,1)S(1)} %copy-done.2, ...), custom_call_target="tpu_custom_call" | custom-call | flops 6899999744 | bytes 1048576 | tf_op jit(solution)/shard_map/gradient/pallas_call | solution.py:780
Async XLA Ops:
  3.0 19.2 %collective-permute-start = (f32[200,1,512]{2,1,0:T(1,128)S(1)}, f32[200,1,512]{2,1,0:T(1,128)S(1)}, u32[]{:S(2)}, u32[]{:S(2)}) collective-permute-start(f32[200,1,512]{2,1,0:T(1,128)S(1)} %get-tuple-element.17), channel_id=1, source_target_pairs={{0,2},{2,4},{4,6},{6,8},{8,10},{10,12},{12,14},{14,16},{16,18},{18... | collective-permute-start | bytes 1228808 | tf_op jit(solution)/shard_map/ppermute | solution.py:830
  3.4 18.8 %collective-permute-start.1 = (f32[200,1,512]{2,1,0:T(1,128)S(1)}, f32[200,1,512]{2,1,0:T(1,128)S(1)}, u32[]{:S(2)}, u32[]{:S(2)}) collective-permute-start(f32[200,1,512]{2,1,0:T(1,128)S(1)} %get-tuple-element.18), channel_id=1, source_target_pairs={{2,0},{4,2},{6,4},{8,6},{10,8},{12,10},{14,12},{16,14},{18,16},{20... | collective-permute-start | bytes 1228808 | tf_op jit(solution)/shard_map/ppermute | solution.py:831
  8.4 10.6 %all-to-all-start = ((f32[16,8,12]{2,1,0:T(8,128)}), f32[16,8,12]{2,1,0:T(8,128)S(1)}, u32[]{:S(2)}, u32[]{:S(2)}) async-start(f32[16,8,12]{2,1,0:T(8,128)} %get-tuple-element.20), calls=%async_computation | async-start | bytes 131072 | tf_op jit(solution)/shard_map/all_to_all | solution.py:829
  12.1 10.0 %collective-permute-start.2 = (f32[8,4,512]{2,1,0:T(4,128)S(1)}, f32[8,4,512]{2,1,0:T(4,128)S(1)}, u32[]{:S(2)}, u32[]{:S(2)}) collective-permute-start(f32[8,4,512]{2,1,0:T(4,128)S(1)} %get-tuple-element.19), channel_id=1, source_target_pairs={{0,1},{1,0},{2,3},{3,2},{4,5},{5,4},{6,7},{7,6},{8,9},{9,8},{10,11... | collective-permute-start | bytes 196616 | tf_op jit(solution)/shard_map/ppermute | solution.py:808
  13.9 23.3 %collective-permute-start.3 = (f32[192,1,512]{2,1,0:T(1,128)S(1)}, f32[192,1,512]{2,1,0:T(1,128)S(1)}, u32[]{:S(2)}, u32[]{:S(2)}) collective-permute-start(f32[192,1,512]{2,1,0:T(1,128)S(1)} %get-tuple-element.25), channel_id=1, source_target_pairs={{0,2},{2,4},{4,6},{6,8},{8,10},{10,12},{12,14},{14,16},{16,18},{18... | collective-permute-start | bytes 1179656 | tf_op jit(solution)/shard_map/ppermute | solution.py:833
  13.9 8.3 %copy-start = (s32[2]{0:T(128)S(1)}, s32[2]{0:T(128)}, u32[]{:S(2)}) copy-start(s32[2]{0:T(128)} %steps_ref.3) | copy-start | bytes 28
  13.9 23.3 %collective-permute-start.4 = (f32[192,1,512]{2,1,0:T(1,128)S(1)}, f32[192,1,512]{2,1,0:T(1,128)S(1)}, u32[]{:S(2)}, u32[]{:S(2)}) collective-permute-start(f32[192,1,512]{2,1,0:T(1,128)S(1)} %get-tuple-element.26), channel_id=1, source_target_pairs={{2,0},{4,2},{6,4},{8,6},{10,8},{12,10},{14,12},{16,14},{18,16},{20... | collective-permute-start | bytes 1179656 | tf_op jit(solution)/shard_map/ppermute | solution.py:834
  22.1 6.5 %copy-start.1 = (bf16[8,192,512]{2,1,0:T(8,128)(2,1)}, bf16[8,192,512]{2,1,0:T(8,128)(2,1)S(1)}, u32[]{:S(2)}) copy-start(bf16[8,192,512]{2,1,0:T(8,128)(2,1)S(1)} %get-tuple-element.21.k_high_ref) | copy-start | bytes 4718596
  22.1 6.5 %copy-start.3 = (bf16[8,192,512]{2,1,0:T(8,128)(2,1)}, bf16[8,192,512]{2,1,0:T(8,128)(2,1)S(1)}, u32[]{:S(2)}) copy-start(bf16[8,192,512]{2,1,0:T(8,128)(2,1)S(1)} %get-tuple-element.22.k_low_ref) | copy-start | bytes 4718596
  28.6 8.7 %collective-permute-start.5 = (f32[8,1,512]{2,1,0:T(1,128)}, f32[8,1,512]{2,1,0:T(1,128)S(1)}, u32[]{:S(2)}, u32[]{:S(2)}) collective-permute-start(f32[8,1,512]{2,1,0:T(1,128)} %get-tuple-element.27), channel_id=1, source_target_pairs={{0,1},{1,0},{2,3},{3,2},{4,5},{5,4},{6,7},{7,6},{8,9},{9,8},{10,11... | collective-permute-start | bytes 49160 | tf_op jit(solution)/shard_map/ppermute | solution.py:808
  30.8 14.1 %all-to-all-start.1 = ((f32[32,1,640]{2,1,0:T(1,128)}), f32[32,1,640]{2,1,0:T(1,128)S(1)}, u32[]{:S(2)}, u32[]{:S(2)}) async-start(f32[32,1,640]{2,1,0:T(1,128)} %get-tuple-element.23), calls=%async_computation.1 | async-start | bytes 163840 | tf_op jit(solution)/shard_map/all_to_all | solution.py:862
  37.3 7.7 %copy-start.2 = (bf16[8,192,512]{2,1,0:T(8,128)(2,1)S(1)}, bf16[8,192,512]{2,1,0:T(8,128)(2,1)}, u32[]{:S(2)}) copy-start(bf16[8,192,512]{2,1,0:T(8,128)(2,1)} %copy-done.1) | copy-start | bytes 4718596

commit v5 on v4

--- a/solution.py
+++ b/solution.py
@@ -103,15 +103,9 @@
     west_ref, east_ref, west2_ref, east2_ref, low_ref, high_ref, packet_ref, *, rad_n,
 ):
     nr, nl, width = v_ref.shape
-    packet = jnp.concatenate(
-        [
-            cells_ref[...].astype(F32),
-            obs_ref[...],
-            wt_ref[...],
-            jnp.zeros((1, obs_ref.shape[1]), F32),
-        ],
-        axis=0,
-    )
+    parts = [cells_ref[...].astype(F32)]
+    parts += [ref[c : c + 1, :] for ref in (obs_ref, wt_ref) for c in range(3)]
+    packet = jnp.concatenate(parts, axis=1)
     for n in range(packet_ref.shape[0]):
         packet_ref[n] = packet
 
@@ -143,10 +137,14 @@
 
 def weights_kernel(gathered_ref, high_ref, low_ref, data_ref, rows_ref, *, total_lon):
     devices, _, own = gathered_ref.shape
+    own = own // 7
     sites = high_ref.shape[1]
     width = high_ref.shape[2]
     for d in range(devices):
-        data_ref[:, d * own : (d + 1) * own] = gathered_ref[d]
+        packet = gathered_ref[d]
+        for k in range(7):
+            data_ref[k : k + 1, d * own : (d + 1) * own] = packet[:, k * own : (k + 1) * own]
+    data_ref[7:8, :] = jnp.zeros((1, sites), F32)
     cells = data_ref[0:1, :]
     lon = jnp.floor((cells + 0.5) * (1.0 / width))
     theta = (cells - lon * width + 0.5) * (1.0 / width)
@@ -819,7 +817,7 @@
         functools.partial(message_kernel, rad_n=rad_n),
         [
             (shape, F32)
-            for shape in [first_column] * 2 + [column] * 2 + [layers] * 2 + [(lon_n, 8, own_sites)]
+            for shape in [first_column] * 2 + [column] * 2 + [layers] * 2 + [(lon_n, 1, 7 * own_sites)]
         ],
         "vvvvvv",
         name="messages",

time: 53.2 us -> 52.7 us (level)
  waiting for transfers between devices: 1.36 us -> 0.82 us
    all_to_all x1, waiting for transfers between devices: 0.64 us -> 0.1 us  [body(): gathered = lax.all_to_all(packets, 'lon', 0, 0)]
  transfers between devices with their start and end apart: 8 -> 8, of which waited for: 2 -> 2; matrix products, arithmetic and copies ran while one was open for 0% -> 0% of each run, Pallas kernels for 31% -> 32%
where the time goes in v5:
time: 52.7 us; the launch traced here: 52.4 us
  Pallas kernels  26.6 us (50%)
  starting transfers between devices  24 us (46%)
  between operations  0.91 us (2%)
  waiting for transfers between devices  0.82 us (2%)
    pallas_call x5, Pallas kernels, run(): made(*[pltpu.with_memory_space_constraint(a, pltpu.VMEM if n in held_in e...  26.6 us
    all_to_all x1, starting transfers between devices, body(): predicted = lax.all_to_all(partial, ('lon', 'rad'), 0, 0)  6.75 us
    ppermute x1, starting transfers between devices, body(): east = lax.ppermute(to_west, 'lon', westward)  4.99 us
    ppermute x1, starting transfers between devices, body(): east2 = lax.ppermute(to_west2, 'lon', westward)  4.44 us
    all_to_all x1, starting transfers between devices, body(): gathered = lax.all_to_all(packets, 'lon', 0, 0)  3.68 us
    ppermute x2, starting transfers between devices, across_rad(): both = lax.ppermute(down, 'rad', [(0, 1), (1, 0)])  3.65 us
  transfers between devices with their start and end apart: 8, of which 2 were waited for; matrix products, arithmetic and copies ran while one was open for 0% of the time, Pallas kernels for 32%

profile of v5, /device:TPU:0, one launch (start us, length us, event | category | flops | bytes accessed | tf_op | source)
XLA Modules:
  0.0 52.4 jit_solution(15871495192330903632)
XLA Ops:
  0.6 2.4 %messages.1 = (f32[200,1,512]{2,1,0:T(1,128)S(1)}, f32[200,1,512]{2,1,0:T(1,128)S(1)}, f32[192,1,512]{2,1,0:T(1,128)S(1)}, f32[192,1,512]{2,1,0:T(1,128)S(1)}, f...) custom-call(f32[48,4,512]{2,1,0:T(4,128)} %v_ref.7, f32[3,48,4,512]{3,2,1,0:T(4,128)} %s_ref.5, ...), custom_call_target="tpu_custom_call" | custom-call | flops 2875000064 | bytes 1048576 | tf_op jit(solution)/shard_map/messages/pallas_call | solution.py:778
  3.0 0.5 collective-permute-start
  3.5 5.0 %collective-permute-start.1 = (f32[200,1,512]{2,1,0:T(1,128)S(1)}, f32[200,1,512]{2,1,0:T(1,128)S(1)}, u32[]{:S(2)}, u32[]{:S(2)}) collective-permute-start(f32[200,1,512]{2,1,0:T(1,128)S(1)} %get-tuple-element.18), channel_id=1, source_target_pairs={{2,0},{4,2},{6,4},{8,6},{10,8},{12,10},{14,12},{16,14},{18,16},{20... | collective-permute-start | bytes 1228808 | tf_op jit(solution)/shard_map/ppermute | solution.py:829
  8.5 3.7 %all-to-all-start = ((f32[16,1,84]{2,1,0:T(1,128)}), f32[16,1,84]{2,1,0:T(1,128)S(1)}, u32[]{:S(2)}, u32[]{:S(2)}) async-start(f32[16,1,84]{2,1,0:T(1,128)} %get-tuple-element.20), calls=%async_computation | async-start | bytes 16384 | tf_op jit(solution)/shard_map/all_to_all | solution.py:827
  12.1 1.8 %collective-permute-start.2 = (f32[8,4,512]{2,1,0:T(4,128)S(1)}, f32[8,4,512]{2,1,0:T(4,128)S(1)}, u32[]{:S(2)}, u32[]{:S(2)}) collective-permute-start(f32[8,4,512]{2,1,0:T(4,128)S(1)} %get-tuple-element.19), channel_id=1, source_target_pairs={{0,1},{1,0},{2,3},{3,2},{4,5},{5,4},{6,7},{7,6},{8,9},{9,8},{10,11... | collective-permute-start | bytes 196616 | tf_op jit(solution)/shard_map/ppermute | solution.py:806
  13.9 0.0 collective-permute-start.3
  13.9 0.0 copy-start
  13.9 4.4 %collective-permute-start.4 = (f32[192,1,512]{2,1,0:T(1,128)S(1)}, f32[192,1,512]{2,1,0:T(1,128)S(1)}, u32[]{:S(2)}, u32[]{:S(2)}) collective-permute-start(f32[192,1,512]{2,1,0:T(1,128)S(1)} %get-tuple-element.26), channel_id=1, source_target_pairs={{2,0},{4,2},{6,4},{8,6},{10,8},{12,10},{14,12},{16,14},{18,16},{20... | collective-permute-start | bytes 1179656 | tf_op jit(solution)/shard_map/ppermute | solution.py:832
  18.4 0.1 all-to-all-done.gathered_ref
  18.5 3.2 %site_weights.1 = (bf16[8,192,512]{2,1,0:T(8,128)(2,1)S(1)}, bf16[8,192,512]{2,1,0:T(8,128)(2,1)S(1)}, f32[8,192]{1,0:T(8,128)S(1)}) custom-call(f32[16,1,84]{2,1,0:T(1,128)S(1)} %all-to-all-done.gathered_ref), custom_call_target="tpu_custom_call" | custom-call | flops 3680000000 | bytes 1048576 | tf_op jit(solution)/shard_map/site_weights/pallas_call | solution.py:778
  21.7 0.0 copy-start.1
  21.7 0.0 copy-start.3
  21.7 0.0 collective-permute-done.2.low_ref.high_ref
  21.7 0.0 collective-permute-done.west_ref
  21.7 0.0 collective-permute-done.1.east_ref
  21.7 0.0 copy-done
  21.8 6.4 %forward.1 = (f32[32,1,640]{2,1,0:T(1,128)}, f32[8,1,512]{2,1,0:T(1,128)}, f32[8,1,512]{2,1,0:T(1,128)}) custom-call(s32[2]{0:T(128)S(1)} %copy-done, f32[48,4,512]{2,1,0:T(4,128)} %v_ref.7, f32[3,48,4,512]{3,2,1,0:T(4,128)} %s_ref.5, f32[200,1,512]{2,1,0:T(1,128)S(1)} %collective-permute-done.west_ref, f32[200,1,512]{2,1,0:T(1,128)S(1)} %collective-permute-done.1.east_ref, ...), custom_call_target="tpu_custom_call" | custom-call | flops 6325000192 | bytes 1048576 | tf_op jit(solution)/shard_map/forward/pallas_call | solution.py:778
  28.2 0.0 copy-done.1
  28.2 0.0 copy-done.3
  28.2 1.9 %collective-permute-start.5 = (f32[8,1,512]{2,1,0:T(1,128)}, f32[8,1,512]{2,1,0:T(1,128)S(1)}, u32[]{:S(2)}, u32[]{:S(2)}) collective-permute-start(f32[8,1,512]{2,1,0:T(1,128)} %get-tuple-element.27), channel_id=1, source_target_pairs={{0,1},{1,0},{2,3},{3,2},{4,5},{5,4},{6,7},{7,6},{8,9},{9,8},{10,11... | collective-permute-start | bytes 49160 | tf_op jit(solution)/shard_map/ppermute | solution.py:806
  30.0 6.7 %all-to-all-start.1 = ((f32[32,1,640]{2,1,0:T(1,128)}), f32[32,1,640]{2,1,0:T(1,128)S(1)}, u32[]{:S(2)}, u32[]{:S(2)}) async-start(f32[32,1,640]{2,1,0:T(1,128)} %get-tuple-element.23), calls=%async_computation.1 | async-start | bytes 163840 | tf_op jit(solution)/shard_map/all_to_all | solution.py:860
  36.8 0.0 collective-permute-done.3.west2_ref
  36.8 0.0 collective-permute-done.4.east2_ref
  36.8 0.0 copy-start.2
  36.8 0.0 collective-permute-done.5.corner_low_ref.corner_high_ref
  36.8 6.9 %prepare.1.blocks_ref = f32[25,25,8,512]{3,2,1,0:T(8,128)} custom-call(s32[2]{0:T(128)S(1)} %copy-done, f32[48,4,512]{2,1,0:T(4,128)} %v_ref.7, f32[48,4,512]{2,1,0:T(4,128)} %m_ref.1, f32[3,48,4,512]{3,2,1,0:T(4,128)} %s_ref.5, f32[8,4,512]{2,1,0:T(4,128)} %ice_ref.5, f32[200,1,512]{2,1,0:T(1,128)S(1)} %collective-permute-done.west_ref, ...), custom_call_target="tpu_custom_call" | custom-call | flops 8049999872 | bytes 1048576 | tf_op jit(solution)/shard_map/prepare/pallas_call | solution.py:778
  43.7 0.7 %all-to-all-done.1.pred_ref = f32[32,1,640]{2,1,0:T(1,128)S(1)} async-done(((f32[32,1,640]{2,1,0:T(1,128)}), f32[32,1,640]{2,1,0:T(1,128)S(1)}, u32[]{:S(2)}, u32[]{:S(2)}) %all-to-all-start.1) | async-done | bytes 81952 | tf_op jit(solution)/shard_map/all_to_all | solution.py:860
  44.5 0.0 copy-done.2
  44.5 7.7 %gradient.1 = (f32[48,4,512]{2,1,0:T(4,128)}, f32[48,4,512]{2,1,0:T(4,128)}, f32[1,1]{1,0:T(1,128)}) custom-call(f32[48,4,512]{2,1,0:T(4,128)} %v_ref.7, f32[32,1,640]{2,1,0:T(1,128)S(1)} %all-to-all-done.1.pred_ref, f32[8,192]{1,0:T(8,128)S(1)} %get-tuple-element.24.data_ref, bf16[8,192,512]{2,1,0:T(8,128)(2,1)S(1)} %copy-done.2, ...), custom_call_target="tpu_custom_call" | custom-call | flops 6899999744 | bytes 1048576 | tf_op jit(solution)/shard_map/gradient/pallas_call | solution.py:778
Async XLA Ops:
  3.0 18.7 %collective-permute-start = (f32[200,1,512]{2,1,0:T(1,128)S(1)}, f32[200,1,512]{2,1,0:T(1,128)S(1)}, u32[]{:S(2)}, u32[]{:S(2)}) collective-permute-start(f32[200,1,512]{2,1,0:T(1,128)S(1)} %get-tuple-element.17), channel_id=1, source_target_pairs={{0,2},{2,4},{4,6},{6,8},{8,10},{10,12},{12,14},{14,16},{16,18},{18... | collective-permute-start | bytes 1228808 | tf_op jit(solution)/shard_map/ppermute | solution.py:828
  3.5 18.3 %collective-permute-start.1 = (f32[200,1,512]{2,1,0:T(1,128)S(1)}, f32[200,1,512]{2,1,0:T(1,128)S(1)}, u32[]{:S(2)}, u32[]{:S(2)}) collective-permute-start(f32[200,1,512]{2,1,0:T(1,128)S(1)} %get-tuple-element.18), channel_id=1, source_target_pairs={{2,0},{4,2},{6,4},{8,6},{10,8},{12,10},{14,12},{16,14},{18,16},{20... | collective-permute-start | bytes 1228808 | tf_op jit(solution)/shard_map/ppermute | solution.py:829
  8.5 10.0 %all-to-all-start = ((f32[16,1,84]{2,1,0:T(1,128)}), f32[16,1,84]{2,1,0:T(1,128)S(1)}, u32[]{:S(2)}, u32[]{:S(2)}) async-start(f32[16,1,84]{2,1,0:T(1,128)} %get-tuple-element.20), calls=%async_computation | async-start | bytes 16384 | tf_op jit(solution)/shard_map/all_to_all | solution.py:827
  12.1 9.6 %collective-permute-start.2 = (f32[8,4,512]{2,1,0:T(4,128)S(1)}, f32[8,4,512]{2,1,0:T(4,128)S(1)}, u32[]{:S(2)}, u32[]{:S(2)}) collective-permute-start(f32[8,4,512]{2,1,0:T(4,128)S(1)} %get-tuple-element.19), channel_id=1, source_target_pairs={{0,1},{1,0},{2,3},{3,2},{4,5},{5,4},{6,7},{7,6},{8,9},{9,8},{10,11... | collective-permute-start | bytes 196616 | tf_op jit(solution)/shard_map/ppermute | solution.py:806
  13.9 22.8 %collective-permute-start.3 = (f32[192,1,512]{2,1,0:T(1,128)S(1)}, f32[192,1,512]{2,1,0:T(1,128)S(1)}, u32[]{:S(2)}, u32[]{:S(2)}) collective-permute-start(f32[192,1,512]{2,1,0:T(1,128)S(1)} %get-tuple-element.25), channel_id=1, source_target_pairs={{0,2},{2,4},{4,6},{6,8},{8,10},{10,12},{12,14},{14,16},{16,18},{18... | collective-permute-start | bytes 1179656 | tf_op jit(solution)/shard_map/ppermute | solution.py:831
  13.9 7.8 %copy-start = (s32[2]{0:T(128)S(1)}, s32[2]{0:T(128)}, u32[]{:S(2)}) copy-start(s32[2]{0:T(128)} %steps_ref.3) | copy-start | bytes 28
  13.9 22.9 %collective-permute-start.4 = (f32[192,1,512]{2,1,0:T(1,128)S(1)}, f32[192,1,512]{2,1,0:T(1,128)S(1)}, u32[]{:S(2)}, u32[]{:S(2)}) collective-permute-start(f32[192,1,512]{2,1,0:T(1,128)S(1)} %get-tuple-element.26), channel_id=1, source_target_pairs={{2,0},{4,2},{6,4},{8,6},{10,8},{12,10},{14,12},{16,14},{18,16},{20... | collective-permute-start | bytes 1179656 | tf_op jit(solution)/shard_map/ppermute | solution.py:832
  21.7 6.5 %copy-start.1 = (bf16[8,192,512]{2,1,0:T(8,128)(2,1)}, bf16[8,192,512]{2,1,0:T(8,128)(2,1)S(1)}, u32[]{:S(2)}) copy-start(bf16[8,192,512]{2,1,0:T(8,128)(2,1)S(1)} %get-tuple-element.21.k_high_ref) | copy-start | bytes 4718596
  21.7 6.5 %copy-start.3 = (bf16[8,192,512]{2,1,0:T(8,128)(2,1)}, bf16[8,192,512]{2,1,0:T(8,128)(2,1)S(1)}, u32[]{:S(2)}) copy-start(bf16[8,192,512]{2,1,0:T(8,128)(2,1)S(1)} %get-tuple-element.22.k_low_ref) | copy-start | bytes 4718596
  28.2 8.7 %collective-permute-start.5 = (f32[8,1,512]{2,1,0:T(1,128)}, f32[8,1,512]{2,1,0:T(1,128)S(1)}, u32[]{:S(2)}, u32[]{:S(2)}) collective-permute-start(f32[8,1,512]{2,1,0:T(1,128)} %get-tuple-element.27), channel_id=1, source_target_pairs={{0,1},{1,0},{2,3},{3,2},{4,5},{5,4},{6,7},{7,6},{8,9},{9,8},{10,11... | collective-permute-start | bytes 49160 | tf_op jit(solution)/shard_map/ppermute | solution.py:806
  30.0 14.4 %all-to-all-start.1 = ((f32[32,1,640]{2,1,0:T(1,128)}), f32[32,1,640]{2,1,0:T(1,128)S(1)}, u32[]{:S(2)}, u32[]{:S(2)}) async-start(f32[32,1,640]{2,1,0:T(1,128)} %get-tuple-element.23), calls=%async_computation.1 | async-start | bytes 163840 | tf_op jit(solution)/shard_map/all_to_all | solution.py:860
  36.8 7.7 %copy-start.2 = (bf16[8,192,512]{2,1,0:T(8,128)(2,1)S(1)}, bf16[8,192,512]{2,1,0:T(8,128)(2,1)}, u32[]{:S(2)}) copy-start(bf16[8,192,512]{2,1,0:T(8,128)(2,1)} %copy-done.1) | copy-start | bytes 4718596

commit v6 on v5

--- a/solution.py
+++ b/solution.py
@@ -854,7 +854,7 @@
         name="forward",
         flops=6325000000,
         held_in=(8, 9),
-        far_in=(1, 2, 7),
+        far_in=(7,),
         near_out=(0, 1, 2),
     )(load_steps, logvisc, displacement, west, east, low, high, ice_history, k_high, k_low)
     predicted = lax.all_to_all(partial, ("lon", "rad"), 0, 0)

time: 52.7 us -> 52.1 us (0.989)
  Pallas kernels: 26.6 us -> 25.5 us
  local copies, waits for them, and re-layouts: 0.02 us -> 0.77 us
    pallas_call x5, Pallas kernels: 26.6 us -> 25.5 us  [run(): made(*[pltpu.with_memory_space_constraint(a, pltpu.VMEM if n in held_in e...]
    unnamed x8 -> x14, local copies, waits for them, and re-layouts: 0.02 us -> 0.77 us
  transfers between devices with their start and end apart: 8 -> 8, of which waited for: 2 -> 2; matrix products, arithmetic and copies ran while one was open for 0% -> 0% of each run, Pallas kernels for 32% -> 30%
where the time goes in v6:
time: 52.1 us; the launch traced here: 51.7 us
  Pallas kernels  25.5 us (49%)
  starting transfers between devices  23.8 us (46%)
  between operations  0.93 us (2%)
  local copies, waits for them, and re-layouts  0.77 us (1%)
  waiting for transfers between devices  0.72 us (1%)
    pallas_call x5, Pallas kernels, run(): made(*[pltpu.with_memory_space_constraint(a, pltpu.VMEM if n in held_in e...  25.5 us
    all_to_all x1, starting transfers between devices, body(): predicted = lax.all_to_all(partial, ('lon', 'rad'), 0, 0)  6.74 us
    ppermute x1, starting transfers between devices, body(): east = lax.ppermute(to_west, 'lon', westward)  4.99 us
    ppermute x1, starting transfers between devices, body(): east2 = lax.ppermute(to_west2, 'lon', westward)  4.43 us
    all_to_all x1, starting transfers between devices, body(): gathered = lax.all_to_all(packets, 'lon', 0, 0)  3.68 us
    ppermute x2, starting transfers between devices, across_rad(): both = lax.ppermute(down, 'rad', [(0, 1), (1, 0)])  3.53 us
  transfers between devices with their start and end apart: 8, of which 2 were waited for; matrix products, arithmetic and copies ran while one was open for 0% of the time, Pallas kernels for 30%

profile of v6, /device:TPU:0, one launch (start us, length us, event | category | flops | bytes accessed | tf_op | source)
XLA Modules:
  0.0 51.7 jit_solution(4261002841868105091)
XLA Ops:
  0.6 2.4 %messages.1 = (f32[200,1,512]{2,1,0:T(1,128)S(1)}, f32[200,1,512]{2,1,0:T(1,128)S(1)}, f32[192,1,512]{2,1,0:T(1,128)S(1)}, f32[192,1,512]{2,1,0:T(1,128)}, f32[8...) custom-call(f32[48,4,512]{2,1,0:T(4,128)} %v_ref.7, f32[3,48,4,512]{3,2,1,0:T(4,128)} %s_ref.5, ...), custom_call_target="tpu_custom_call" | custom-call | flops 2875000064 | bytes 1048576 | tf_op jit(solution)/shard_map/messages/pallas_call | solution.py:778
  3.1 0.0 copy-start.2
  3.1 0.7 %copy-done.2 = f32[192,1,512]{2,1,0:T(1,128)} copy-done((f32[192,1,512]{2,1,0:T(1,128)}, f32[192,1,512]{2,1,0:T(1,128)S(1)}, u32[]{:S(2)}) %copy-start.2) | copy-done | bytes 393240
  3.8 0.5 collective-permute-start
  4.3 5.0 %collective-permute-start.1 = (f32[200,1,512]{2,1,0:T(1,128)S(1)}, f32[200,1,512]{2,1,0:T(1,128)S(1)}, u32[]{:S(2)}, u32[]{:S(2)}) collective-permute-start(f32[200,1,512]{2,1,0:T(1,128)S(1)} %get-tuple-element.18), channel_id=1, source_target_pairs={{2,0},{4,2},{6,4},{8,6},{10,8},{12,10},{14,12},{16,14},{18,16},{20... | collective-permute-start | bytes 1228808 | tf_op jit(solution)/shard_map/ppermute | solution.py:829
  9.3 3.7 %all-to-all-start = ((f32[16,1,84]{2,1,0:T(1,128)}), f32[16,1,84]{2,1,0:T(1,128)S(1)}, u32[]{:S(2)}, u32[]{:S(2)}) async-start(f32[16,1,84]{2,1,0:T(1,128)} %get-tuple-element.20), calls=%async_computation | async-start | bytes 16384 | tf_op jit(solution)/shard_map/all_to_all | solution.py:827
  13.0 1.7 %collective-permute-start.2 = (f32[8,4,512]{2,1,0:T(4,128)S(1)}, f32[8,4,512]{2,1,0:T(4,128)S(1)}, u32[]{:S(2)}, u32[]{:S(2)}) collective-permute-start(f32[8,4,512]{2,1,0:T(4,128)S(1)} %get-tuple-element.19), channel_id=1, source_target_pairs={{0,1},{1,0},{2,3},{3,2},{4,5},{5,4},{6,7},{7,6},{8,9},{9,8},{10,11... | collective-permute-start | bytes 196616 | tf_op jit(solution)/shard_map/ppermute | solution.py:806
  14.7 0.0 collective-permute-start.3
  14.7 4.4 %collective-permute-start.4 = (f32[192,1,512]{2,1,0:T(1,128)}, f32[192,1,512]{2,1,0:T(1,128)}, u32[]{:S(2)}, u32[]{:S(2)}) collective-permute-start(f32[192,1,512]{2,1,0:T(1,128)} %copy-done.2), channel_id=1, source_target_pairs={{2,0},{4,2},{6,4},{8,6},{10,8},{12,10},{14,12},{16,14},{18,16},{20... | collective-permute-start | bytes 1179656 | tf_op jit(solution)/shard_map/ppermute | solution.py:832
  19.1 0.2 all-to-all-done.gathered_ref
  19.4 3.2 %site_weights.1 = (bf16[8,192,512]{2,1,0:T(8,128)(2,1)S(1)}, bf16[8,192,512]{2,1,0:T(8,128)(2,1)S(1)}, f32[8,192]{1,0:T(8,128)S(1)}) custom-call(f32[16,1,84]{2,1,0:T(1,128)S(1)} %all-to-all-done.gathered_ref), custom_call_target="tpu_custom_call" | custom-call | flops 3680000000 | bytes 1048576 | tf_op jit(solution)/shard_map/site_weights/pallas_call | solution.py:778
  22.6 0.0 copy-start.4
  22.6 0.0 copy-start.6
  22.6 0.0 collective-permute-done.2.low_ref.high_ref
  22.6 0.0 collective-permute-done.west_ref
  22.6 0.0 collective-permute-done.1.east_ref
  22.6 0.0 copy-done
  22.6 0.0 copy-done.1
  22.6 0.0 copy-done.3
  22.7 4.9 %forward.1 = (f32[32,1,640]{2,1,0:T(1,128)}, f32[8,1,512]{2,1,0:T(1,128)}, f32[8,1,512]{2,1,0:T(1,128)}) custom-call(s32[2]{0:T(128)S(1)} %copy-done.3, f32[48,4,512]{2,1,0:T(4,128)S(1)} %copy-done.1, f32[3,48,4,512]{3,2,1,0:T(4,128)S(1)} %copy-done, f32[200,1,512]{2,1,0:T(1,128)S(1)} %collective-permute-done.west_ref, ...), custom_call_target="tpu_custom_call" | custom-call | flops 6325000192 | bytes 1048576 | tf_op jit(solution)/shard_map/forward/pallas_call | solution.py:778
  27.6 0.0 copy-done.4
  27.6 0.0 copy-done.6
  27.6 1.8 %collective-permute-start.5 = (f32[8,1,512]{2,1,0:T(1,128)}, f32[8,1,512]{2,1,0:T(1,128)S(1)}, u32[]{:S(2)}, u32[]{:S(2)}) collective-permute-start(f32[8,1,512]{2,1,0:T(1,128)} %get-tuple-element.27), channel_id=1, source_target_pairs={{0,1},{1,0},{2,3},{3,2},{4,5},{5,4},{6,7},{7,6},{8,9},{9,8},{10,11... | collective-permute-start | bytes 49160 | tf_op jit(solution)/shard_map/ppermute | solution.py:806
  29.4 6.7 %all-to-all-start.1 = ((f32[32,1,640]{2,1,0:T(1,128)}), f32[32,1,640]{2,1,0:T(1,128)S(1)}, u32[]{:S(2)}, u32[]{:S(2)}) async-start(f32[32,1,640]{2,1,0:T(1,128)} %get-tuple-element.23), calls=%async_computation.1 | async-start | bytes 163840 | tf_op jit(solution)/shard_map/all_to_all | solution.py:860
  36.1 0.0 copy-start.5
  36.1 0.0 collective-permute-done.3.west2_ref
  36.2 0.0 collective-permute-done.4.east2_ref
  36.2 0.0 collective-permute-done.5.corner_low_ref.corner_high_ref
  36.2 7.1 %prepare.1.blocks_ref = f32[25,25,8,512]{3,2,1,0:T(8,128)} custom-call(s32[2]{0:T(128)S(1)} %copy-done.3, f32[48,4,512]{2,1,0:T(4,128)} %v_ref.7, f32[48,4,512]{2,1,0:T(4,128)} %m_ref.1, f32[3,48,4,512]{3,2,1,0:T(4,128)} %s_ref.5, f32[8,4,512]{2,1,0:T(4,128)} %ice_ref.5, f32[200,1,512]{2,1,0:T(1,128)S(1)} %collective-permute-done.west_ref, ...), custom_call_target="tpu_custom_call" | custom-call | flops 8049999872 | bytes 1048576 | tf_op jit(solution)/shard_map/prepare/pallas_call | solution.py:778
  43.3 0.5 all-to-all-done.1.pred_ref
  43.8 0.0 copy-done.5
  43.8 7.7 %gradient.1 = (f32[48,4,512]{2,1,0:T(4,128)}, f32[48,4,512]{2,1,0:T(4,128)}, f32[1,1]{1,0:T(1,128)}) custom-call(f32[48,4,512]{2,1,0:T(4,128)} %v_ref.7, f32[32,1,640]{2,1,0:T(1,128)S(1)} %all-to-all-done.1.pred_ref, f32[8,192]{1,0:T(8,128)S(1)} %get-tuple-element.24.data_ref, bf16[8,192,512]{2,1,0:T(8,128)(2,1)S(1)} %copy-done.5, ...), custom_call_target="tpu_custom_call" | custom-call | flops 6899999744 | bytes 1048576 | tf_op jit(solution)/shard_map/gradient/pallas_call | solution.py:778
  (3 shorter events, 0.0 us)
Async XLA Ops:
  3.1 0.7 %copy-start.2 = (f32[192,1,512]{2,1,0:T(1,128)}, f32[192,1,512]{2,1,0:T(1,128)S(1)}, u32[]{:S(2)}) copy-start(f32[192,1,512]{2,1,0:T(1,128)S(1)} %get-tuple-element.26) | copy-start | bytes 1179652
  3.8 18.8 %collective-permute-start = (f32[200,1,512]{2,1,0:T(1,128)S(1)}, f32[200,1,512]{2,1,0:T(1,128)S(1)}, u32[]{:S(2)}, u32[]{:S(2)}) collective-permute-start(f32[200,1,512]{2,1,0:T(1,128)S(1)} %get-tuple-element.17), channel_id=1, source_target_pairs={{0,2},{2,4},{4,6},{6,8},{8,10},{10,12},{12,14},{14,16},{16,18},{18... | collective-permute-start | bytes 1228808 | tf_op jit(solution)/shard_map/ppermute | solution.py:828
  4.3 18.3 %collective-permute-start.1 = (f32[200,1,512]{2,1,0:T(1,128)S(1)}, f32[200,1,512]{2,1,0:T(1,128)S(1)}, u32[]{:S(2)}, u32[]{:S(2)}) collective-permute-start(f32[200,1,512]{2,1,0:T(1,128)S(1)} %get-tuple-element.18), channel_id=1, source_target_pairs={{2,0},{4,2},{6,4},{8,6},{10,8},{12,10},{14,12},{16,14},{18,16},{20... | collective-permute-start | bytes 1228808 | tf_op jit(solution)/shard_map/ppermute | solution.py:829
  9.3 10.1 %all-to-all-start = ((f32[16,1,84]{2,1,0:T(1,128)}), f32[16,1,84]{2,1,0:T(1,128)S(1)}, u32[]{:S(2)}, u32[]{:S(2)}) async-start(f32[16,1,84]{2,1,0:T(1,128)} %get-tuple-element.20), calls=%async_computation | async-start | bytes 16384 | tf_op jit(solution)/shard_map/all_to_all | solution.py:827
  13.0 9.6 %collective-permute-start.2 = (f32[8,4,512]{2,1,0:T(4,128)S(1)}, f32[8,4,512]{2,1,0:T(4,128)S(1)}, u32[]{:S(2)}, u32[]{:S(2)}) collective-permute-start(f32[8,4,512]{2,1,0:T(4,128)S(1)} %get-tuple-element.19), channel_id=1, source_target_pairs={{0,1},{1,0},{2,3},{3,2},{4,5},{5,4},{6,7},{7,6},{8,9},{9,8},{10,11... | collective-permute-start | bytes 196616 | tf_op jit(solution)/shard_map/ppermute | solution.py:806
  14.7 21.5 %collective-permute-start.3 = (f32[192,1,512]{2,1,0:T(1,128)}, f32[192,1,512]{2,1,0:T(1,128)}, u32[]{:S(2)}, u32[]{:S(2)}) collective-permute-start(f32[192,1,512]{2,1,0:T(1,128)} %get-tuple-element.25), channel_id=1, source_target_pairs={{0,2},{2,4},{4,6},{6,8},{8,10},{10,12},{12,14},{14,16},{16,18},{18... | collective-permute-start | bytes 1179656 | tf_op jit(solution)/shard_map/ppermute | solution.py:831
  14.7 7.9 %copy-start = (f32[3,48,4,512]{3,2,1,0:T(4,128)S(1)}, f32[3,48,4,512]{3,2,1,0:T(4,128)}, u32[]{:S(2)}) copy-start(f32[3,48,4,512]{3,2,1,0:T(4,128)} %s_ref.5) | copy-start | bytes 3538948
  14.7 7.9 %copy-start.1 = (f32[48,4,512]{2,1,0:T(4,128)S(1)}, f32[48,4,512]{2,1,0:T(4,128)}, u32[]{:S(2)}) copy-start(f32[48,4,512]{2,1,0:T(4,128)} %v_ref.7) | copy-start | bytes 1179652
  14.7 7.9 %copy-start.3 = (s32[2]{0:T(128)S(1)}, s32[2]{0:T(128)}, u32[]{:S(2)}) copy-start(s32[2]{0:T(128)} %steps_ref.3) | copy-start | bytes 28
  14.7 21.4 %collective-permute-start.4 = (f32[192,1,512]{2,1,0:T(1,128)}, f32[192,1,512]{2,1,0:T(1,128)}, u32[]{:S(2)}, u32[]{:S(2)}) collective-permute-start(f32[192,1,512]{2,1,0:T(1,128)} %copy-done.2), channel_id=1, source_target_pairs={{2,0},{4,2},{6,4},{8,6},{10,8},{12,10},{14,12},{16,14},{18,16},{20... | collective-permute-start | bytes 1179656 | tf_op jit(solution)/shard_map/ppermute | solution.py:832
  22.6 5.0 %copy-start.4 = (bf16[8,192,512]{2,1,0:T(8,128)(2,1)}, bf16[8,192,512]{2,1,0:T(8,128)(2,1)S(1)}, u32[]{:S(2)}) copy-start(bf16[8,192,512]{2,1,0:T(8,128)(2,1)S(1)} %get-tuple-element.21.k_high_ref) | copy-start | bytes 4718596
  22.6 5.0 %copy-start.6 = (bf16[8,192,512]{2,1,0:T(8,128)(2,1)}, bf16[8,192,512]{2,1,0:T(8,128)(2,1)S(1)}, u32[]{:S(2)}) copy-start(bf16[8,192,512]{2,1,0:T(8,128)(2,1)S(1)} %get-tuple-element.22.k_low_ref) | copy-start | bytes 4718596
  27.6 8.6 %collective-permute-start.5 = (f32[8,1,512]{2,1,0:T(1,128)}, f32[8,1,512]{2,1,0:T(1,128)S(1)}, u32[]{:S(2)}, u32[]{:S(2)}) collective-permute-start(f32[8,1,512]{2,1,0:T(1,128)} %get-tuple-element.27), channel_id=1, source_target_pairs={{0,1},{1,0},{2,3},{3,2},{4,5},{5,4},{6,7},{7,6},{8,9},{9,8},{10,11... | collective-permute-start | bytes 49160 | tf_op jit(solution)/shard_map/ppermute | solution.py:806
  29.4 14.4 %all-to-all-start.1 = ((f32[32,1,640]{2,1,0:T(1,128)}), f32[32,1,640]{2,1,0:T(1,128)S(1)}, u32[]{:S(2)}, u32[]{:S(2)}) async-start(f32[32,1,640]{2,1,0:T(1,128)} %get-tuple-element.23), calls=%async_computation.1 | async-start | bytes 163840 | tf_op jit(solution)/shard_map/all_to_all | solution.py:860
  36.1 7.7 %copy-start.5 = (bf16[8,192,512]{2,1,0:T(8,128)(2,1)S(1)}, bf16[8,192,512]{2,1,0:T(8,128)(2,1)}, u32[]{:S(2)}) copy-start(bf16[8,192,512]{2,1,0:T(8,128)(2,1)} %copy-done.4) | copy-start | bytes 4718596
